TPU v7x, 128 devices: a whole 4x4x4 slice. The times are simulated.
128 devices in a mesh: ctx: 32 (over x_lo, z, y), wsh: 4 (over x_hi, core).
Axes of the slice: x: 4 (x_hi: 2, x_lo: 2; x = x_hi * 2 + x_lo), y: 4, z: 4, core: 2. Of those that a mesh axis runs over, the one named last changes fastest.
Arguments:
- tokens: bfloat16 [16384, 896], P(('ctx', 'wsh')), may hold values from -6 to 6
- out_grad: bfloat16 [16384, 896], P(('ctx', 'wsh')), may hold values from -6 to 6
- norm1_gain: bfloat16 [896], P('wsh'), may hold values from 0.099609375 to 1.8984375
- qkv_weight: bfloat16 [896, 1152], P('wsh'), may hold values from -0.25 to 0.25
- qkv_bias: bfloat16 [1152], P('wsh'), may hold values from -3 to 3
- out_weight: bfloat16 [896, 896], P('wsh'), may hold values from -2 to 2
- norm2_gain: bfloat16 [896], P('wsh'), may hold values from 0.099609375 to 1.8984375
- gate_weight: bfloat16 [896, 4864], P(None, 'wsh'), may hold values from -0.1875 to 0.1875
- up_weight: bfloat16 [896, 4864], P(None, 'wsh'), may hold values from -0.1875 to 0.1875
- down_weight: bfloat16 [4864, 896], P('wsh'), may hold values from -0.15625 to 0.15625
- positions: int32 [16384], P(('ctx', 'wsh')), may hold values from 0 to 16383, as said below
Outputs:
- output: bfloat16 [16384, 896], P(('ctx', 'wsh'))
- token_grad: float32 [16384, 896], P(('ctx', 'wsh'))
- norm1_gain_grad: float32 [896], P('wsh')
- qkv_weight_grad: float32 [896, 1152], P('wsh')
- qkv_bias_grad: float32 [1152], P('wsh')
- out_weight_grad: float32 [896, 896], P('wsh')
- norm2_gain_grad: float32 [896], P('wsh')
- gate_weight_grad: float32 [896, 4864], P(None, 'wsh')
- up_weight_grad: float32 [896, 4864], P(None, 'wsh')
- down_weight_grad: float32 [4864, 896], P('wsh')
Inputs may be any that keep to these rules, and one draw needn't show every extreme that they name: A permutation of the positions. The sequence is cut into 64 blocks of 256 consecutive positions. Each index c of ctx holds two blocks, b(c) and 63 - b(c), where b is a permutation of 0 to 31 drawn from the seed. The device at index w of wsh in it holds, in order, positions b(c) * 256 + w * 64 onward in its first 64 rows, and the same stretch of block 63 - b(c) in its other rows.
All inputs are finite; a program needn't handle non-finite values.
Results may differ from a plain program's by a relative error of at most 0.035.
Values may be sent and summed in bfloat16 or wider, within the bound.
A program may use at most 192 MiB of HBM per device.

v0:
```python
import math

import jax
import jax.numpy as jnp
from jax import lax
from jax.sharding import PartitionSpec as P

H = 14
KVH = 2
HD = 64
TOK_DEV = 128


norm_eps = 1e-06
rope_base = 1000000.0
masked_score = -1e30


def passed_along(array, axis, by):
    size = lax.axis_size(axis)
    return lax.ppermute(array, axis, [(i, (i + by) % size) for i in range(size)])


def rms_forward(values, gain_vec):
    inverse = lax.rsqrt(jnp.mean(values * values, -1, keepdims=True) + norm_eps)
    return (values * inverse * gain_vec, inverse)


def rms_backward(values, inverse, gain_vec, grad_norm):
    scaled = values * inverse
    grad_scaled = grad_norm * gain_vec
    gain_grad = jnp.sum(grad_norm * scaled, 0)
    value_grad = inverse * (
        grad_scaled - scaled * jnp.mean(grad_scaled * scaled, -1, keepdims=True)
    )
    return (gain_grad, value_grad)


def rotary_tables(positions, width):
    half_width = width // 2
    frequency = rope_base ** (-(2.0 * jnp.arange(half_width, dtype=jnp.float32)) / width)
    angles = positions.astype(jnp.float32)[:, None] * frequency[None, :]
    return (jnp.cos(angles)[:, None, :], jnp.sin(angles)[:, None, :])


def rotate(values, cosine, sine_vals):
    half_width = values.shape[-1] // 2
    first_half = values[..., :half_width]
    second_half = values[..., half_width:]
    return jnp.concatenate(
        [
            first_half * cosine - second_half * sine_vals,
            second_half * cosine + first_half * sine_vals,
        ],
        -1,
    )


def rotate_back(grads, cosine, sine_vals):
    half_width = grads.shape[-1] // 2
    first_half = grads[..., :half_width]
    second_half = grads[..., half_width:]
    return jnp.concatenate(
        [
            first_half * cosine + second_half * sine_vals,
            second_half * cosine - first_half * sine_vals,
        ],
        -1,
    )


def pick(array_in, index_at):
    return lax.dynamic_index_in_dim(array_in, index_at, 0, keepdims=False)


def place(array_in, update, index_at):
    return lax.dynamic_update_index_in_dim(array_in, update, index_at, 0)


def body(
    tokens,
    out_grad,
    norm1_gain,
    qkv_weight,
    qkv_bias,
    out_weight,
    norm2_gain,
    gate_weight,
    up_weight,
    down_weight,
    positions,
):
    cycle_size = lax.axis_size("ctx")
    shard_count = lax.axis_size("wsh")
    my_cycle = lax.axis_index("ctx")
    half_rows = TOK_DEV // 2
    block_rows = shard_count * half_rows
    groups = H // KVH
    kv_width = KVH * HD
    score_scale = 1.0 / math.sqrt(HD)
    f32 = jnp.float32
    bf16 = jnp.bfloat16
    gain_one, qkv_full, bias_full, out_full, gain_two = (
        lax.all_gather(norm1_gain, "wsh", axis=0, tiled=True),
        lax.all_gather(qkv_weight, "wsh", axis=0, tiled=True),
        lax.all_gather(qkv_bias, "wsh", axis=0, tiled=True),
        lax.all_gather(out_weight, "wsh", axis=0, tiled=True),
        lax.all_gather(norm2_gain, "wsh", axis=0, tiled=True),
    )
    block_starts = lax.all_gather(positions[:1], "ctx", axis=0, tiled=True)
    block_table = block_starts // block_rows
    my_block = positions[0] // block_rows
    resid = tokens.astype(f32)
    gain_one_f = gain_one.astype(f32)
    normed_f, inverse_one = rms_forward(resid, gain_one_f)
    normed_one = normed_f.astype(bf16)
    projected = jnp.dot(normed_one, qkv_full, preferred_element_type=f32) + bias_full.astype(f32)
    cosine, sine_vals = rotary_tables(positions, HD)
    query_rot = rotate(projected[:, : H * HD].reshape(TOK_DEV, H, HD), cosine, sine_vals).astype(
        bf16
    )
    key_rot = rotate(
        projected[:, H * HD : H * HD + kv_width].reshape(TOK_DEV, KVH, HD), cosine, sine_vals
    ).astype(bf16)
    value_part = projected[:, H * HD + kv_width :].astype(bf16)
    kv_local = jnp.concatenate([key_rot.reshape(TOK_DEV, kv_width), value_part], 1).reshape(
        2, half_rows, 2 * kv_width
    )
    kv_group = lax.all_gather(kv_local, "wsh", axis=1, tiled=True)
    query_halves = query_rot.reshape(2, half_rows, KVH, groups, HD)
    key_offsets = jnp.arange(block_rows, dtype=jnp.int32)
    early_visible = positions[:half_rows, None] >= my_block * block_rows + key_offsets[None, :]
    late_visible = (
        positions[half_rows:, None]
        >= (2 * cycle_size - 1 - my_block) * block_rows + key_offsets[None, :]
    )

    def split_block(key_block, key_half):
        block_part = pick(key_block, key_half)
        return (
            block_part[:, :kv_width].reshape(block_rows, KVH, HD),
            block_part[:, kv_width:].reshape(block_rows, KVH, HD),
        )

    def forward_update(fold_state, half_index, key_half, key_block, visible):
        run_max, run_sum, run_acc = fold_state
        queries = pick(query_halves, half_index)
        key_rows, value_rows = split_block(key_block, key_half)
        scores = (
            jnp.einsum("qkgd,nkd->kgqn", queries, key_rows, preferred_element_type=f32)
            * score_scale
        )
        if visible is not None:
            scores = jnp.where(visible[None, None], scores, masked_score)
        old_max = pick(run_max, half_index)
        new_max = jnp.maximum(old_max, jnp.max(scores, -1))
        shrink = jnp.exp(old_max - new_max)
        weights_raw = jnp.exp(scores - new_max[..., None])
        new_sum = pick(run_sum, half_index) * shrink + jnp.sum(weights_raw, -1)
        new_acc = pick(run_acc, half_index) * shrink[..., None] + jnp.einsum(
            "kgqn,nkd->kgqd", weights_raw.astype(bf16), value_rows, preferred_element_type=f32
        )
        return (
            place(run_max, new_max, half_index),
            place(run_sum, new_sum, half_index),
            place(run_acc, new_acc, half_index),
        )

    start_state = (
        jnp.full((2, KVH, groups, half_rows), masked_score, f32),
        jnp.zeros((2, KVH, groups, half_rows), f32),
        jnp.zeros((2, KVH, groups, half_rows, HD), f32),
    )
    kv_piece = lax.all_gather(kv_group[None], "ctx", axis=0, tiled=True)

    def one_shard(shard_index, current):
        key_block = pick(kv_piece, shard_index)
        source_block = block_table[shard_index]

        def one_on_diagonal(inner_state):
            inner_state = forward_update(inner_state, 0, 0, key_block, early_visible)
            inner_state = forward_update(inner_state, 1, 0, key_block, None)
            return forward_update(inner_state, 1, 1, key_block, late_visible)

        def one_off_diagonal(inner_state):
            inner_state = forward_update(inner_state, 1, 0, key_block, None)
            chosen = (source_block > my_block).astype(jnp.int32)
            return forward_update(inner_state, chosen, chosen, key_block, None)

        return lax.cond(shard_index == my_cycle, one_on_diagonal, one_off_diagonal, current)

    run_max, run_sum, run_acc = lax.fori_loop(0, kv_piece.shape[0], one_shard, start_state)
    log_total = run_max + jnp.log(run_sum)
    attended_f = jnp.transpose(run_acc / run_sum[..., None], (0, 3, 1, 2, 4)).reshape(
        TOK_DEV, H * HD
    )
    attended = attended_f.astype(bf16)
    stream = resid + jnp.dot(attended, out_full, preferred_element_type=f32)
    gain_two_f = gain_two.astype(f32)
    normed_two_f, inverse_two = rms_forward(stream, gain_two_f)
    normed_two = normed_two_f.astype(bf16)
    gate_full, up_full, down_full = (
        lax.all_gather(gate_weight, "wsh", axis=1, tiled=True),
        lax.all_gather(up_weight, "wsh", axis=1, tiled=True),
        lax.all_gather(down_weight, "wsh", axis=0, tiled=True),
    )
    mlp_in, cot_rows = (normed_two, out_grad)
    gate_pre = jnp.dot(mlp_in, gate_full, preferred_element_type=f32)
    up_pre = jnp.dot(mlp_in, up_full, preferred_element_type=f32)
    sigmoid_gate = jax.nn.sigmoid(gate_pre)
    activated = gate_pre * sigmoid_gate
    hidden = (activated * up_pre).astype(bf16)
    mlp_part = jnp.dot(hidden, down_full, preferred_element_type=f32)
    hidden_grad = jnp.einsum("td,fd->tf", cot_rows, down_full, preferred_element_type=f32)
    gate_grad = (
        hidden_grad * up_pre * sigmoid_gate * (1.0 + gate_pre * (1.0 - sigmoid_gate))
    ).astype(bf16)
    up_grad = (hidden_grad * activated).astype(bf16)
    down_wgrad = jnp.einsum("tf,td->fd", hidden, cot_rows, preferred_element_type=f32)
    gate_wgrad = jnp.einsum("td,tf->df", mlp_in, gate_grad, preferred_element_type=f32)
    up_wgrad = jnp.einsum("td,tf->df", mlp_in, up_grad, preferred_element_type=f32)
    norm_grad_part = jnp.einsum(
        "tf,df->td", gate_grad, gate_full, preferred_element_type=f32
    ) + jnp.einsum("tf,df->td", up_grad, up_full, preferred_element_type=f32)
    gate_wgrad, up_wgrad, down_wgrad = (
        lax.psum_scatter(
            gate_wgrad.astype(jnp.bfloat16), "wsh", scatter_dimension=1, tiled=True
        ).astype(jnp.float32),
        lax.psum_scatter(
            up_wgrad.astype(jnp.bfloat16), "wsh", scatter_dimension=1, tiled=True
        ).astype(jnp.float32),
        lax.psum_scatter(
            down_wgrad.astype(jnp.bfloat16), "wsh", scatter_dimension=0, tiled=True
        ).astype(jnp.float32),
    )
    output = (stream + mlp_part).astype(bf16)
    gain_two_grad, stream_from = rms_backward(stream, inverse_two, gain_two_f, norm_grad_part)
    stream_grad = out_grad.astype(f32) + stream_from
    branch_grad = stream_grad.astype(bf16)
    out_wgrad = jnp.einsum("ti,td->id", attended, branch_grad, preferred_element_type=f32)
    attended_grad = jnp.einsum(
        "td,id->ti", branch_grad, out_full, preferred_element_type=f32
    ).astype(bf16)
    delta_rows = jnp.sum(
        (attended_grad.astype(f32) * attended_f).reshape(2, half_rows, KVH, groups, HD), -1
    )
    delta_halves = jnp.transpose(delta_rows, (0, 2, 3, 1))
    grad_halves = attended_grad.reshape(2, half_rows, KVH, groups, HD)

    def backward_update(grad_state, half_index, key_half, key_block, visible):
        query_grad, kv_grad = grad_state
        queries = pick(query_halves, half_index)
        grads_out = pick(grad_halves, half_index)
        key_rows, value_rows = split_block(key_block, key_half)
        scores = (
            jnp.einsum("qkgd,nkd->kgqn", queries, key_rows, preferred_element_type=f32)
            * score_scale
        )
        if visible is not None:
            scores = jnp.where(visible[None, None], scores, masked_score)
        probabilities = jnp.exp(scores - pick(log_total, half_index)[..., None])
        prob_grad = jnp.einsum("qkgd,nkd->kgqn", grads_out, value_rows, preferred_element_type=f32)
        score_grad = (
            probabilities * (prob_grad - pick(delta_halves, half_index)[..., None])
        ).astype(bf16)
        query_step = (
            jnp.einsum("kgqn,nkd->kgqd", score_grad, key_rows, preferred_element_type=f32)
            * score_scale
        )
        key_step = (
            jnp.einsum("kgqn,qkgd->nkd", score_grad, queries, preferred_element_type=f32)
            * score_scale
        )
        value_step = jnp.einsum(
            "kgqn,qkgd->nkd", probabilities.astype(bf16), grads_out, preferred_element_type=f32
        )
        query_grad = place(query_grad, pick(query_grad, half_index) + query_step, half_index)
        kv_step = jnp.concatenate(
            [key_step.reshape(block_rows, kv_width), value_step.reshape(block_rows, kv_width)], 1
        )
        kv_grad = place(kv_grad, pick(kv_grad, key_half) + kv_step, key_half)
        return (query_grad, kv_grad)

    def cycle_step(step_index, cycle_carry):
        kv_block, kv_grad, query_grad = cycle_carry
        source = (my_cycle - step_index) % cycle_size
        source_block = block_table[source]
        current_block = kv_block

        def cycle_on_diagonal(inner_state):
            inner_state = backward_update(inner_state, 0, 0, current_block, early_visible)
            inner_state = backward_update(inner_state, 1, 0, current_block, None)
            return backward_update(inner_state, 1, 1, current_block, late_visible)

        def cycle_off_diagonal(inner_state):
            inner_state = backward_update(inner_state, 1, 0, current_block, None)
            chosen = (source_block > my_block).astype(jnp.int32)
            return backward_update(inner_state, chosen, chosen, current_block, None)

        query_grad, kv_grad = lax.cond(
            step_index == 0, cycle_on_diagonal, cycle_off_diagonal, (query_grad, kv_grad)
        )
        kv_grad = passed_along(kv_grad.astype(jnp.bfloat16), "ctx", 1).astype(kv_grad.dtype)
        kv_block = passed_along(kv_block, "ctx", 1)
        return (kv_block, kv_grad, query_grad)

    def cycle_pair(pair_index, cycle_carry):
        return cycle_step(2 * pair_index + 1, cycle_step(2 * pair_index, cycle_carry))

    cycle_start = (
        kv_group,
        jnp.zeros((2, block_rows, 2 * kv_width), f32),
        jnp.zeros((2, KVH, groups, half_rows, HD), f32),
    )
    kv_block, kv_grad, query_grad = lax.fori_loop(0, cycle_size // 2, cycle_pair, cycle_start)
    kv_home = (
        lax.psum_scatter(kv_grad.astype(jnp.bfloat16), "wsh", scatter_dimension=1, tiled=True)
        .astype(jnp.float32)
        .reshape(TOK_DEV, 2 * kv_width)
    )
    key_grad = kv_home[:, :kv_width].reshape(TOK_DEV, KVH, HD)
    value_grad = kv_home[:, kv_width:]
    query_rows = jnp.transpose(query_grad, (0, 3, 1, 2, 4)).reshape(TOK_DEV, H, HD)
    projected_grad = jnp.concatenate(
        [
            rotate_back(query_rows, cosine, sine_vals).reshape(TOK_DEV, H * HD),
            rotate_back(key_grad, cosine, sine_vals).reshape(TOK_DEV, kv_width),
            value_grad,
        ],
        1,
    ).astype(bf16)
    bias_grad = jnp.sum(projected_grad.astype(f32), 0)
    qkv_wgrad = jnp.einsum("td,tf->df", normed_one, projected_grad, preferred_element_type=f32)
    normed_one_grad = jnp.einsum("tf,df->td", projected_grad, qkv_full, preferred_element_type=f32)
    gain_one_grad, resid_from = rms_backward(resid, inverse_one, gain_one_f, normed_one_grad)
    token_grad = stream_grad + resid_from
    gain_one_grad, qkv_wgrad, bias_grad, out_wgrad, gain_two_grad = (
        lax.psum_scatter(
            gain_one_grad.astype(jnp.bfloat16), "wsh", scatter_dimension=0, tiled=True
        ).astype(jnp.float32),
        lax.psum_scatter(
            qkv_wgrad.astype(jnp.bfloat16), "wsh", scatter_dimension=0, tiled=True
        ).astype(jnp.float32),
        lax.psum_scatter(
            bias_grad.astype(jnp.bfloat16), "wsh", scatter_dimension=0, tiled=True
        ).astype(jnp.float32),
        lax.psum_scatter(
            out_wgrad.astype(jnp.bfloat16), "wsh", scatter_dimension=0, tiled=True
        ).astype(jnp.float32),
        lax.psum_scatter(
            gain_two_grad.astype(jnp.bfloat16), "wsh", scatter_dimension=0, tiled=True
        ).astype(jnp.float32),
    )
    summed = (
        lax.psum(gain_one_grad.astype(jnp.bfloat16), "ctx").astype(jnp.float32),
        lax.psum(qkv_wgrad.astype(jnp.bfloat16), "ctx").astype(jnp.float32),
        lax.psum(bias_grad.astype(jnp.bfloat16), "ctx").astype(jnp.float32),
        lax.psum(out_wgrad.astype(jnp.bfloat16), "ctx").astype(jnp.float32),
        lax.psum(gain_two_grad.astype(jnp.bfloat16), "ctx").astype(jnp.float32),
        lax.psum(gate_wgrad.astype(jnp.bfloat16), "ctx").astype(jnp.float32),
        lax.psum(up_wgrad.astype(jnp.bfloat16), "ctx").astype(jnp.float32),
        lax.psum(down_wgrad.astype(jnp.bfloat16), "ctx").astype(jnp.float32),
    )
    return (
        output,
        token_grad,
        summed[0],
        summed[1],
        summed[2],
        summed[3],
        summed[4],
        summed[5],
        summed[6],
        summed[7],
    )


def solution(mesh):
    return jax.shard_map(
        body,
        mesh=mesh,
        in_specs=(
            P(("ctx", "wsh"), None),
            P(("ctx", "wsh"), None),
            P("wsh"),
            P("wsh", None),
            P("wsh"),
            P("wsh", None),
            P("wsh"),
            P(None, "wsh"),
            P(None, "wsh"),
            P("wsh", None),
            P(("ctx", "wsh")),
        ),
        out_specs=(
            P(("ctx", "wsh"), None),
            P(("ctx", "wsh"), None),
            P("wsh"),
            P("wsh", None),
            P("wsh"),
            P("wsh", None),
            P("wsh"),
            P(None, "wsh"),
            P(None, "wsh"),
            P("wsh", None),
        ),
        check_vma=False,
    )
```

profile of v0, /device:TPU:0, one launch (start us, length us, event | category | flops | bytes accessed | tf_op | source)
XLA Modules:
  0.0 1796.8 jit_solution(13314896307941730490)
XLA Ops:
  13.2 10.1 all-reduce.10
  25.2 13.4 all-gather.8.cloned.1.call-done
  41.3 7.8 all_gather.36
  56.0 18.8 %all-reduce.2 = s32[32]{0:T(128)S(1)} all-reduce(s32[32]{0:T(128)S(1)} %get-tuple-element.1259), channel_id=1, replica_groups=mesh['ctx'=32,'wsh'=4] {'ctx'}, use_global_device_ids=true, to_apply=%add.2 | all-reduce | flops 32 | bytes 256
  76.8 139.7 %all-gather.18.cloned.1.call-done = bf16[64,256,256]{2,1,0:T(8,128)(2,1)} async-done(((bf16[2,256,256]{2,1,0:T(8,128)(2,1)}), bf16[64,256,256]{2,1,0:T(8,128)(2,1)}) %all-gather.18.cloned.1.call-update) | async-done | bytes 8388624 | tf_op jit(solution)/shard_map/all_gather | solution.py:174
  216.6 152.9 %while.38 = (s32[]{:T(128)}, f32[2,2,7,64]{3,2,1,0:T(8,128)S(1)}, f32[2,2,7,64]{3,2,1,0:T(8,128)S(1)}, f32[2,2,7,64,64]{4,3,2,1,0:T(8,128)S(1)}, s32[]{:T(128)},...) while((s32[]{:T(128)}, f32[2,2,7,64]{3,2,1,0:T(8,128)S(1)}, ...), condition=%wide.region_14.15_spmd.clone, body=%wide.region_1.14_spmd.clone.sunk | while | flops 181140352 | bytes 15505727 | solution.py:192
  377.9 7.5 fusion.326
  385.4 9.0 fusion.327
  394.4 43.4 %all-gather.16.cloned.1.call-done = bf16[4864,896]{1,0:T(8,128)(2,1)} async-done(((bf16[1216,896]{1,0:T(8,128)(2,1)}), bf16[4864,896]{1,0:T(8,128)(2,1)}) %all-gather.16.cloned.1.call-update) | async-done | bytes 8716304 | tf_op jit(solution)/shard_map/all_gather | solution.py:205
  437.8 8.7 multiply_convert_fusion
  446.5 5.9 fusion.328
  458.5 623.0 %while.39 = (s32[]{:T(128)}, bf16[2,256,256]{1,2,0:T(8,128)(2,1)S(1)}, f32[2,256,256]{1,2,0:T(8,128)S(1)}, f32[2,2,7,64,64]{4,3,2,1,0:T(8,128)S(1)}, s32[]{:T(12...) while((s32[]{:T(128)}, ...), condition=%wide.region_23.24_spmd.clone, body=%wide.region_18.23_spmd.clone.sunk | while | flops 892338176 | bytes 56880368 | solution.py:315
  466.4 10.4 collective-permute-done.2
  476.8 4.9 collective-permute-done
  486.2 13.4 collective-permute-done.3
  508.2 13.4 collective-permute-done.2
  529.1 12.7 collective-permute-done.3
  549.3 11.8 collective-permute-done.2
  568.3 10.9 collective-permute-done.3
  586.6 10.5 collective-permute-done.2
  604.3 10.5 collective-permute-done.3
  622.2 10.5 collective-permute-done.2
  640.0 10.5 collective-permute-done.3
  657.9 10.5 collective-permute-done.2
  675.6 10.5 collective-permute-done.3
  694.2 10.5 collective-permute-done.2
  704.7 4.6 collective-permute-done
  713.8 10.5 collective-permute-done.3
  724.3 5.5 collective-permute-done.1
  734.5 11.7 collective-permute-done.2
  746.2 5.6 collective-permute-done
  756.2 12.7 collective-permute-done.3
  769.0 5.6 collective-permute-done.1
  779.2 13.3 collective-permute-done.2
  792.5 4.9 collective-permute-done
  801.8 13.4 collective-permute-done.3
  824.0 13.4 collective-permute-done.2
  844.9 12.9 collective-permute-done.3
  865.2 11.8 collective-permute-done.2
  884.2 11.0 collective-permute-done.3
  902.7 10.5 collective-permute-done.2
  920.4 10.5 collective-permute-done.3
  938.3 10.5 collective-permute-done.2
  956.1 10.5 collective-permute-done.3
  974.0 10.5 collective-permute-done.2
  991.7 10.5 collective-permute-done.3
  1010.2 10.5 collective-permute-done.2
  1029.6 10.5 collective-permute-done.3
  1040.2 5.5 collective-permute-done.1
  1050.3 10.5 collective-permute-done.2
  1068.0 10.5 collective-permute-done.3
  1086.7 18.9 %reduce-scatter.7.cloned.1.call-done = bf16[2,64,256]{2,1,0:T(8,128)(2,1)} async-done(((bf16[2,256,256]{2,1,0:T(8,128)(2,1)}), bf16[2,64,256]{2,1,0:T(8,128)(2,1)}) %reduce-scatter.7.cloned.1.call-update) | async-done | bytes 65552 | tf_op jit(solution)/shard_map/reduce_scatter | solution.py:317
  1108.8 4.8 convolution_convert_fusion.2
  1115.0 4.9 convolution_convert_fusion.1
  1121.2 4.7 convolution_convert_fusion
  1125.9 17.8 reduce-scatter.11.cloned.1.call-done
  1143.7 40.9 %reduce-scatter.9.cloned.1.call-done = bf16[224,1152]{1,0:T(8,128)(2,1)} async-done(((bf16[896,1152]{1,0:T(8,128)(2,1)}), bf16[224,1152]{1,0:T(8,128)(2,1)}) %reduce-scatter.9.cloned.1.call-update) | async-done | bytes 516112 | tf_op jit(solution)/shard_map/reduce_scatter | solution.py:341
  1184.6 82.9 %reduce-scatter.13.cloned.1.call-done = bf16[896,1216]{0,1:T(8,128)(2,1)} async-done(((bf16[896,4864]{0,1:T(8,128)(2,1)}), bf16[896,1216]{0,1:T(8,128)(2,1)}) %reduce-scatter.13.cloned.1.call-update) | async-done | bytes 2179088 | tf_op jit(solution)/shard_map/reduce_scatter | solution.py:226
  1267.5 83.1 %reduce-scatter.15.cloned.1.call-done = bf16[896,1216]{0,1:T(8,128)(2,1)} async-done(((bf16[896,4864]{0,1:T(8,128)(2,1)}), bf16[896,1216]{0,1:T(8,128)(2,1)}) %reduce-scatter.15.cloned.1.call-update) | async-done | bytes 2179088 | tf_op jit(solution)/shard_map/reduce_scatter | solution.py:229
  1350.6 82.9 %reduce-scatter.17.cloned.1.call-done = bf16[1216,896]{1,0:T(8,128)(2,1)} async-done(((bf16[4864,896]{1,0:T(8,128)(2,1)}), bf16[1216,896]{1,0:T(8,128)(2,1)}) %reduce-scatter.17.cloned.1.call-update) | async-done | bytes 2179088 | tf_op jit(solution)/shard_map/reduce_scatter | solution.py:232
  1434.7 5.8 fusion.286
  1441.6 7.4 all-reduce.9
  1449.2 83.4 %all-reduce.7 = (bf16[224]{0:T(256)(128)(2,1)S(1)}, bf16[288]{0:T(512)(128)(2,1)S(1)}, bf16[224]{0:T(256)(128)(2,1)S(1)}) all-reduce(bf16[224]{0:T(256)(128)(2,1)S(1)} %dynamic-slice.5, bf16[288]{0:T(512)(128)(2,1)S(1)} %dynamic-slice.7, bf16[224]{0:T(256)(128)(2,1)S(1)} %dynamic-slice.9), channel_id=1, replica_groups=mesh['ctx'=32,'wsh'=4] {'ctx'}, use_global_device_ids=true, to_apply=%region_28.29 | all-reduce | flops 736 | bytes 2944 | tf_op jit(solution)/shard_map/psum | solution.py:355
  1535.3 243.0 %all-reduce.13.cloned.1.call-done = (bf16[224,1152]{1,0:T(8,128)(2,1)}, bf16[224,896]{1,0:T(8,128)(2,1)}, bf16[896,1216]{0,1:T(8,128)(2,1)}, bf16[896,1216]{0,1:T(8,128)(2,1)}, bf16[1216,896]{1,0:T(8,128)(2,1)}) async-done(((bf16[224,1152]{1,0:T(8,128)(2,1)}, bf16[224,896]{1,0:T(8,128)(2,1)}, bf16[896,1216]{0,1:T(8,128)(2,1)}, bf16[896,1216]{0,1:T(8,128)(2,1)}, bf16[1216,896]{1,0:T(8,128)(2,1)}), ...) | async-done | bytes 7454736 | tf_op jit(solution)/shard_map/psum | solution.py:356
  (1575 shorter events, 633.5 us)
Async XLA Ops:
  7.2 31.4 %all-gather.8.cloned.1.call-start = ((), (), s32[]{:S(2)}) async-start(), calls=%async_computation.6 | async-start | bytes 2580480 | tf_op jit(solution)/shard_map/all_gather | solution.py:105
  7.9 208.6 %all-gather.18.cloned.1.call-start = ((), (), s32[]{:S(2)}) async-start(), calls=%async_computation.17 | async-start | bytes 8650752 | tf_op jit(solution)/shard_map/all_gather | solution.py:174
  49.1 326.7 %all-gather.10.cloned.1.call-start = ((), (), s32[]{:S(2)}) async-start(), calls=%async_computation.7 | async-start | bytes 2007040 | tf_op jit(solution)/shard_map/all_gather | solution.py:107
  49.8 328.1 %all-gather.12.cloned.1.call-start = ((), (), s32[]{:S(2)}) async-start(), calls=%async_computation.8 | async-start | bytes 10895360 | tf_op jit(solution)/shard_map/all_gather | solution.py:203
  50.4 335.0 %all-gather.14.cloned.1.call-start = ((), (), s32[]{:S(2)}) async-start(), calls=%async_computation.9 | async-start | bytes 10895360 | tf_op jit(solution)/shard_map/all_gather | solution.py:204
  51.0 386.8 %all-gather.16.cloned.1.call-start = ((), (), s32[]{:S(2)}) async-start(), calls=%async_computation.10 | async-start | bytes 10895360 | tf_op jit(solution)/shard_map/all_gather | solution.py:205
  51.6 1054.0 %reduce-scatter.7.cloned.1.call-start = ((), (), s32[]{:S(2)}) async-start(), calls=%async_computation.11 | async-start | bytes 327680 | tf_op jit(solution)/shard_map/reduce_scatter | solution.py:317
  463.3 13.4 collective-permute-start.2
  464.9 16.8 collective-permute-start
  486.0 13.5 collective-permute-start.3
  486.1 17.5 collective-permute-start.1
  508.0 13.5 collective-permute-start.2
  508.1 16.5 collective-permute-start
  528.9 12.9 collective-permute-start.3
  529.0 15.6 collective-permute-start.1
  549.1 11.9 collective-permute-start.2
  549.2 14.7 collective-permute-start
  568.1 11.0 collective-permute-start.3
  568.2 13.8 collective-permute-start.1
  586.4 10.7 collective-permute-start.2
  586.5 13.4 collective-permute-start
  604.2 10.7 collective-permute-start.3
  604.2 13.4 collective-permute-start.1
  622.1 10.7 collective-permute-start.2
  622.2 13.4 collective-permute-start
  639.8 10.7 collective-permute-start.3
  639.9 13.4 collective-permute-start.1
  657.7 10.7 collective-permute-start.2
  657.8 13.4 collective-permute-start
  675.6 14.0 collective-permute-start.1
  694.1 15.3 collective-permute-start
  713.7 16.2 collective-permute-start.1
  734.3 11.9 collective-permute-start.2
  734.4 17.4 collective-permute-start
  756.1 12.9 collective-permute-start.3
  756.2 18.4 %collective-permute-start.1 = (bf16[2,256,256]{1,2,0:T(8,128)(2,1)S(1)}, bf16[2,256,256]{1,2,0:T(8,128)(2,1)S(1)}, u32[]{:S(2)}, u32[]{:S(2)}) collective-permute-start(bf16[2,256,256]{1,2,0:T(8,128)(2,1)S(1)} %collective-permute-done), channel_id=1, source_target_pairs={{0,4},{4,8},{8,12},{12,16},{16,20},{20,24},{24,28},{28,32},{32,36}... | collective-permute-start | bytes 786440 | tf_op jit(solution)/shard_map/while/body/eval_jaxpr/ppermute | solution.py:21
  779.0 13.4 collective-permute-start.2
  779.1 18.3 %collective-permute-start = (bf16[2,256,256]{1,2,0:T(8,128)(2,1)S(1)}, bf16[2,256,256]{1,2,0:T(8,128)(2,1)S(1)}, u32[]{:S(2)}, u32[]{:S(2)}) collective-permute-start(bf16[2,256,256]{1,2,0:T(8,128)(2,1)S(1)} %get-tuple-element.1531), channel_id=1, source_target_pairs={{0,4},{4,8},{8,12},{12,16},{16,20},{20,24},{24,28},{28,32},{32,36}... | collective-permute-start | bytes 786440 | tf_op jit(solution)/shard_map/while/body/eval_jaxpr/ppermute | solution.py:21
  801.7 13.5 collective-permute-start.3
  801.7 17.6 collective-permute-start.1
  823.8 13.5 collective-permute-start.2
  823.9 16.5 collective-permute-start
  844.7 13.1 collective-permute-start.3
  844.8 15.8 collective-permute-start.1
  865.0 12.0 collective-permute-start.2
  865.1 14.7 collective-permute-start
  884.0 11.2 collective-permute-start.3
  884.1 13.9 collective-permute-start.1
  902.6 13.4 collective-permute-start
  920.3 13.4 collective-permute-start.1
  938.2 13.4 collective-permute-start
  956.0 13.4 collective-permute-start.1
  973.9 13.4 collective-permute-start
  991.6 14.0 collective-permute-start.1
  1010.1 15.1 collective-permute-start
  1029.6 16.1 collective-permute-start.1
  1050.2 13.4 collective-permute-start
  1068.0 13.4 collective-permute-start.1
  1082.4 61.3 %reduce-scatter.11.cloned.1.call-start = ((), (), s32[]{:S(2)}) async-start(), calls=%async_computation.13 | async-start | bytes 2007040 | tf_op jit(solution)/shard_map/reduce_scatter | solution.py:347
  1085.4 99.2 %reduce-scatter.9.cloned.1.call-start = ((), (), s32[]{:S(2)}) async-start(), calls=%async_computation.12 | async-start | bytes 2580480 | tf_op jit(solution)/shard_map/reduce_scatter | solution.py:341
  1108.8 158.7 %reduce-scatter.13.cloned.1.call-start = ((), (), s32[]{:S(2)}) async-start(), calls=%async_computation.14 | async-start | bytes 10895360 | tf_op jit(solution)/shard_map/reduce_scatter | solution.py:226
  1113.7 236.9 %reduce-scatter.15.cloned.1.call-start = ((), (), s32[]{:S(2)}) async-start(), calls=%async_computation.15 | async-start | bytes 10895360 | tf_op jit(solution)/shard_map/reduce_scatter | solution.py:229
  1119.8 313.7 %reduce-scatter.17.cloned.1.call-start = ((), (), s32[]{:S(2)}) async-start(), calls=%async_computation.16 | async-start | bytes 10895360 | tf_op jit(solution)/shard_map/reduce_scatter | solution.py:232
  1125.9 652.4 %all-reduce.13.cloned.1.call-start = ((), (), s32[]{:S(2)}) async-start(), calls=%async_computation.18 | async-start | bytes 14909440 | tf_op jit(solution)/shard_map/psum | solution.py:356
  (50 other events, 690.8 us)
Sparse Core Ops, SparseCore 0:
  9.7 28.8 all-gather.7
  49.2 167.2 all-gather.17
  218.1 24.0 all-gather.9
  243.8 63.6 all-gather.11
  309.0 63.6 all-gather.13
  374.2 63.6 all-gather.15
  1082.6 22.9 reduce-scatter.6
  1109.0 34.6 reduce-scatter.10
  1147.0 37.5 reduce-scatter.8
  1187.4 80.0 reduce-scatter.12
  1270.5 80.0 reduce-scatter.14
  1353.4 80.0 reduce-scatter.16
  1436.7 341.5 all-reduce.12
where the time goes:
time: 1810 us; the launch traced here: 1800 us
  waiting for transfers between devices  1240 us (69%)
  matrix products  194 us (11%)
  blocking collectives  127 us (7%)
  local copies, waits for them, and re-layouts  99.6 us (6%)
  other arithmetic  52.8 us (3%)
  loops' own time  52.8 us (3%)
  between operations  20.2 us (1%)
    ppermute x64, waiting for transfers between devices, passed_along(): lax.ppermute(array, axis, [(i, (i + by) % size) for i in range(size)])  473 us
    psum x1, waiting for transfers between devices, body(): lax.psum(qkv_wgrad.astype(jnp.bfloat16), 'ctx').astype(jnp.float32)  243 us
    all_gather x1, waiting for transfers between devices, body(): kv_piece = lax.all_gather(kv_group[None], 'ctx', axis=0, tiled=True)  140 us
    psum x1, blocking collectives, body(): lax.psum(gain_one_grad.astype(jnp.bfloat16), 'ctx').astype(jnp.float32)  83.4 us
    reduce_scatter x1, waiting for transfers between devices, body(): lax.psum_scatter(up_wgrad.astype(jnp.bfloat16), 'wsh', scatter_dimension=...  83.1 us
    reduce_scatter x1, waiting for transfers between devices, body(): lax.psum_scatter(down_wgrad.astype(jnp.bfloat16), 'wsh', scatter_dimensio...  82.9 us
    reduce_scatter x1, waiting for transfers between devices, body(): lax.psum_scatter(gate_wgrad.astype(jnp.bfloat16), 'wsh', scatter_dimensio...  82.9 us
    all_gather x1, waiting for transfers between devices, body(): lax.all_gather(down_weight, 'wsh', axis=0, tiled=True)  43.4 us
  transfers between devices with their start and end apart: 77, of which 74 were waited for; matrix products, arithmetic and copies ran while one was open for 11% of the time, Pallas kernels for 0%

commit v1 on v0

v1 whole, which is shorter than its diff:
```python
import functools
import math

import jax
import jax.numpy as jnp
from jax import lax
from jax.experimental import pallas as pl
from jax.experimental.pallas import tpu as pltpu
from jax.sharding import PartitionSpec as P

H = 14
KVH = 2
HD = 64
G = H // KVH
D = 896
FS = 1216
QKV = 1152
QC = G * HD
PC = QC + 2 * HD
TOK = 128
CHIP = 256
KROWS = 272

MESH = pl.DeviceIdType.MESH
VLIM = 56 * 1024 * 1024
norm_eps = 1e-06
rope_base = 1000000.0
f32 = jnp.float32
bf16 = jnp.bfloat16


def my_place():
    c = lax.axis_index("ctx")
    w = lax.axis_index("wsh")
    return (w // 2) * 2 + c // 16, c % 4, (c // 4) % 4, w % 2


def dev(x, y, z, core):
    return ((x % 2) * 16 + z * 4 + y, (x // 2) * 2 + core)


def moved(place, axis, by):
    x, y, z, core = place
    if axis == "x":
        return dev((x + by + 4) % 4, y, z, core)
    if axis == "y":
        return dev(x, (y + by + 4) % 4, z, core)
    return dev(x, y, (z + by + 4) % 4, core)


def along(place, axis):
    return place["xyz".index(axis)]


def greet(devices):
    barrier = pltpu.get_barrier_semaphore()
    for device in devices:
        pl.semaphore_signal(barrier, inc=1, device_id=device, device_id_type=MESH)
    pl.semaphore_wait(barrier, len(devices))


class Sems:
    def __init__(self, send, recv):
        self.send, self.recv, self.at = send, recv, 0
        self.started = []

    def copy(self, src, dst, device):
        i = self.at
        self.at += 1
        return pltpu.make_async_remote_copy(
            src_ref=src,
            dst_ref=dst,
            send_sem=self.send.at[i],
            recv_sem=self.recv.at[i],
            device_id=device,
            device_id_type=MESH,
        )

    def start(self, src, dst, device):
        copy = self.copy(src, dst, device)
        copy.start()
        self.started.append(copy)
        return copy

    def finish(self):
        for copy in self.started:
            copy.wait_send()


def call(kernel, out_shape, scratch, n_sems, cid, args, specs=None):
    vmem = pl.BlockSpec(memory_space=pltpu.VMEM)
    outs = jax.tree.map(lambda _: vmem, out_shape)
    return pl.pallas_call(
        kernel,
        out_shape=out_shape,
        in_specs=specs if specs is not None else [vmem] * len(args),
        out_specs=outs,
        scratch_shapes=[
            *scratch,
            pltpu.SemaphoreType.DMA((n_sems,)),
            pltpu.SemaphoreType.DMA((n_sems,)),
        ],
        compiler_params=pltpu.CompilerParams(
            collective_id=cid, has_side_effects=True, vmem_limit_bytes=VLIM
        ),
    )(*args)


def pair_of(place):
    x, y, z, core = place
    return dev(x, y, z, 1 - core), dev(3 - x, y, z, core)


def start_kernel(w_ref, t_ref, w_out, t_out, local_sem, send, recv):
    place = my_place()
    x, y, z, core = place
    sibling, cross = pair_of(place)
    greet([sibling, cross])
    sems = Sems(send, recv)
    mine = (x // 2) * 2 + core
    theirs = (1 - x // 2) * 2 + core
    pieces = [pl.ds(48 * i, 48) for i in range(5)]
    over = [sems.start(w_ref.at[p], w_out.at[mine, p], cross) for p in pieces]
    toks = sems.start(t_ref, t_out.at[:, :, core], sibling)
    own = sems.start(w_ref, w_out.at[mine], sibling)
    keep = [
        pltpu.make_async_copy(w_ref, w_out.at[mine], local_sem.at[0]),
        pltpu.make_async_copy(t_ref, t_out.at[:, :, core], local_sem.at[1]),
    ]
    for copy in keep:
        copy.start()
    passed = []
    for copy, p in zip(over, pieces):
        copy.wait_recv()
        passed.append(sems.start(w_out.at[theirs, p], w_out.at[theirs, p], sibling))
    for copy in [toks, own, *passed]:
        copy.wait_recv()
    for copy in keep:
        copy.wait()
    sems.finish()


def group_kernel(a_ref, out_ref, local_sem, send, recv):
    place = my_place()
    core = place[3]
    sibling, cross = pair_of(place)
    greet([sibling, cross])
    sems = Sems(send, recv)
    pieces = [pl.ds(64 * i, 64) for i in range(4)]
    over = [sems.start(a_ref.at[p], out_ref.at[1, core, p], cross) for p in pieces]
    own = sems.start(a_ref, out_ref.at[0, core], sibling)
    keep = pltpu.make_async_copy(a_ref, out_ref.at[0, core], local_sem.at[0])
    keep.start()
    passed = []
    for copy, p in zip(over, pieces):
        copy.wait_recv()
        passed.append(sems.start(out_ref.at[1, core, p], out_ref.at[1, core, p], sibling))
    for copy in [own, *passed]:
        copy.wait_recv()
    keep.wait()
    sems.finish()


def group_gather(array, cid):
    return call(
        group_kernel,
        jax.ShapeDtypeStruct((2, 2, *array.shape), array.dtype),
        [pltpu.SemaphoreType.DMA((1,))],
        9,
        cid,
        (array,),
    )


def group_sum_kernel(p_ref, out_ref, got, total, far, send, recv):
    place = my_place()
    core = place[3]
    sibling, cross = pair_of(place)
    greet([sibling, cross])
    sems = Sems(send, recv)
    in_other = [sems.start(p_ref.at[1, h, 1 - core], got.at[1, h], sibling) for h in range(2)]
    in_own = [sems.start(p_ref.at[0, h, 1 - core], got.at[0, h], sibling) for h in range(2)]
    over = []
    for h in range(2):
        in_other[h].wait_recv()
        total[1, h] = (p_ref[1, h, core].astype(f32) + got[1, h].astype(f32)).astype(bf16)
        over.append(sems.start(total.at[1, h], far.at[h], cross))
    last = []
    for h in range(2):
        in_own[h].wait_recv()
        over[h].wait_recv()
        out_ref[h, core] = (
            p_ref[0, h, core].astype(f32) + got[0, h].astype(f32) + far[h].astype(f32)
        ).astype(bf16)
        last.append(sems.start(out_ref.at[h, core], out_ref.at[h, core], sibling))
    for copy in last:
        copy.wait_recv()
    sems.finish()


def group_sum(part, cid):
    rows = (2, 64, D)
    return call(
        group_sum_kernel,
        jax.ShapeDtypeStruct((2, 2, 64, D), bf16),
        [pltpu.VMEM((2, *rows), bf16), pltpu.VMEM((2, *rows), bf16), pltpu.VMEM(rows, bf16)],
        8,
        cid,
        (part,),
    )


orders = (("z", "y", "x"), ("y", "x", "z"), ("x", "z", "y"))


def chips(ref, place, free, axis, at, rows):
    x, y, z, _ = place
    index = {"x": x, "y": y, "z": z}
    index[axis] = at
    every = slice(None)
    xlo, xhi = (every, every) if "x" in free else (index["x"] % 2, index["x"] // 2)
    return ref.at[
        xlo, every if "z" in free else index["z"], every if "y" in free else index["y"], xhi, rows
    ]


def kv_gather_kernel(own_ref, all_ref, local_sem, send, recv):
    place = my_place()
    x, y, z, core = place
    greet([moved(place, a, b) for a in "xyz" for b in (1, -1)])
    sems = Sems(send, recv)
    parts = [(0, 48, 48), (96, 48, 48), (192, 48, 32)]
    keep = pltpu.make_async_copy(own_ref, all_ref.at[x % 2, z, y, x // 2], local_sem.at[0])
    keep.start()
    keep.wait()
    for stage in range(3):
        firsts = []
        for (row, n0, n1), order in zip(parts, orders):
            axis, free = order[stage], order[:stage]
            at = along(place, axis)
            here = chips(all_ref, place, free, axis, at, pl.ds(row, n0 + n1))
            firsts.append(
                [sems.start(here, here, moved(place, axis, by)) for by in (1, -1)]
            )
        seconds = []
        for (row, n0, n1), order, (to_right, to_left) in zip(parts, orders, firsts):
            axis, free = order[stage], order[:stage]
            at = along(place, axis)
            to_right.wait_recv()
            left = chips(all_ref, place, free, axis, (at + 3) % 4, pl.ds(row, n0))
            seconds.append(sems.start(left, left, moved(place, axis, 1)))
            to_left.wait_recv()
            right = chips(all_ref, place, free, axis, (at + 1) % 4, pl.ds(row + n0, n1))
            seconds.append(sems.start(right, right, moved(place, axis, -1)))
        for copy in seconds:
            copy.wait_recv()
    sems.finish()


def kv_gather(chunk, cid):
    return call(
        kv_gather_kernel,
        jax.ShapeDtypeStruct((2, 4, 4, 2, KROWS, 128), bf16),
        [pltpu.SemaphoreType.DMA((1,))],
        36,
        cid,
        (chunk,),
    )


def added(into, terms, shape):
    if not shape:
        into[...] = sum([t[...].astype(f32) for t in terms], into[...].astype(f32)).astype(bf16)
        return

    def one(i, carry):
        rest, index = i, []
        for size in reversed(shape):
            index.insert(0, rest % size)
            rest = rest // size
        index = tuple(index)
        into[index] = sum(
            [t[index].astype(f32) for t in terms], into[index].astype(f32)
        ).astype(bf16)
        return carry

    lax.fori_loop(0, math.prod(shape), one, 0)


def ring_sum(place, sems, jobs):
    state = []
    for axis, view, land, shape in jobs:
        at = along(place, axis)
        right, left = moved(place, axis, 1), moved(place, axis, -1)
        far = (at + 2) % 4
        state.append(
            (
                sems.start(view(far, 1), land[0], right),
                sems.start(view(far, 0), land[1], left),
                sems.start(view((at + 1) % 4, 0), land[2], right),
                sems.start(view((at + 3) % 4, 1), land[3], left),
            )
        )
    lasts = []
    for (axis, view, land, shape), (far_right, far_left, _, _) in zip(jobs, state):
        at = along(place, axis)
        right, left = moved(place, axis, 1), moved(place, axis, -1)
        far_right.wait_recv()
        added(view((at + 1) % 4, 1), [land[0]], shape)
        one = sems.start(view((at + 1) % 4, 1), land[4], right)
        far_left.wait_recv()
        added(view((at + 3) % 4, 0), [land[1]], shape)
        lasts.append((one, sems.start(view((at + 3) % 4, 0), land[5], left)))
    for (axis, view, land, shape), (_, _, near_r, near_l), (one, two) in zip(jobs, state, lasts):
        at = along(place, axis)
        near_r.wait_recv()
        two.wait_recv()
        added(view(at, 0), [land[2], land[5]], shape)
        near_l.wait_recv()
        one.wait_recv()
        added(view(at, 1), [land[3], land[4]], shape)


sum_parts = [(0, 48, 48), (96, 48, 48), (192, 32, 32)]


def kv_lead(free):
    return sum([(2, 2) if a == "x" else (4,) for a in free], ())


def kv_shape(free):
    lead = ()
    if "x" in free:
        lead += (2,)
    if "z" in free:
        lead += (4,)
    if "y" in free:
        lead += (4,)
    if "x" in free:
        lead += (2,)
    return lead


def kv_sum_kernel(part_ref, out_ref, work, local_sem, *rest):
    lands, (send, recv) = rest[:-2], rest[-2:]
    place = my_place()
    x, y, z, core = place
    greet([moved(place, a, b) for a in "xyz" for b in (1, -1)])
    keep = pltpu.make_async_copy(part_ref, work, local_sem.at[0])
    keep.start()
    keep.wait()
    sems = Sems(send, recv)
    at_land = 0
    for stage in range(3):
        jobs = []
        for (row, n0, n1), order in zip(sum_parts, orders):
            axis, free = order[stage], order[stage + 1 :]

            def view(at, half, row=row, n0=n0, n1=n1, axis=axis, free=free):
                rows = pl.ds(row, n0) if half == 0 else pl.ds(row + n0, n1)
                return chips(work, place, free, axis, at, rows)

            jobs.append((axis, view, lands[at_land : at_land + 6], kv_shape(free)))
            at_land += 6
        ring_sum(place, sems, jobs)
    out_ref[...] = work[x % 2, z, y, x // 2].astype(f32)
    sems.finish()


def kv_sum(part, cid):
    lands = []
    for stage in range(3):
        for (row, n0, n1), order in zip(sum_parts, orders):
            lead = kv_shape(order[stage + 1 :])
            for n in (n1, n0, n0, n1, n1, n0):
                lands.append(pltpu.VMEM((*lead, n, 128), bf16))
    shape = (2, 4, 4, 2, CHIP, 128)
    return call(
        kv_sum_kernel,
        jax.ShapeDtypeStruct((CHIP, 128), f32),
        [pltpu.VMEM(shape, bf16), pltpu.SemaphoreType.DMA((1,)), *lands],
        54,
        cid,
        (part,),
    )


weight_parts = [
    (0, 0, 32, 32, "zy"),
    (0, 64, 16, 32, "yz"),
    (1, 0, 32, 16, "zy"),
    (1, 48, 32, 32, "yz"),
]
wide = (FS, D)
chunk_rows = 112


def weight_view(ref, place, first, at, rows, second=None):
    _, y, z, _ = place
    every = slice(None)
    if second is None:
        return ref.at[at, every, rows] if first == "z" else ref.at[every, at, rows]
    return ref.at[z, at, rows] if first == "z" else ref.at[at, y, rows]


def weight_kernel(gate, up, down, rest_ref, out_a, out_b, work_a, work_b, local_sem, *more):
    lands, (send, recv) = more[:-2], more[-2:]
    place = my_place()
    x, y, z, core = place
    mate = dev(x + 1 - 2 * (x % 2), y, z, core)
    works, outs = (work_a, work_b), (out_a, out_b)
    loads = [
        pltpu.make_async_copy(gate, work_a.at[0:2], local_sem.at[0]),
        pltpu.make_async_copy(up, work_a.at[2:4], local_sem.at[1]),
        pltpu.make_async_copy(down, work_b.at[0:2], local_sem.at[2]),
        pltpu.make_async_copy(rest_ref, work_b.at[2:4], local_sem.at[3]),
    ]
    for copy in loads:
        copy.start()
    greet([moved(place, a, b) for a in "yz" for b in (1, -1)] + [mate])
    for copy in loads:
        copy.wait()
    sems = Sems(send, recv)
    at_land = 0
    for stage in range(2):
        jobs = []
        for buf, row, n0, n1, order in weight_parts:

            def view(at, half, buf=buf, row=row, n0=n0, n1=n1, order=order):
                rows = pl.ds(row, n0) if half == 0 else pl.ds(row + n0, n1)
                if stage == 0:
                    return weight_view(works[buf], place, order[0], at, rows)
                return weight_view(works[buf], place, order[0], at, rows, order[1])

            jobs.append(
                (order[stage], view, lands[at_land : at_land + 6], (4,) if stage == 0 else ())
            )
            at_land += 6
        ring_sum(place, sems, jobs)
    swaps = []
    for buf, row, n0, n1, order in weight_parts:
        mine = works[buf].at[z, y, pl.ds(row, n0 + n1)]
        swaps.append(sems.start(mine, lands[at_land], mate))
        at_land += 1
    for i, ((buf, row, n0, n1, order), copy) in enumerate(zip(weight_parts, swaps)):
        copy.wait_recv()
        rows = pl.ds(row, n0 + n1)
        land = lands[at_land - len(weight_parts) + i]
        outs[buf][z, y, rows] = (
            works[buf][z, y, rows].astype(f32) + land[...].astype(f32)
        ).astype(bf16)
    for stage in (1, 0):
        firsts = []
        for buf, row, n0, n1, order in weight_parts:
            axis = order[stage]
            rows = pl.ds(row, n0 + n1)
            second = order[1] if stage == 1 else None
            here = weight_view(outs[buf], place, order[0], along(place, axis), rows, second)
            firsts.append([sems.start(here, here, moved(place, axis, by)) for by in (1, -1)])
        seconds = []
        for (buf, row, n0, n1, order), (to_right, to_left) in zip(weight_parts, firsts):
            axis = order[stage]
            at = along(place, axis)
            second = order[1] if stage == 1 else None
            to_right.wait_recv()
            left = weight_view(
                outs[buf], place, order[0], (at + 3) % 4, pl.ds(row, n0), second
            )
            seconds.append(sems.start(left, left, moved(place, axis, 1)))
            to_left.wait_recv()
            right = weight_view(
                outs[buf], place, order[0], (at + 1) % 4, pl.ds(row + n0, n1), second
            )
            seconds.append(sems.start(right, right, moved(place, axis, -1)))
        for copy in seconds:
            copy.wait_recv()
    sems.finish()


def weight_sum(gate, up, down, rest, cid):
    lands = []
    for stage in range(2):
        for buf, row, n0, n1, order in weight_parts:
            lead = (4,) if stage == 0 else ()
            for n in (n1, n0, n0, n1, n1, n0):
                lands.append(pltpu.VMEM((*lead, n, wide[buf]), bf16))
    for buf, row, n0, n1, order in weight_parts:
        lands.append(pltpu.VMEM((n0 + n1, wide[buf]), bf16))
    big = [(4, 4, chunk_rows, w) for w in wide]
    half = (2, 4, chunk_rows)
    args = (
        gate.reshape(*half, FS),
        up.reshape(*half, FS),
        down.reshape(*half, D),
        rest.reshape(*half, D),
    )
    return call(
        weight_kernel,
        tuple(jax.ShapeDtypeStruct(s, bf16) for s in big),
        [*[pltpu.VMEM(s, bf16) for s in big], pltpu.SemaphoreType.DMA((4,)), *lands],
        4 * 6 * 2 + 4 + 4 * 4 * 2,
        cid,
        args,
        [pl.BlockSpec(memory_space=pl.ANY)] * 4,
    )


NT = (((1,), (1,)), ((), ()))
ROWS = G * 128


def lanes(shape):
    return lax.broadcasted_iota(jnp.int32, shape, len(shape) - 1)


def split3(value):
    one = value.astype(bf16).astype(f32)
    two = (value - one).astype(bf16).astype(f32)
    three = (value - one - two).astype(bf16).astype(f32)
    return one, two, three


def keys_of(kv_ref, c, half):
    rows = pl.ds(pl.multiple_of(half * 128, 128), 128)
    tile = kv_ref[c, :, rows, :].reshape(256, 128)
    lane = lanes((256, 128))
    ones = jnp.ones((256, 128), bf16)
    return jnp.where(lane < HD, tile, ones), jnp.where(lane < HD, ones, tile)


def hidden_keys(xhi):
    row = lax.broadcasted_iota(jnp.int32, (ROWS, 256), 0) % 128
    key = lax.broadcasted_iota(jnp.int32, (ROWS, 256), 1)
    return key > row + xhi * 128


def forward_kernel(scal, q_ref, kv_ref, o_ref, qe_ref, peak, acc):
    me, xhi = scal[32], scal[33]
    lane = lanes((128, 128))
    for h in range(2):
        for g in range(G):
            piece = q_ref[h, :, g * HD : (g + 1) * HD].astype(f32) * (1.0 / math.sqrt(HD))
            wide_piece = jnp.concatenate([piece, jnp.zeros((128, HD), f32)], 1)
            qe_ref[h, g * 128 : (g + 1) * 128, :] = wide_piece.astype(bf16)
    peak[...] = jnp.full((2, ROWS, 128), -1e30, f32)
    acc[...] = jnp.zeros((2, ROWS, 128), f32)

    def scores(half, kk):
        return lax.dot_general(qe_ref[half], kk, NT, preferred_element_type=f32)

    def top(half, s):
        peak[half] = jnp.maximum(peak[half], jnp.maximum(s[:, :128], s[:, 128:]))

    def fold(half, s, vv):
        p = jnp.exp(s).astype(bf16)
        acc[half] += jnp.dot(p, vv, preferred_element_type=f32)

    def others(work):
        def one(i, carry):
            c = (me + i) % 32
            kk, vv = keys_of(kv_ref, c, 0)
            work(1, kk, vv, None)
            sel = scal[c]
            kk, vv = keys_of(kv_ref, c, sel)
            work(sel, kk, vv, None)
            return carry

        lax.fori_loop(1, 32, one, 0)
        early_k, early_v = keys_of(kv_ref, me, 0)
        late_k, late_v = keys_of(kv_ref, me, 1)
        work(1, early_k, early_v, None)
        work(0, early_k, early_v, hidden_keys(xhi))
        work(1, late_k, late_v, hidden_keys(xhi))

    def first(half, kk, vv, hide):
        s = scores(half, kk)
        top(half, s if hide is None else jnp.where(hide, -1e30, s))

    def second(half, kk, vv, hide):
        s = scores(half, kk)
        fold(half, s if hide is None else jnp.where(hide, -1e30, s), vv)

    others(first)
    wide_lane = lanes((ROWS, 128))

    def with_column(half, column):
        one, two, three = split3(-column)
        held = qe_ref[half].astype(f32)
        held = jnp.where(wide_lane == HD, one, held)
        held = jnp.where(wide_lane == HD + 1, two, held)
        held = jnp.where(wide_lane == HD + 2, three, held)
        qe_ref[half] = held.astype(bf16)

    for h in range(2):
        highest = jnp.max(peak[h], 1, keepdims=True)
        peak[h] = jnp.broadcast_to(highest, (ROWS, 128))
        with_column(h, highest)
    others(second)
    for h in range(2):
        total = acc[h][:, :1]
        with_column(h, peak[h][:, :1] + jnp.log(total))
        out = acc[h] / total
        for g in range(G):
            o_ref[h, :, g * HD : (g + 1) * HD] = out[g * 128 : (g + 1) * 128, HD:]


def local_call(kernel, out_shape, scratch, args, flops):
    vmem = pl.BlockSpec(memory_space=pltpu.VMEM)
    return pl.pallas_call(
        kernel,
        out_shape=out_shape,
        in_specs=[pl.BlockSpec(memory_space=pltpu.SMEM)] + [vmem] * (len(args) - 1),
        out_specs=jax.tree.map(lambda _: vmem, out_shape),
        scratch_shapes=scratch,
        compiler_params=pltpu.CompilerParams(vmem_limit_bytes=VLIM),
        cost_estimate=pl.CostEstimate(
            flops=flops, bytes_accessed=10_000_000, transcendentals=15_000_000
        ),
    )(*args)


def attention_forward(scal, q, kv):
    return local_call(
        forward_kernel,
        (
            jax.ShapeDtypeStruct((2, 128, QC), f32),
            jax.ShapeDtypeStruct((2, ROWS, 128), bf16),
        ),
        [pltpu.VMEM((2, ROWS, 128), f32), pltpu.VMEM((2, ROWS, 128), f32)],
        (scal, q, kv),
        20_000_000_000,
    )


def backward_kernel(scal, qe_ref, o_ref, g_ref, kv_ref, dq_ref, dkv_ref, ge, qt, gt, dq, step):
    me, xhi = scal[32], scal[33]
    lane = lanes((128, 128))
    for h in range(2):
        for g in range(G):
            cols = slice(g * HD, (g + 1) * HD)
            piece = g_ref[h, :, cols].astype(f32)
            delta = jnp.sum(piece * o_ref[h, :, cols], 1, keepdims=True)
            one, two, three = split3(-delta)
            held = jnp.concatenate([jnp.zeros((128, HD), f32), piece], 1)
            held = jnp.where(lane == 0, one, held)
            held = jnp.where(lane == 1, two, held)
            held = jnp.where(lane == 2, three, held)
            rows = slice(g * 128, (g + 1) * 128)
            ge[h, rows, :] = held.astype(bf16)
            gt[h, :, rows] = held.T.astype(bf16)
            qt[h, :, rows] = qe_ref[h, rows, :].astype(f32).T.astype(bf16)
    dq[...] = jnp.zeros((2, ROWS, 128), f32)
    under = lax.broadcasted_iota(jnp.int32, (128, 256), 0) < HD

    def tile(half, kk, vv, hide):
        s = lax.dot_general(qe_ref[half], kk, NT, preferred_element_type=f32)
        if hide is not None:
            s = jnp.where(hide, -1e30, s)
        p = jnp.exp(s)
        dp = lax.dot_general(ge[half], vv, NT, preferred_element_type=f32)
        ds = (p * dp).astype(bf16)
        dq[half] += jnp.dot(ds, kk, preferred_element_type=f32)
        dk = jnp.dot(qt[half], ds, preferred_element_type=f32)
        dv = jnp.dot(gt[half], p.astype(bf16), preferred_element_type=f32)
        return jnp.where(under, dk, dv).T

    def put(c, half, value):
        rows = pl.ds(pl.multiple_of(half * 128, 128), 128)
        dkv_ref[c, :, rows, :] = value.astype(bf16).reshape(2, 128, 128)

    def one(i, carry):
        c = (me + i) % 32
        kk, vv = keys_of(kv_ref, c, 0)
        step[0] = tile(1, kk, vv, None)
        step[1] = jnp.zeros((256, 128), f32)
        sel = scal[c]
        kk, vv = keys_of(kv_ref, c, sel)
        step[sel] += tile(sel, kk, vv, None)
        put(c, 0, step[0])
        put(c, 1, step[1])
        return carry

    lax.fori_loop(1, 32, one, 0)
    early_k, early_v = keys_of(kv_ref, me, 0)
    late_k, late_v = keys_of(kv_ref, me, 1)
    put(
        me,
        0,
        tile(1, early_k, early_v, None) + tile(0, early_k, early_v, hidden_keys(xhi)),
    )
    put(me, 1, tile(1, late_k, late_v, hidden_keys(xhi)))
    for h in range(2):
        for g in range(G):
            dq_ref[h, :, g * HD : (g + 1) * HD] = dq[h, g * 128 : (g + 1) * 128, :HD] * (
                1.0 / math.sqrt(HD)
            )


def attention_backward(scal, qe, o, grad, kv):
    return local_call(
        backward_kernel,
        (
            jax.ShapeDtypeStruct((2, 128, QC), f32),
            jax.ShapeDtypeStruct((32, 2, CHIP, 128), bf16),
        ),
        [
            pltpu.VMEM((2, ROWS, 128), bf16),
            pltpu.VMEM((2, 128, ROWS), bf16),
            pltpu.VMEM((2, 128, ROWS), bf16),
            pltpu.VMEM((2, ROWS, 128), f32),
            pltpu.VMEM((2, 256, 128), f32),
        ],
        (scal, qe, o, grad, kv),
        50_000_000_000,
    )


def rms_inverse(values):
    return lax.rsqrt(jnp.mean(values * values, -1, keepdims=True) + norm_eps)


def rms_pull(values, inverse, gain, grad):
    scaled = values * inverse
    e = grad * gain
    return inverse * (e - scaled * jnp.mean(e * scaled, -1, keepdims=True))


def rotation(positions):
    frequency = rope_base ** (-(2.0 * jnp.arange(HD // 2, dtype=f32)) / HD)
    angles = positions.astype(f32)[:, None] * frequency[None, :]
    cosine, sine = jnp.cos(angles), jnp.sin(angles)
    return (
        jnp.tile(jnp.concatenate([cosine, cosine], 1), (1, G + 1)),
        jnp.tile(jnp.concatenate([-sine, sine], 1), (1, G + 1)),
    )


def swapped(values):
    heads = values.shape[1] // HD
    parts = values.reshape(-1, heads, 2, HD // 2)
    return jnp.flip(parts, 2).reshape(values.shape)


def dot(a, b):
    return jnp.dot(a, b, preferred_element_type=f32)


def body(
    tokens,
    out_grad,
    norm1_gain,
    qkv_weight,
    qkv_bias,
    out_weight,
    norm2_gain,
    gate_weight,
    up_weight,
    down_weight,
    positions,
):
    ctx = lax.axis_index("ctx")
    wsh = lax.axis_index("wsh")
    xhi, core = wsh // 2, wsh % 2
    my_block = positions[0] // 256

    def cut(array, start, size, axis):
        return lax.dynamic_slice_in_dim(array, start, size, axis)

    def own_rows(array):
        return cut(array.reshape(2, 2, 64, -1), core, 1, 1).reshape(TOK, -1)

    swap = [
        (c * 4 + w, ((c + 16) % 32) * 4 + (w + 2) % 4) for c in range(32) for w in range(4)
    ]
    twin = [(c * 4 + w, c * 4 + w + 1 - 2 * (w % 2)) for c in range(32) for w in range(4)]

    def crossed(array):
        return lax.ppermute(array, ("ctx", "wsh"), swap)

    small = jnp.stack(
        [jnp.pad(v, (0, QKV - v.shape[0])) for v in (qkv_bias, norm1_gain, norm2_gain)]
    )
    w_in = jnp.concatenate([qkv_weight, jnp.pad(small, ((0, 13), (0, 0)))], 0)
    t_in = jnp.stack([tokens, out_grad]).reshape(2, 2, 64, D)
    w_all, t_all = call(
        start_kernel,
        (
            jax.ShapeDtypeStruct((4, 240, QKV), bf16),
            jax.ShapeDtypeStruct((2, 2, 2, 64, D), bf16),
        ),
        [pltpu.SemaphoreType.DMA((2,))],
        12,
        0,
        (w_in, t_in),
    )
    out_full = lax.all_gather(out_weight, "wsh", axis=0, tiled=True)
    qkv_full = w_all[:, :224].reshape(D, QKV)
    bias_full = w_all[:, 224, :288].reshape(QKV).astype(f32)
    gain_one = w_all[:, 225, :224].reshape(D).astype(f32)
    gain_two = w_all[:, 226, :224].reshape(D).astype(f32)
    t_chip = t_all.reshape(2, CHIP, D)

    def my_columns(array):
        return jnp.concatenate(
            [
                cut(array, core * QC, QC, array.ndim - 1),
                cut(array, H * HD + core * HD, HD, array.ndim - 1),
                cut(array, (H + KVH) * HD + core * HD, HD, array.ndim - 1),
            ],
            -1,
        )

    resid = t_chip[0].astype(f32)
    normed_one = (resid * rms_inverse(resid) * gain_one).astype(bf16)
    projected = dot(normed_one, my_columns(qkv_full)) + my_columns(bias_full)
    offset = jnp.arange(128, dtype=jnp.int32) + xhi * 128
    cosine, sine = rotation(
        jnp.concatenate([my_block * 256 + offset, (63 - my_block) * 256 + offset])
    )
    turning = projected[:, : QC + HD]
    turned = (turning * cosine + swapped(turning) * sine).astype(bf16)
    queries = turned[:, :QC].reshape(2, 128, QC)
    chunk = jnp.concatenate([turned[:, QC:], projected[:, QC + HD :].astype(bf16)], 1)
    mark = jnp.broadcast_to(my_block.astype(bf16), (KROWS - CHIP, 128))
    kv_all = kv_gather(jnp.concatenate([chunk, mark], 0), 1).reshape(32, 2, KROWS, 128)
    blocks = kv_all[:, 0, CHIP, 0].astype(jnp.int32)
    scal = jnp.concatenate(
        [(blocks > my_block).astype(jnp.int32), jnp.stack([ctx, xhi]).astype(jnp.int32)]
    )
    t_chip, kv_all = lax.optimization_barrier((t_chip, kv_all))
    t_other = crossed(t_chip)
    attended_f, qe = attention_forward(scal, queries, kv_all)
    att = group_gather(attended_f.astype(bf16).reshape(CHIP, QC), 2)
    t_both = jnp.stack([t_chip, t_other], 1).reshape(2, 2 * CHIP, D)
    resid_both = t_both[0].astype(f32)
    cot = t_both[1]
    att_cols = [att[:, i].reshape(2 * CHIP, QC) for i in range(2)]
    stream = resid_both + dot(att_cols[0], out_full[:QC]) + dot(att_cols[1], out_full[QC:])
    inv_two = rms_inverse(stream)
    normed_two = (stream * inv_two * gain_two).astype(bf16)
    gate_pre = dot(normed_two, gate_weight)
    up_pre = dot(normed_two, up_weight)
    hidden_grad = jnp.einsum("td,fd->tf", cot, down_weight, preferred_element_type=f32)
    sigma = jax.nn.sigmoid(gate_pre)
    activated = gate_pre * sigma
    hidden = (activated * up_pre).astype(bf16)
    gate_grad = (hidden_grad * up_pre * sigma * (1.0 + gate_pre * (1.0 - sigma))).astype(bf16)
    up_grad = (hidden_grad * activated).astype(bf16)
    norm_part = jnp.einsum(
        "tf,df->td", gate_grad, gate_weight, preferred_element_type=f32
    ) + jnp.einsum("tf,df->td", up_grad, up_weight, preferred_element_type=f32)
    norm_grad = group_sum(norm_part.astype(bf16).reshape(2, 2, 2, 64, D), 3).reshape(CHIP, D)

    mlp_part = dot(hidden, down_weight).astype(bf16).reshape(2, 2, 2, 64, D)
    norm_other = crossed(norm_grad)
    mlp_got = lax.ppermute(cut(mlp_part, 1 - core, 1, 2), ("ctx", "wsh"), twin)
    mlp_sum = cut(mlp_part, core, 1, 2).astype(f32) + mlp_got.astype(f32)
    mlp_far = crossed(mlp_sum[1].astype(bf16))
    mlp_own = (mlp_sum[0] + mlp_far.astype(f32)).reshape(TOK, D)
    output = (own_rows(stream[:CHIP]) + mlp_own).astype(bf16)
    gate_wgrad = jnp.einsum("td,tf->df", normed_two, gate_grad, preferred_element_type=f32)
    up_wgrad = jnp.einsum("td,tf->df", normed_two, up_grad, preferred_element_type=f32)
    down_wgrad = jnp.einsum("tf,td->fd", hidden, cot, preferred_element_type=f32)

    def stream_pull(part, grad):
        rows = slice(part * CHIP, (part + 1) * CHIP)
        return cot[rows].astype(f32) + rms_pull(
            stream[rows], inv_two[rows], gain_two, grad.astype(f32)
        )

    stream_grad = stream_pull(0, norm_grad)
    branch_grad = stream_grad.astype(bf16)
    att_grad = jnp.einsum(
        "td,id->ti", branch_grad, cut(out_full, core * QC, QC, 0), preferred_element_type=f32
    ).astype(bf16)
    dq, dkv_part = attention_backward(
        scal, qe, attended_f, att_grad.reshape(2, 128, QC), kv_all
    )
    dkv = kv_sum(dkv_part.reshape(2, 4, 4, 2, CHIP, 128), 4)
    turning = jnp.concatenate([dq.reshape(CHIP, QC), dkv[:, :HD]], 1)
    turned = turning * cosine - swapped(turning) * sine
    pg_mine = jnp.concatenate([turned, dkv[:, HD:]], 1).astype(bf16)
    pg = group_gather(pg_mine, 5)
    pg = jnp.concatenate(
        [
            pg[:, 0, :, :QC],
            pg[:, 1, :, :QC],
            pg[:, 0, :, QC : QC + HD],
            pg[:, 1, :, QC : QC + HD],
            pg[:, 0, :, QC + HD :],
            pg[:, 1, :, QC + HD :],
        ],
        -1,
    ).reshape(2 * CHIP, QKV)

    bias_grad = cut(jnp.sum(pg.astype(f32), 0), wsh * 288, 288, 0)
    inv_one = rms_inverse(resid_both)
    scaled_one = cut(resid_both, wsh * 224, 224, 1) * inv_one
    normed_cols = (scaled_one * norm1_gain.astype(f32)).astype(bf16)
    qkv_wgrad = jnp.einsum("td,tf->df", normed_cols, pg, preferred_element_type=f32)
    one_cols = jnp.einsum("tf,df->td", pg, qkv_weight, preferred_element_type=f32)
    gain_one_grad = jnp.sum(one_cols * scaled_one, 0)
    branch_both = jnp.concatenate(
        [branch_grad, stream_pull(1, norm_other).astype(bf16)], 0
    )
    norm_both = jnp.concatenate([norm_grad, norm_other], 0)
    scaled_two = cut(stream, wsh * 224, 224, 1) * inv_two
    gain_two_grad = jnp.sum(cut(norm_both, wsh * 224, 224, 1).astype(f32) * scaled_two, 0)
    att_mine = cut(jnp.where(wsh < 2, att_cols[0], att_cols[1]), (wsh % 2) * 224, 224, 1)
    out_wgrad = jnp.einsum("ti,td->id", att_mine, branch_both, preferred_element_type=f32)
    pg_own = own_rows(pg[:CHIP])
    one_grad = jnp.einsum("tf,df->td", pg_own, qkv_full, preferred_element_type=f32)
    resid_own = tokens.astype(f32)
    token_grad = own_rows(stream_grad) + rms_pull(
        resid_own, rms_inverse(resid_own), gain_one, one_grad
    )
    vectors = jnp.stack(
        [jnp.pad(v, (0, D - v.shape[0])) for v in (bias_grad, gain_one_grad, gain_two_grad)]
    )
    down_low = down_wgrad.astype(bf16)
    rest = jnp.concatenate(
        [
            down_low[896:],
            out_wgrad.astype(bf16),
            qkv_wgrad.astype(bf16).reshape(288, D),
            jnp.pad(vectors, ((0, 61), (0, 0))).astype(bf16),
        ],
        0,
    )
    sum_a, sum_b = weight_sum(
        gate_wgrad.astype(bf16), up_wgrad.astype(bf16), down_low[:896], rest, 6
    )
    sum_a = sum_a.reshape(2 * D, FS).astype(f32)
    sum_b = sum_b.reshape(2 * D, D).astype(f32)
    return (
        output,
        token_grad,
        sum_b[1729, :224],
        sum_b[1440:1728].reshape(224, QKV),
        sum_b[1728, :288],
        sum_b[1216:1440],
        sum_b[1730, :224],
        sum_a[:D],
        sum_a[D:],
        sum_b[:1216],
    )


def solution(mesh):
    rows = P(("ctx", "wsh"), None)
    return jax.shard_map(
        body,
        mesh=mesh,
        in_specs=(
            rows,
            rows,
            P("wsh"),
            P("wsh", None),
            P("wsh"),
            P("wsh", None),
            P("wsh"),
            P(None, "wsh"),
            P(None, "wsh"),
            P("wsh", None),
            P(("ctx", "wsh")),
        ),
        out_specs=(
            rows,
            rows,
            P("wsh"),
            P("wsh", None),
            P("wsh"),
            P("wsh", None),
            P("wsh"),
            P(None, "wsh"),
            P(None, "wsh"),
            P("wsh", None),
        ),
        check_vma=False,
    )
```

time: 1810 us -> 544 us (0.30)
  waiting for transfers between devices: 1240 us -> 2.3 us
  Pallas kernels: 0 us -> 349 us
  matrix products: 194 us -> 29.8 us
  blocking collectives: 127 us -> 0 us
  loops' own time: 52.8 us -> 0 us
    ppermute x64 -> x4, waiting for transfers between devices: 473 us -> 1.62 us  [the longest x3 1.62 us: crossed(): return lax.ppermute(array, ('ctx', 'wsh'), swap)]
    pallas_call x0 -> x9, Pallas kernels: none -> 349 us  [the longest x7 252 us: call(): pl.pallas_call(kernel, out_shape=out_shape, in_specs=specs if specs is no...]
    reduce_scatter x6 -> x0, waiting for transfers between devices: 326 us -> none  [the longest x1 83.1 us: body(): lax.psum_scatter(up_wgrad.astype(jnp.bfloat16), 'wsh', scatter_dimension=...]
    psum x1 -> x0, waiting for transfers between devices: 243 us -> none  [body(): lax.psum(qkv_wgrad.astype(jnp.bfloat16), 'ctx').astype(jnp.float32)]
    all_gather x6 -> x1, waiting for transfers between devices: 196 us -> 0.01 us  [body(): out_full = lax.all_gather(out_weight, 'wsh', axis=0, tiled=True)]
    dot_general x470 -> x17, matrix products: 194 us -> 29.8 us  [the longest x6 10.5 us: dot(): return jnp.dot(a, b, preferred_element_type=f32)]
    psum x1 -> x0, blocking collectives: 83.4 us -> none  [body(): lax.psum(gain_one_grad.astype(jnp.bfloat16), 'ctx').astype(jnp.float32)]
    dynamic_slice x252 -> x7, local copies, waits for them, and re-layouts: 76.4 us -> 5.97 us  [cut(): return lax.dynamic_slice_in_dim(array, start, size, axis)]
  transfers between devices with their start and end apart: 77 -> 5, of which waited for: 74 -> 1; matrix products, arithmetic and copies ran while one was open for 11% -> 24% of each run, Pallas kernels for 0% -> 65%
where the time goes in v1:
time: 544 us; the launch traced here: 534 us
  Pallas kernels  349 us (64%)
  local copies, waits for them, and re-layouts  87.8 us (16%)
  other arithmetic  41.2 us (8%)
  matrix products  29.8 us (5%)
  between operations  17.9 us (3%)
  starting transfers between devices  5.87 us (1%)
    pallas_call x7, Pallas kernels, call(): pl.pallas_call(kernel, out_shape=out_shape, in_specs=specs if specs is no...  252 us
    pallas_call x2, Pallas kernels, local_call(): pl.pallas_call(kernel, out_shape=out_shape, in_specs=[pl.BlockSpec(memory...  97 us
    unnamed x104, local copies, waits for them, and re-layouts  19 us
  transfers between devices with their start and end apart: 5, of which 1 were waited for; matrix products, arithmetic and copies ran while one was open for 24% of the time, Pallas kernels for 65%

profile of v1, /device:TPU:0, one launch (start us, length us, event | category | flops | bytes accessed | tf_op | source)
XLA Modules:
  0.0 534.2 jit_solution(13237233742338981481)
XLA Ops:
  12.4 1.9 pad_maximum_fusion.4.t_ref
  14.3 1.9 pad_maximum_fusion.2.w_ref
  16.2 28.7 %shard_map.186 = (bf16[4,240,1152]{2,1,0:T(8,128)(2,1)}, bf16[2,2,2,64,896]{4,3,2,1,0:T(8,128)(2,1)}) custom-call(bf16[240,1152]{1,0:T(8,128)(2,1)} %pad_maximum_fusion.2.w_ref, bf16[2,2,64,896]{3,2,1,0:T(8,128)(2,1)} %pad_maximum_fusion.4.t_ref), custom_call_target="tpu_custom_call" | custom-call | tf_op jit(solution)/shard_map/pallas_call | solution.py:93
  45.7 1.4 convert_reduce_fusion.2
  47.1 3.1 slice.158
  52.8 2.6 constant_dynamic-slice_fusion.4
  58.4 1.4 reshape.320
  61.9 1.8 convolution_add_fusion
  67.8 2.0 copy.36
  70.7 2.0 copy.33
  72.7 2.0 copy.34
  74.8 1.9 rev.7
  76.6 2.0 copy.35
  78.7 1.7 add_convert_fusion.1
  81.2 40.2 %shard_map.187 = bf16[2,4,4,2,272,128]{5,4,3,2,1,0:T(8,128)(2,1)} custom-call(bf16[272,128]{1,0:T(8,128)(2,1)} %fusion.45.own_ref), custom_call_target="tpu_custom_call" | custom-call | tf_op jit(solution)/shard_map/pallas_call | solution.py:93
  121.4 1.6 collective-permute-start
  123.0 1.5 fusion.48
  125.1 43.4 %shard_map.188 = (f32[2,128,448]{2,1,0:T(8,128)}, bf16[2,896,128]{2,1,0:T(8,128)(2,1)}) custom-call(s32[34]{0:T(128)} %pad_add_fusion.scal, bf16[2,128,448]{2,1,0:T(8,128)(2,1)} %bitcast.187, bf16[32,2,272,128]{3,2,1,0:T(8,128)(2,1)} %bitcast.153), custom_call_target="tpu_custom_call" | custom-call | flops 20000000000 | bytes 10000000 | tf_op jit(solution)/shard_map/pallas_call | solution.py:609
  169.2 1.8 convert_element_type.218
  171.0 11.7 %shard_map.189 = bf16[2,2,256,448]{3,2,1,0:T(8,128)(2,1)} custom-call(bf16[256,448]{1,0:T(8,128)(2,1)} %bitcast.177), custom_call_target="tpu_custom_call" | custom-call | tf_op jit(solution)/shard_map/pallas_call | solution.py:93
  183.4 2.3 fusion.62
  187.5 2.9 pad_maximum_fusion.1
  190.4 2.2 fusion.16
  192.6 2.0 multiply_reduce_fusion.1
  194.8 2.0 copy-done.48
  196.8 1.5 fusion.66
  198.8 1.5 fusion.65
  200.3 2.6 multiply_convert_fusion
  202.9 1.6 convolution_convert_fusion.4
  204.4 1.5 convolution_convert_fusion.2
  205.9 1.4 slice.216
  207.7 1.5 fusion.67
  209.3 1.5 convolution_convert_fusion.1
  211.9 2.5 add_convert_fusion
  214.4 13.4 %shard_map.190 = bf16[2,2,64,896]{3,2,1,0:T(8,128)(2,1)} custom-call(bf16[2,2,2,64,896]{4,3,2,1,0:T(8,128)(2,1)} %bitcast.178), custom_call_target="tpu_custom_call" | custom-call | tf_op jit(solution)/shard_map/pallas_call | solution.py:93
  227.9 1.8 collective-permute-start.3
  229.7 2.5 copy.46
  232.2 4.4 convolution_convert_fusion
  236.6 4.3 copy.47
  240.9 1.6 collective-permute-done.3
  242.5 1.4 multiply_reduce_fusion.2
  244.0 3.2 fusion.57
  249.2 53.6 %shard_map.191 = (f32[2,128,448]{2,1,0:T(8,128)}, bf16[32,2,256,128]{3,2,1,0:T(8,128)(2,1)}) custom-call(s32[34]{0:T(128)} %pad_add_fusion.scal, bf16[2,896,128]{2,1,0:T(8,128)(2,1)} %get-tuple-element.25.qe_ref, f32[2,128,448]{2,1,0:T(8,128)} %get-tuple-element.24.o_ref, bf16[2,128,448]{2,1,0:T(8,128)(2,1)} %bitcast.188, bf16[32,2,272,128]{3,2,1,0:T(8,128)(2,1)} %bitcast.154), custom_call_target="tpu_custom_call" | custom-call | flops 49999998976 | bytes 10000000 | tf_op jit(solution)/shard_map/pallas_call | solution.py:609
  302.8 37.4 %shard_map.192 = f32[256,128]{1,0:T(8,128)} custom-call(bf16[2,4,4,2,256,128]{5,4,3,2,1,0:T(8,128)(2,1)} %bitcast.155), custom_call_target="tpu_custom_call" | custom-call | tf_op jit(solution)/shard_map/pallas_call | solution.py:93
  341.3 1.8 pad_maximum_fusion.3
  343.1 2.1 copy.42
  345.2 1.9 rev.8
  347.1 2.0 copy.43
  349.1 1.6 subtract_convert_fusion
  351.4 12.9 %shard_map.193 = bf16[2,2,256,576]{3,2,1,0:T(8,128)(2,1)} custom-call(bf16[256,576]{1,0:T(8,128)(2,1)} %pad_maximum_fusion.5.a_ref), custom_call_target="tpu_custom_call" | custom-call | tf_op jit(solution)/shard_map/pallas_call | solution.py:93
  364.4 2.2 fusion.60
  370.1 2.0 collective-permute-start.2
  374.2 2.7 concatenate.85
  377.2 1.7 fusion.1
  378.9 2.0 convolution_convert_fusion.3
  380.9 1.4 reshape.316
  382.4 3.3 concatenate.77
  390.4 108.0 %shard_map.194 = (bf16[4,4,112,1216]{3,2,1,0:T(8,128)(2,1)}, bf16[4,4,112,896]{3,2,1,0:T(8,128)(2,1)}) custom-call(bf16[2,4,112,1216]{3,2,1,0:T(8,128)(2,1)} %bitcast.146, bf16[2,4,112,1216]{3,2,1,0:T(8,128)(2,1)} %bitcast.147, bf16[2,4,112,896]{3,2,1,0:T(8,128)(2,1)} %bitcast.150, bf16[2,4,112,896]{3,2,1,0:T(8,128)(2,1)} %bitcast.151), custom_call_target="tpu_custom_call" | custom-call | tf_op jit(solution)/shard_map/pallas_call | solution.py:93
  498.4 2.5 bitcast_convert_fusion
  501.6 4.7 fusion.59
  508.9 2.3 slice.227
  512.4 5.6 %copy.50 = f32[896,1216]{0,1:T(8,128)} copy(f32[896,1216]{1,0:T(8,128)} %bitcast.135) | data formatting | bytes 8716288
  518.0 5.7 %copy.49 = f32[896,1216]{0,1:T(8,128)} copy(f32[896,1216]{1,0:T(8,128)} %bitcast.134) | data formatting | bytes 8716288
  525.0 1.9 fusion.28
  (182 shorter events, 43.1 us)
Async XLA Ops:
  7.2 193.1 %copy-start = (bf16[1216,896]{1,0:T(8,128)(2,1)S(1)}, bf16[1216,896]{1,0:T(8,128)(2,1)}, u32[]{:S(2)}) copy-start(bf16[1216,896]{1,0:T(8,128)(2,1)} %param.20) | copy-start | bytes 6537220
  7.2 183.2 %all-gather.2.cloned.1.call-start = ((), (), s32[]{:S(2)}) async-start(), calls=%async_computation | async-start | bytes 2007040 | tf_op jit(solution)/shard_map/all_gather | solution.py:796
  50.2 5.1 copy-start.7
  63.7 0.8 copy-start.26
  80.4 41.0 %copy-start.37 = (bf16[256,512]{1,0:T(8,128)(2,1)}, bf16[256,512]{1,0:T(8,128)(2,1)S(1)}, u32[]{:S(2)}) copy-start(bf16[256,512]{1,0:T(8,128)(2,1)S(1)} %add_convert_fusion.1) | copy-start | bytes 786436
  121.4 64.2 %collective-permute-start = (bf16[2,256,896]{2,1,0:T(8,128)(2,1)S(1)}, bf16[2,256,896]{2,1,0:T(8,128)(2,1)}, u32[]{:S(2)}, u32[]{:S(2)}) collective-permute-start(bf16[2,256,896]{2,1,0:T(8,128)(2,1)S(1)} %bitcast.139), channel_id=1, source_target_pairs={{0,66},{1,67},{2,64},{3,65},{4,70},{5,71},{6,68},{7,69},{8,74},{9,... | collective-permute-start | bytes 2752520 | tf_op jit(solution)/shard_map/ppermute | solution.py:778
  125.1 43.4 %copy-start.47 = (bf16[224]{0:T(256)(128)(2,1)S(1)}, bf16[224]{0:T(256)(128)(2,1)}, u32[]{:S(2)}) copy-start(bf16[224]{0:T(256)(128)(2,1)} %param.13) | copy-start | bytes 1348
  125.1 44.0 %copy-start.43 = (f32[4,224]{1,0:T(4,128)S(1)}, f32[4,224]{1,0:T(4,128)}, u32[]{:S(2)}) copy-start(f32[4,224]{1,0:T(4,128)} %get-tuple-element.50) | copy-start | bytes 10756
  168.5 14.2 %copy-start.12 = (bf16[128,896]{1,0:T(8,128)(2,1)S(1)}, bf16[128,896]{1,0:T(8,128)(2,1)}, u32[]{:S(2)}) copy-start(bf16[128,896]{1,0:T(8,128)(2,1)} %param.11) | copy-start | bytes 688132
  169.2 25.4 %copy-start.38 = (f32[896]{0:T(1024)}, f32[896]{0:T(1024)S(1)}, u32[]{:S(2)}) copy-start(f32[896]{0:T(1024)S(1)} %reshape.324) | copy-start | bytes 10756
  190.4 2.2 copy-start.8
  190.4 2.2 copy-start.20
  194.5 3.8 copy-start.2
  194.5 2.3 copy-start.48
  194.5 3.8 copy-start.41
  196.8 12.5 %copy-start.31 = (bf16[512,896]{1,0:T(8,128)(2,1)}, bf16[512,896]{1,0:T(8,128)(2,1)S(1)}, u32[]{:S(2)}) copy-start(bf16[512,896]{1,0:T(8,128)(2,1)S(1)} %multiply_convert_fusion.3) | copy-start | bytes 2752516
  196.8 1.9 copy-start.18
  198.7 1.5 copy-start.34
  202.9 9.1 %copy-start.49 = (bf16[512,1216]{0,1:T(8,128)(2,1)}, bf16[512,1216]{0,1:T(8,128)(2,1)S(1)}, u32[]{:S(2)}) copy-start(bf16[512,1216]{0,1:T(8,128)(2,1)S(1)} %get-tuple-element.58) | copy-start | bytes 3735556
  204.4 6.3 %copy-start.32 = (bf16[512,896]{1,0:T(8,128)(2,1)}, bf16[512,896]{1,0:T(8,128)(2,1)S(1)}, u32[]{:S(2)}) copy-start(bf16[512,896]{1,0:T(8,128)(2,1)S(1)} %convolution_convert_fusion.4) | copy-start | bytes 2752516
  205.9 1.8 copy-start.17
  211.6 156.2 %collective-permute-start.1 = (bf16[2,2,1,64,896]{4,3,1,2,0:T(8,128)(2,1)}, bf16[2,2,1,64,896]{4,3,1,2,0:T(8,128)(2,1)}, u32[]{:S(2)}, u32[]{:S(2)}) collective-permute-start(bf16[2,2,1,64,896]{4,3,1,2,0:T(8,128)(2,1)} %dynamic-slice_bitcast_fusion), channel_id=1, source_target_pairs={{0,1},{1,0},{2,3},{3,2},{4,5},{5,4},{6,7},{7,6},{8,9},{9,8},{10,11... | collective-permute-start | bytes 1376264 | tf_op jit(solution)/shard_map/ppermute | solution.py:856
  227.9 14.6 %collective-permute-start.3 = (bf16[256,896]{1,0:T(8,128)(2,1)}, bf16[256,896]{1,0:T(8,128)(2,1)}, u32[]{:S(2)}, u32[]{:S(2)}) collective-permute-start(bf16[256,896]{1,0:T(8,128)(2,1)} %bitcast.148), channel_id=1, source_target_pairs={{0,66},{1,67},{2,64},{3,65},{4,70},{5,71},{6,68},{7,69},{8,74},{9,... | collective-permute-start | bytes 1376264 | tf_op jit(solution)/shard_map/ppermute | solution.py:778
  236.6 4.3 copy-start.42
  236.6 5.9 %copy-start.3 = (f32[512,896]{1,0:T(8,128)S(1)}, f32[512,896]{1,0:T(8,128)}, u32[]{:S(2)}) copy-start(f32[512,896]{1,0:T(8,128)} %copy-done.2) | copy-start | bytes 5505028
  236.6 5.9 %copy-start.9 = (bf16[2,2,64,896]{3,2,1,0:T(8,128)(2,1)S(1)}, bf16[2,2,64,896]{3,2,1,0:T(8,128)(2,1)}, u32[]{:S(2)}) copy-start(bf16[2,2,64,896]{3,2,1,0:T(8,128)(2,1)} %shard_map.190) | copy-start | bytes 1376260
  236.6 5.9 %copy-start.39 = (f32[896]{0:T(1024)S(1)}, f32[896]{0:T(1024)}, u32[]{:S(2)}) copy-start(f32[896]{0:T(1024)} %copy-done.38) | copy-start | bytes 10756
  244.0 4.0 copy-start.14
  247.2 0.8 copy-start.27
  302.8 38.4 %copy-start.19 = (f32[2,128,448]{2,1,0:T(8,128)S(1)}, f32[2,128,448]{2,1,0:T(8,128)}, u32[]{:S(2)}) copy-start(f32[2,128,448]{2,1,0:T(8,128)} %get-tuple-element.26) | copy-start | bytes 1376260
  343.1 6.0 %copy-start.11 = (f32[256,512]{1,0:T(8,128)S(1)}, f32[256,512]{1,0:T(8,128)}, u32[]{:S(2)}) copy-start(f32[256,512]{1,0:T(8,128)} %copy.36) | copy-start | bytes 1572868
  343.1 6.0 %copy-start.30 = (f32[256,128]{1,0:T(8,128)S(1)}, f32[256,128]{1,0:T(8,128)}, u32[]{:S(2)}) copy-start(f32[256,128]{1,0:T(8,128)} %shard_map.192) | copy-start | bytes 393220
  364.4 2.2 copy-start.10
  366.6 1.6 copy-start.33
  367.8 5.6 %copy-start.24 = (f32[256,896]{1,0:T(8,128)S(1)}, f32[256,896]{1,0:T(8,128)}, u32[]{:S(2)}) copy-start(f32[256,896]{1,0:T(8,128)} %get-tuple-element.55) | copy-start | bytes 2752516
  369.3 5.0 copy-start.15
  370.1 154.9 %collective-permute-start.2 = (bf16[2,1,64,896]{3,2,1,0:T(8,128)(2,1)}, bf16[2,1,64,896]{3,2,1,0:T(8,128)(2,1)}, u32[]{:S(2)}, u32[]{:S(2)}) collective-permute-start(bf16[2,1,64,896]{3,2,1,0:T(8,128)(2,1)} %fusion.34), channel_id=1, source_target_pairs={{0,66},{1,67},{2,64},{3,65},{4,70},{5,71},{6,68},{7,69},{8,74},{9,... | collective-permute-start | bytes 688136 | tf_op jit(solution)/shard_map/ppermute | solution.py:778
  374.2 3.0 copy-start.35
  374.2 3.0 copy-start.44
  377.0 1.9 copy-start.46
  378.9 3.5 copy-start.23
  382.4 4.5 copy-start.6
  382.4 4.5 copy-start.13
  382.4 4.5 copy-start.40
  382.4 4.5 copy-start.45
  386.8 1.0 copy-start.21
  386.8 1.2 copy-start.22
  386.8 1.3 copy-start.28
  386.9 1.4 copy-start.36
  387.8 1.2 slice-start
  387.8 1.3 copy-start.25
  498.4 3.3 copy-start.5
  500.8 8.0 %copy-start.4 = (f32[1792,896]{1,0:T(8,128)}, f32[1792,896]{1,0:T(8,128)S(1)}, u32[]{:S(2)}) copy-start(f32[1792,896]{1,0:T(8,128)S(1)} %bitcast_convert_fusion) | copy-start | bytes 19267588
  501.6 4.7 copy-start.29
  518.0 7.1 %copy-start.16 = (f32[2,2,1,64,896]{4,3,1,2,0:T(8,128)S(1)}, f32[2,2,1,64,896]{4,3,1,2,0:T(8,128)}, u32[]{:S(2)}) copy-start(f32[2,2,1,64,896]{4,3,1,2,0:T(8,128)} %copy-done.15) | copy-start | bytes 2752516
  518.0 9.0 %copy-start.1 = (bf16[1216,896]{1,0:T(8,128)(2,1)S(1)}, bf16[1216,896]{1,0:T(8,128)(2,1)}, u32[]{:S(2)}) copy-start(bf16[1216,896]{1,0:T(8,128)(2,1)} %param.20) | copy-start | bytes 6537220
Sparse Core Ops, SparseCore 0:
  9.7 26.4 all-gather.1

commit v2 on v1

--- a/solution.py
+++ b/solution.py
@@ -109,35 +109,6 @@
 def pair_of(place):
     x, y, z, core = place
     return dev(x, y, z, 1 - core), dev(3 - x, y, z, core)
-
-
-def start_kernel(w_ref, t_ref, w_out, t_out, local_sem, send, recv):
-    place = my_place()
-    x, y, z, core = place
-    sibling, cross = pair_of(place)
-    greet([sibling, cross])
-    sems = Sems(send, recv)
-    mine = (x // 2) * 2 + core
-    theirs = (1 - x // 2) * 2 + core
-    pieces = [pl.ds(48 * i, 48) for i in range(5)]
-    over = [sems.start(w_ref.at[p], w_out.at[mine, p], cross) for p in pieces]
-    toks = sems.start(t_ref, t_out.at[:, :, core], sibling)
-    own = sems.start(w_ref, w_out.at[mine], sibling)
-    keep = [
-        pltpu.make_async_copy(w_ref, w_out.at[mine], local_sem.at[0]),
-        pltpu.make_async_copy(t_ref, t_out.at[:, :, core], local_sem.at[1]),
-    ]
-    for copy in keep:
-        copy.start()
-    passed = []
-    for copy, p in zip(over, pieces):
-        copy.wait_recv()
-        passed.append(sems.start(w_out.at[theirs, p], w_out.at[theirs, p], sibling))
-    for copy in [toks, own, *passed]:
-        copy.wait_recv()
-    for copy in keep:
-        copy.wait()
-    sems.finish()
 
 
 def group_kernel(a_ref, out_ref, local_sem, send, recv):
@@ -224,23 +195,94 @@
     ]
 
 
-def kv_gather_kernel(own_ref, all_ref, local_sem, send, recv):
+def swapped(values):
+    width = values.shape[1]
+    first = lanes(values.shape) % HD < HD // 2
+    return jnp.where(first, pltpu.roll(values, width - 32, 1), pltpu.roll(values, 32, 1))
+
+
+def opening_kernel(
+    tok, cot, w_ref, small, turn, mark, t_out, w_out, s_out, q_out, all_ref, local_sem, send, recv
+):
     place = my_place()
     x, y, z, core = place
-    greet([moved(place, a, b) for a in "xyz" for b in (1, -1)])
+    sibling, cross = pair_of(place)
+    mate = dev(x + 1 - 2 * (x % 2), y, z, core)
+    greet([sibling] + [moved(place, a, b) for a in "xyz" for b in (1, -1)])
     sems = Sems(send, recv)
+    mine = (x // 2) * 2 + core
+    theirs = (1 - x // 2) * 2 + core
+    cut = ((0, 48), (48, 64))
+    got, sent = (x % 2) * 112, (1 - x % 2) * 112
+
+    def rows(start, at, size):
+        return pl.ds(pl.multiple_of(start + at, 16), size)
+
+    mark_rows = pl.ds(CHIP, KROWS - CHIP)
+    here = all_ref.at[x % 2, z, y, x // 2]
+    own = [sems.start(ref, t_out.at[i, :, core], sibling) for i, ref in enumerate((tok, cot))]
+    over = [
+        sems.start(w_ref.at[rows(sent, at, n)], w_out.at[mine, rows(sent, at, n)], cross)
+        for at, n in cut
+    ]
+    over_small = sems.start(small, s_out.at[mine], cross)
+    own += [sems.start(w_ref, w_out.at[mine], sibling), sems.start(small, s_out.at[mine], sibling)]
+    keep = [
+        pltpu.make_async_copy(tok, t_out.at[0, :, core], local_sem.at[0]),
+        pltpu.make_async_copy(cot, t_out.at[1, :, core], local_sem.at[1]),
+        pltpu.make_async_copy(w_ref, w_out.at[mine], local_sem.at[2]),
+        pltpu.make_async_copy(small, s_out.at[mine], local_sem.at[3]),
+        pltpu.make_async_copy(mark, here.at[mark_rows], local_sem.at[4]),
+    ]
+    for copy in keep:
+        copy.start()
+    shared, passed = [], []
+    for copy, (at, n) in zip(over, cut):
+        copy.wait_recv()
+        piece = w_out.at[theirs, rows(got, at, n)]
+        shared.append(sems.start(piece, piece, mate))
+        passed.append(sems.start(piece, piece, sibling))
+    over_small.wait_recv()
+    passed.append(sems.start(s_out.at[theirs], s_out.at[theirs], sibling))
+    for copy in keep:
+        copy.wait()
+    own[0].wait_recv()
+    resid = t_out[0].reshape(CHIP, D).astype(f32)
+    for copy, (at, n) in zip(shared, cut):
+        copy.wait_recv()
+        piece = w_out.at[theirs, rows(sent, at, n)]
+        passed.append(sems.start(piece, piece, sibling))
+    for copy in own[1:] + passed:
+        copy.wait_recv()
+    vectors = jnp.sum(s_out[...].astype(f32), 0)
+    inverse = lax.rsqrt(jnp.mean(resid * resid, -1, keepdims=True) + norm_eps)
+    normed = (resid * inverse * vectors[1:2, :D]).astype(bf16)
+    projected = jnp.dot(
+        normed, w_out[...].reshape(D, QKV), preferred_element_type=f32
+    ) + vectors[0:1]
+    first = core == 0
+    queries = jnp.where(first, projected[:, :QC], projected[:, QC : 2 * QC])
+    keys = projected[:, H * HD : H * HD + KVH * HD]
+    keys = jnp.where(first, keys, pltpu.roll(keys, HD, 1))
+    values = projected[:, (H + KVH) * HD :]
+    values = jnp.where(first, pltpu.roll(values, HD, 1), values)
+    cosine, sine = turn[0], turn[1]
+    keys = keys * cosine + swapped(keys) * sine
+    wide_turn = [jnp.concatenate([t] * 4, 1)[:, :QC] for t in (cosine, sine)]
+    padded = jnp.concatenate([queries, jnp.zeros((CHIP, HD), f32)], 1)
+    queries = queries * wide_turn[0] + swapped(padded)[:, :QC] * wide_turn[1]
+    q_out[...] = queries.astype(bf16).reshape(2, 128, QC)
+    here[0:CHIP, :] = jnp.where(lanes((CHIP, 128)) < HD, keys, values).astype(bf16)
+
     parts = [(0, 48, 48), (96, 48, 48), (192, 48, 32)]
-    keep = pltpu.make_async_copy(own_ref, all_ref.at[x % 2, z, y, x // 2], local_sem.at[0])
-    keep.start()
-    keep.wait()
     for stage in range(3):
         firsts = []
         for (row, n0, n1), order in zip(parts, orders):
             axis, free = order[stage], order[:stage]
             at = along(place, axis)
-            here = chips(all_ref, place, free, axis, at, pl.ds(row, n0 + n1))
+            block = chips(all_ref, place, free, axis, at, pl.ds(row, n0 + n1))
             firsts.append(
-                [sems.start(here, here, moved(place, axis, by)) for by in (1, -1)]
+                [sems.start(block, block, moved(place, axis, by)) for by in (1, -1)]
             )
         seconds = []
         for (row, n0, n1), order, (to_right, to_left) in zip(parts, orders, firsts):
@@ -257,14 +299,20 @@
     sems.finish()
 
 
-def kv_gather(chunk, cid):
+def opening(tokens, out_grad, weight, small, turn, mark, cid):
     return call(
-        kv_gather_kernel,
-        jax.ShapeDtypeStruct((2, 4, 4, 2, KROWS, 128), bf16),
-        [pltpu.SemaphoreType.DMA((1,))],
-        36,
+        opening_kernel,
+        (
+            jax.ShapeDtypeStruct((2, 2, 2, 64, D), bf16),
+            jax.ShapeDtypeStruct((4, 224, QKV), bf16),
+            jax.ShapeDtypeStruct((4, 16, QKV), bf16),
+            jax.ShapeDtypeStruct((2, 128, QC), bf16),
+            jax.ShapeDtypeStruct((2, 4, 4, 2, KROWS, 128), bf16),
+        ),
+        [pltpu.SemaphoreType.DMA((5,))],
+        50,
         cid,
-        (chunk,),
+        (tokens.reshape(2, 64, D), out_grad.reshape(2, 64, D), weight, small, turn, mark),
     )
 
 
@@ -324,10 +372,6 @@
 sum_parts = [(0, 48, 48), (96, 48, 48), (192, 32, 32)]
 
 
-def kv_lead(free):
-    return sum([(2, 2) if a == "x" else (4,) for a in free], ())
-
-
 def kv_shape(free):
     lead = ()
     if "x" in free:
@@ -341,11 +385,12 @@
     return lead
 
 
-def kv_sum_kernel(part_ref, out_ref, work, local_sem, *rest):
+def closing_kernel(part_ref, dq_ref, turn, out_ref, work, own, group, local_sem, *rest):
     lands, (send, recv) = rest[:-2], rest[-2:]
     place = my_place()
     x, y, z, core = place
-    greet([moved(place, a, b) for a in "xyz" for b in (1, -1)])
+    sibling, cross = pair_of(place)
+    greet([sibling] + [moved(place, a, b) for a in "xyz" for b in (1, -1)])
     keep = pltpu.make_async_copy(part_ref, work, local_sem.at[0])
     keep.start()
     keep.wait()
@@ -363,11 +408,47 @@
             jobs.append((axis, view, lands[at_land : at_land + 6], kv_shape(free)))
             at_land += 6
         ring_sum(place, sems, jobs)
-    out_ref[...] = work[x % 2, z, y, x // 2].astype(f32)
+    grads = work[x % 2, z, y, x // 2].astype(f32)
+    cosine, sine = turn[0], turn[1]
+    keys = grads * cosine - swapped(grads) * sine
+    dq = dq_ref[...].reshape(CHIP, QC)
+    padded = jnp.concatenate([dq, jnp.zeros((CHIP, HD), f32)], 1)
+    wide_turn = [jnp.concatenate([t] * 4, 1)[:, :QC] for t in (cosine, sine)]
+    queries = dq * wide_turn[0] - swapped(padded)[:, :QC] * wide_turn[1]
+    lane = lanes((CHIP, 128))
+    both = jnp.where(lane < HD, keys, grads)
+    own[...] = jnp.concatenate([queries, jnp.zeros((CHIP, HD), f32), both], 1).astype(bf16)
+    pieces = [pl.ds(64 * i, 64) for i in range(4)]
+    over = [sems.start(own.at[p], group.at[1, core, p], cross) for p in pieces]
+    beside = sems.start(own, group.at[0, core], sibling)
+    group[0, core] = own[...]
+    passed = []
+    for copy, p in zip(over, pieces):
+        copy.wait_recv()
+        passed.append(sems.start(group.at[1, core, p], group.at[1, core, p], sibling))
+
+    def put(chip):
+        low, high = group[chip, 0].astype(f32), group[chip, 1].astype(f32)
+        low_kv, high_kv = low[:, 512:], high[:, 512:]
+        out_ref[chip] = jnp.concatenate(
+            [
+                low[:, :QC],
+                high[:, :QC],
+                jnp.where(lane < HD, low_kv, pltpu.roll(high_kv, HD, 1)),
+                jnp.where(lane < HD, pltpu.roll(low_kv, HD, 1), high_kv),
+            ],
+            1,
+        ).astype(bf16)
+
+    beside.wait_recv()
+    put(0)
+    for copy in passed:
+        copy.wait_recv()
+    put(1)
     sems.finish()
 
 
-def kv_sum(part, cid):
+def closing(part, dq, turn, cid):
     lands = []
     for stage in range(3):
         for (row, n0, n1), order in zip(sum_parts, orders):
@@ -376,23 +457,22 @@
                 lands.append(pltpu.VMEM((*lead, n, 128), bf16))
     shape = (2, 4, 4, 2, CHIP, 128)
     return call(
-        kv_sum_kernel,
-        jax.ShapeDtypeStruct((CHIP, 128), f32),
-        [pltpu.VMEM(shape, bf16), pltpu.SemaphoreType.DMA((1,)), *lands],
-        54,
+        closing_kernel,
+        jax.ShapeDtypeStruct((2, CHIP, QKV), bf16),
+        [
+            pltpu.VMEM(shape, bf16),
+            pltpu.VMEM((CHIP, 640), bf16),
+            pltpu.VMEM((2, 2, CHIP, 640), bf16),
+            pltpu.SemaphoreType.DMA((1,)),
+            *lands,
+        ],
+        63,
         cid,
-        (part,),
-    )
-
-
-weight_parts = [
-    (0, 0, 32, 32, "zy"),
-    (0, 64, 16, 32, "yz"),
-    (1, 0, 32, 16, "zy"),
-    (1, 48, 32, 32, "yz"),
-]
-wide = (FS, D)
-chunk_rows = 112
+        (part, dq, turn),
+    )
+
+
+weight_parts = [(0, 80, 64, "zy"), (144, 64, 64, "yz")]
 
 
 def weight_view(ref, place, first, at, rows, second=None):
@@ -403,34 +483,25 @@
     return ref.at[z, at, rows] if first == "z" else ref.at[at, y, rows]
 
 
-def weight_kernel(gate, up, down, rest_ref, out_a, out_b, work_a, work_b, local_sem, *more):
+def weight_kernel(part_ref, out_ref, work, local_sem, *more):
     lands, (send, recv) = more[:-2], more[-2:]
     place = my_place()
     x, y, z, core = place
     mate = dev(x + 1 - 2 * (x % 2), y, z, core)
-    works, outs = (work_a, work_b), (out_a, out_b)
-    loads = [
-        pltpu.make_async_copy(gate, work_a.at[0:2], local_sem.at[0]),
-        pltpu.make_async_copy(up, work_a.at[2:4], local_sem.at[1]),
-        pltpu.make_async_copy(down, work_b.at[0:2], local_sem.at[2]),
-        pltpu.make_async_copy(rest_ref, work_b.at[2:4], local_sem.at[3]),
-    ]
-    for copy in loads:
-        copy.start()
+    load = pltpu.make_async_copy(part_ref, work, local_sem.at[0])
+    load.start()
     greet([moved(place, a, b) for a in "yz" for b in (1, -1)] + [mate])
-    for copy in loads:
-        copy.wait()
+    load.wait()
     sems = Sems(send, recv)
     at_land = 0
     for stage in range(2):
         jobs = []
-        for buf, row, n0, n1, order in weight_parts:
-
-            def view(at, half, buf=buf, row=row, n0=n0, n1=n1, order=order):
+        for row, n0, n1, order in weight_parts:
+
+            def view(at, half, row=row, n0=n0, n1=n1, order=order, stage=stage):
                 rows = pl.ds(row, n0) if half == 0 else pl.ds(row + n0, n1)
-                if stage == 0:
-                    return weight_view(works[buf], place, order[0], at, rows)
-                return weight_view(works[buf], place, order[0], at, rows, order[1])
+                second = order[1] if stage == 1 else None
+                return weight_view(work, place, order[0], at, rows, second)
 
             jobs.append(
                 (order[stage], view, lands[at_land : at_land + 6], (4,) if stage == 0 else ())
@@ -438,38 +509,36 @@
             at_land += 6
         ring_sum(place, sems, jobs)
     swaps = []
-    for buf, row, n0, n1, order in weight_parts:
-        mine = works[buf].at[z, y, pl.ds(row, n0 + n1)]
+    for row, n0, n1, order in weight_parts:
+        mine = work.at[z, y, pl.ds(row, n0 + n1)]
         swaps.append(sems.start(mine, lands[at_land], mate))
         at_land += 1
-    for i, ((buf, row, n0, n1, order), copy) in enumerate(zip(weight_parts, swaps)):
+    for i, ((row, n0, n1, order), copy) in enumerate(zip(weight_parts, swaps)):
         copy.wait_recv()
         rows = pl.ds(row, n0 + n1)
         land = lands[at_land - len(weight_parts) + i]
-        outs[buf][z, y, rows] = (
-            works[buf][z, y, rows].astype(f32) + land[...].astype(f32)
+        out_ref[z, y, rows] = (
+            work[z, y, rows].astype(f32) + land[...].astype(f32)
         ).astype(bf16)
     for stage in (1, 0):
         firsts = []
-        for buf, row, n0, n1, order in weight_parts:
+        for row, n0, n1, order in weight_parts:
             axis = order[stage]
             rows = pl.ds(row, n0 + n1)
             second = order[1] if stage == 1 else None
-            here = weight_view(outs[buf], place, order[0], along(place, axis), rows, second)
+            here = weight_view(out_ref, place, order[0], along(place, axis), rows, second)
             firsts.append([sems.start(here, here, moved(place, axis, by)) for by in (1, -1)])
         seconds = []
-        for (buf, row, n0, n1, order), (to_right, to_left) in zip(weight_parts, firsts):
+        for (row, n0, n1, order), (to_right, to_left) in zip(weight_parts, firsts):
             axis = order[stage]
             at = along(place, axis)
             second = order[1] if stage == 1 else None
             to_right.wait_recv()
-            left = weight_view(
-                outs[buf], place, order[0], (at + 3) % 4, pl.ds(row, n0), second
-            )
+            left = weight_view(out_ref, place, order[0], (at + 3) % 4, pl.ds(row, n0), second)
             seconds.append(sems.start(left, left, moved(place, axis, 1)))
             to_left.wait_recv()
             right = weight_view(
-                outs[buf], place, order[0], (at + 1) % 4, pl.ds(row + n0, n1), second
+                out_ref, place, order[0], (at + 1) % 4, pl.ds(row + n0, n1), second
             )
             seconds.append(sems.start(right, right, moved(place, axis, -1)))
         for copy in seconds:
@@ -477,31 +546,24 @@
     sems.finish()
 
 
-def weight_sum(gate, up, down, rest, cid):
+def weight_sum(part, cid):
     lands = []
     for stage in range(2):
-        for buf, row, n0, n1, order in weight_parts:
+        for row, n0, n1, order in weight_parts:
             lead = (4,) if stage == 0 else ()
             for n in (n1, n0, n0, n1, n1, n0):
-                lands.append(pltpu.VMEM((*lead, n, wide[buf]), bf16))
-    for buf, row, n0, n1, order in weight_parts:
-        lands.append(pltpu.VMEM((n0 + n1, wide[buf]), bf16))
-    big = [(4, 4, chunk_rows, w) for w in wide]
-    half = (2, 4, chunk_rows)
-    args = (
-        gate.reshape(*half, FS),
-        up.reshape(*half, FS),
-        down.reshape(*half, D),
-        rest.reshape(*half, D),
-    )
+                lands.append(pltpu.VMEM((*lead, n, D), bf16))
+    for row, n0, n1, order in weight_parts:
+        lands.append(pltpu.VMEM((n0 + n1, D), bf16))
+    big = (4, 4, 272, D)
     return call(
         weight_kernel,
-        tuple(jax.ShapeDtypeStruct(s, bf16) for s in big),
-        [*[pltpu.VMEM(s, bf16) for s in big], pltpu.SemaphoreType.DMA((4,)), *lands],
-        4 * 6 * 2 + 4 + 4 * 4 * 2,
+        jax.ShapeDtypeStruct(big, bf16),
+        [pltpu.VMEM(big, bf16), pltpu.SemaphoreType.DMA((1,)), *lands],
+        len(weight_parts) * (6 * 2 + 1 + 4 * 2),
         cid,
-        args,
-        [pl.BlockSpec(memory_space=pl.ANY)] * 4,
+        (part.reshape(big),),
+        [pl.BlockSpec(memory_space=pl.ANY)],
     )
 
 
@@ -726,19 +788,11 @@
 
 
 def rotation(positions):
-    frequency = rope_base ** (-(2.0 * jnp.arange(HD // 2, dtype=f32)) / HD)
+    lane = jnp.arange(128)
+    frequency = rope_base ** (-(2.0 * (lane % 32).astype(f32)) / HD)
     angles = positions.astype(f32)[:, None] * frequency[None, :]
-    cosine, sine = jnp.cos(angles), jnp.sin(angles)
-    return (
-        jnp.tile(jnp.concatenate([cosine, cosine], 1), (1, G + 1)),
-        jnp.tile(jnp.concatenate([-sine, sine], 1), (1, G + 1)),
-    )
-
-
-def swapped(values):
-    heads = values.shape[1] // HD
-    parts = values.reshape(-1, heads, 2, HD // 2)
-    return jnp.flip(parts, 2).reshape(values.shape)
+    sign = jnp.where(lane % HD < HD // 2, -1.0, 1.0)
+    return jnp.stack([jnp.cos(angles), jnp.sin(angles) * sign])
 
 
 def dot(a, b):
@@ -777,52 +831,26 @@
     def crossed(array):
         return lax.ppermute(array, ("ctx", "wsh"), swap)
 
-    small = jnp.stack(
-        [jnp.pad(v, (0, QKV - v.shape[0])) for v in (qkv_bias, norm1_gain, norm2_gain)]
-    )
-    w_in = jnp.concatenate([qkv_weight, jnp.pad(small, ((0, 13), (0, 0)))], 0)
-    t_in = jnp.stack([tokens, out_grad]).reshape(2, 2, 64, D)
-    w_all, t_all = call(
-        start_kernel,
-        (
-            jax.ShapeDtypeStruct((4, 240, QKV), bf16),
-            jax.ShapeDtypeStruct((2, 2, 2, 64, D), bf16),
-        ),
-        [pltpu.SemaphoreType.DMA((2,))],
-        12,
-        0,
-        (w_in, t_in),
-    )
+    def spread(vector, width):
+        column = jnp.arange(QKV)
+        values = jnp.pad(jnp.tile(vector, 4), (0, QKV - 4 * width))
+        return jnp.where(column // width == wsh, values, 0)
+
+    small = jnp.stack([spread(qkv_bias, 288), spread(norm1_gain, 224), spread(norm2_gain, 224)])
+    small = jnp.pad(small, ((0, 13), (0, 0))).astype(bf16)
+    offset = jnp.arange(128, dtype=jnp.int32) + xhi * 128
+    turn = rotation(jnp.concatenate([my_block * 256 + offset, (63 - my_block) * 256 + offset]))
+    mark = jnp.broadcast_to(my_block.astype(bf16), (KROWS - CHIP, 128))
+    t_all, w_all, s_all, queries, kv_all = opening(
+        tokens, out_grad, qkv_weight, small, turn, mark, 0
+    )
+    out_weight, kv_all = lax.optimization_barrier((out_weight, kv_all))
     out_full = lax.all_gather(out_weight, "wsh", axis=0, tiled=True)
-    qkv_full = w_all[:, :224].reshape(D, QKV)
-    bias_full = w_all[:, 224, :288].reshape(QKV).astype(f32)
-    gain_one = w_all[:, 225, :224].reshape(D).astype(f32)
-    gain_two = w_all[:, 226, :224].reshape(D).astype(f32)
+    qkv_full = w_all.reshape(D, QKV)
+    vectors = jnp.sum(s_all[:, 1:3, :D].astype(f32), 0)
+    gain_one, gain_two = vectors[0], vectors[1]
     t_chip = t_all.reshape(2, CHIP, D)
-
-    def my_columns(array):
-        return jnp.concatenate(
-            [
-                cut(array, core * QC, QC, array.ndim - 1),
-                cut(array, H * HD + core * HD, HD, array.ndim - 1),
-                cut(array, (H + KVH) * HD + core * HD, HD, array.ndim - 1),
-            ],
-            -1,
-        )
-
-    resid = t_chip[0].astype(f32)
-    normed_one = (resid * rms_inverse(resid) * gain_one).astype(bf16)
-    projected = dot(normed_one, my_columns(qkv_full)) + my_columns(bias_full)
-    offset = jnp.arange(128, dtype=jnp.int32) + xhi * 128
-    cosine, sine = rotation(
-        jnp.concatenate([my_block * 256 + offset, (63 - my_block) * 256 + offset])
-    )
-    turning = projected[:, : QC + HD]
-    turned = (turning * cosine + swapped(turning) * sine).astype(bf16)
-    queries = turned[:, :QC].reshape(2, 128, QC)
-    chunk = jnp.concatenate([turned[:, QC:], projected[:, QC + HD :].astype(bf16)], 1)
-    mark = jnp.broadcast_to(my_block.astype(bf16), (KROWS - CHIP, 128))
-    kv_all = kv_gather(jnp.concatenate([chunk, mark], 0), 1).reshape(32, 2, KROWS, 128)
+    kv_all = kv_all.reshape(32, 2, KROWS, 128)
     blocks = kv_all[:, 0, CHIP, 0].astype(jnp.int32)
     scal = jnp.concatenate(
         [(blocks > my_block).astype(jnp.int32), jnp.stack([ctx, xhi]).astype(jnp.int32)]
@@ -858,8 +886,8 @@
     mlp_far = crossed(mlp_sum[1].astype(bf16))
     mlp_own = (mlp_sum[0] + mlp_far.astype(f32)).reshape(TOK, D)
     output = (own_rows(stream[:CHIP]) + mlp_own).astype(bf16)
-    gate_wgrad = jnp.einsum("td,tf->df", normed_two, gate_grad, preferred_element_type=f32)
-    up_wgrad = jnp.einsum("td,tf->df", normed_two, up_grad, preferred_element_type=f32)
+    gate_wgrad = jnp.einsum("tf,td->fd", gate_grad, normed_two, preferred_element_type=f32)
+    up_wgrad = jnp.einsum("tf,td->fd", up_grad, normed_two, preferred_element_type=f32)
     down_wgrad = jnp.einsum("tf,td->fd", hidden, cot, preferred_element_type=f32)
 
     def stream_pull(part, grad):
@@ -876,22 +904,7 @@
     dq, dkv_part = attention_backward(
         scal, qe, attended_f, att_grad.reshape(2, 128, QC), kv_all
     )
-    dkv = kv_sum(dkv_part.reshape(2, 4, 4, 2, CHIP, 128), 4)
-    turning = jnp.concatenate([dq.reshape(CHIP, QC), dkv[:, :HD]], 1)
-    turned = turning * cosine - swapped(turning) * sine
-    pg_mine = jnp.concatenate([turned, dkv[:, HD:]], 1).astype(bf16)
-    pg = group_gather(pg_mine, 5)
-    pg = jnp.concatenate(
-        [
-            pg[:, 0, :, :QC],
-            pg[:, 1, :, :QC],
-            pg[:, 0, :, QC : QC + HD],
-            pg[:, 1, :, QC : QC + HD],
-            pg[:, 0, :, QC + HD :],
-            pg[:, 1, :, QC + HD :],
-        ],
-        -1,
-    ).reshape(2 * CHIP, QKV)
+    pg = closing(dkv_part.reshape(2, 4, 4, 2, CHIP, 128), dq, turn, 4).reshape(2 * CHIP, QKV)
 
     bias_grad = cut(jnp.sum(pg.astype(f32), 0), wsh * 288, 288, 0)
     inv_one = rms_inverse(resid_both)
@@ -917,32 +930,26 @@
     vectors = jnp.stack(
         [jnp.pad(v, (0, D - v.shape[0])) for v in (bias_grad, gain_one_grad, gain_two_grad)]
     )
-    down_low = down_wgrad.astype(bf16)
-    rest = jnp.concatenate(
+    part = jnp.concatenate(
         [
-            down_low[896:],
-            out_wgrad.astype(bf16),
+            *[w.astype(bf16) for w in (gate_wgrad, up_wgrad, down_wgrad, out_wgrad)],
             qkv_wgrad.astype(bf16).reshape(288, D),
-            jnp.pad(vectors, ((0, 61), (0, 0))).astype(bf16),
+            jnp.pad(vectors, ((0, 189), (0, 0))).astype(bf16),
         ],
         0,
     )
-    sum_a, sum_b = weight_sum(
-        gate_wgrad.astype(bf16), up_wgrad.astype(bf16), down_low[:896], rest, 6
-    )
-    sum_a = sum_a.reshape(2 * D, FS).astype(f32)
-    sum_b = sum_b.reshape(2 * D, D).astype(f32)
+    total = weight_sum(part, 6).reshape(16 * 272, D).astype(f32)
     return (
         output,
         token_grad,
-        sum_b[1729, :224],
-        sum_b[1440:1728].reshape(224, QKV),
-        sum_b[1728, :288],
-        sum_b[1216:1440],
-        sum_b[1730, :224],
-        sum_a[:D],
-        sum_a[D:],
-        sum_b[:1216],
+        total[4161, :224],
+        total[3872:4160].reshape(224, QKV),
+        total[4160, :288],
+        total[3648:3872],
+        total[4162, :224],
+        total[:1216].T,
+        total[1216:2432].T,
+        total[2432:3648],
     )
 
 

time: 544 us -> 470 us (0.86)
  local copies, waits for them, and re-layouts: 87.8 us -> 32.8 us
  Pallas kernels: 349 us -> 336 us
  other arithmetic: 41.2 us -> 33.6 us
    unnamed x104 -> x79, local copies, waits for them, and re-layouts: 19 us -> 4.98 us
    pallas_call x7 -> x5, Pallas kernels: 252 us -> 239 us  [call(): pl.pallas_call(kernel, out_shape=out_shape, in_specs=specs if specs is no...]
    convert_element_type x5 -> x0, local copies, waits for them, and re-layouts: 8.31 us -> none  [the longest x1 4.29 us: body(): up_wgrad.astype(bf16)]
    concatenate x3 -> x0, local copies, waits for them, and re-layouts: 8.12 us -> none  [the longest x2 6.02 us: body(): jnp.concatenate([pg[:, 0, :, :QC], pg[:, 1, :, :QC], pg[:, 0, :, QC:QC +...]
    slice x17 -> x7, local copies, waits for them, and re-layouts: 21.9 us -> 15.3 us  [the longest x1 9.93 us: body(): total[2432:3648]]
    concatenate x8 -> x1, other arithmetic: 7.25 us -> 0.76 us  [body(): jnp.concatenate([*[w.astype(bf16) for w in (gate_wgrad, up_wgrad, down_wg...]
  transfers between devices with their start and end apart: 5 -> 5, of which waited for: 1 -> 1; matrix products, arithmetic and copies ran while one was open for 24% -> 15% of each run, Pallas kernels for 65% -> 61%
where the time goes in v2:
time: 470 us; the launch traced here: 461 us
  Pallas kernels  336 us (71%)
  other arithmetic  33.6 us (7%)
  local copies, waits for them, and re-layouts  32.8 us (7%)
  matrix products  30.6 us (7%)
  between operations  17.9 us (4%)
  waiting for transfers between devices  6.63 us (1%)
    pallas_call x5, Pallas kernels, call(): pl.pallas_call(kernel, out_shape=out_shape, in_specs=specs if specs is no...  239 us
    pallas_call x2, Pallas kernels, local_call(): pl.pallas_call(kernel, out_shape=out_shape, in_specs=[pl.BlockSpec(memory...  97.1 us
    slice x1, local copies, waits for them, and re-layouts, body(): total[2432:3648]  9.93 us
    convert_element_type x1, other arithmetic, body(): total = weight_sum(part, 6).reshape(16 * 272, D).astype(f32)  9.68 us
  transfers between devices with their start and end apart: 5, of which 1 were waited for; matrix products, arithmetic and copies ran while one was open for 15% of the time, Pallas kernels for 61%

profile of v2, /device:TPU:0, one launch (start us, length us, event | category | flops | bytes accessed | tf_op | source)
XLA Modules:
  0.0 461.4 jit_solution(1409680438596359235)
XLA Ops:
  10.0 0.7 tile.31
  10.8 0.7 tile.14
  11.5 0.7 tile.12
  12.4 0.5 multiply_cosine_fusion
  13.0 0.7 pad_maximum_fusion.1.turn
  13.7 0.6 fusion.43.small
  14.3 0.6 broadcast_in_dim.33.mark
  14.9 56.2 %shard_map.186 = (bf16[2,2,2,64,896]{4,3,2,1,0:T(8,128)(2,1)}, bf16[4,224,1152]{2,1,0:T(8,128)(2,1)}, bf16[4,16,1152]{2,1,0:T(8,128)(2,1)}, bf16[2,128,448]{2,1,0:T(8,128)(2,1)}, bf16[2,4,4,2,272,128]{5,4,3,2,1,0:T(8,128)(2,1)}) custom-call(bf16[2,64,896]{2,1,0:T(8,128)(2,1)} %bitcast.109, bf16[2,64,896]{2,1,0:T(8,128)(2,1)} %bitcast.126, ...), custom_call_target="tpu_custom_call" | custom-call | tf_op jit(solution)/shard_map/pallas_call | solution.py:93
  71.2 1.5 fusion.44
  72.8 0.6 pad_add_fusion.scal
  73.4 43.4 %shard_map.187 = (f32[2,128,448]{2,1,0:T(8,128)}, bf16[2,896,128]{2,1,0:T(8,128)(2,1)}) custom-call(s32[34]{0:T(128)} %pad_add_fusion.scal, bf16[2,128,448]{2,1,0:T(8,128)(2,1)} %get-tuple-element.27.q_ref, bf16[32,2,272,128]{3,2,1,0:T(8,128)(2,1)} %bitcast.137), custom_call_target="tpu_custom_call" | custom-call | flops 20000000000 | bytes 10000000 | tf_op jit(solution)/shard_map/pallas_call | solution.py:671
  116.8 0.6 convert_element_type.205
  117.3 1.9 convert_element_type.176
  119.2 13.2 %shard_map.188 = bf16[2,2,256,448]{3,2,1,0:T(8,128)(2,1)} custom-call(bf16[256,448]{1,0:T(8,128)(2,1)} %bitcast.119), custom_call_target="tpu_custom_call" | custom-call | tf_op jit(solution)/shard_map/pallas_call | solution.py:93
  132.4 0.9 convert_reduce_fusion.1
  133.3 0.6 slice_reduce_fusion
  134.5 2.2 fusion.62
  136.8 1.3 multiply_reduce_fusion
  138.1 0.6 copy.34
  138.7 2.9 pad_maximum_fusion
  141.5 2.1 fusion.13
  143.7 2.0 multiply_reduce_fusion.1
  146.0 2.0 copy-done.34
  148.0 1.5 fusion.65
  149.9 1.5 fusion.64
  151.5 2.6 multiply_convert_fusion
  154.1 1.6 fusion.66
  155.7 2.8 fusion
  158.5 1.6 convolution_convert_fusion.4
  160.1 0.9 dynamic-slice_bitcast_fusion
  161.4 2.5 add_convert_fusion
  163.9 13.5 %shard_map.189 = bf16[2,2,64,896]{3,2,1,0:T(8,128)(2,1)} custom-call(bf16[2,2,2,64,896]{4,3,2,1,0:T(8,128)(2,1)} %bitcast.120), custom_call_target="tpu_custom_call" | custom-call | tf_op jit(solution)/shard_map/pallas_call | solution.py:93
  177.4 0.9 collective-permute-start.3
  178.3 4.1 fusion.1
  182.4 2.9 fusion.2
  185.3 6.6 %collective-permute-done.3 = bf16[256,896]{1,0:T(8,128)(2,1)S(1)} collective-permute-done((bf16[256,896]{1,0:T(8,128)(2,1)}, bf16[256,896]{1,0:T(8,128)(2,1)S(1)}, u32[]{:S(2)}, u32[]{:S(2)}) %collective-permute-start.3) | collective-permute-done | bytes 458784 | tf_op jit(solution)/shard_map/ppermute | solution.py:832
  192.4 3.0 fusion.59
  195.8 0.8 copy.29
  196.7 53.7 %shard_map.190 = (f32[2,128,448]{2,1,0:T(8,128)}, bf16[32,2,256,128]{3,2,1,0:T(8,128)(2,1)}) custom-call(s32[34]{0:T(128)} %pad_add_fusion.scal, bf16[2,896,128]{2,1,0:T(8,128)(2,1)} %get-tuple-element.32.qe_ref, f32[2,128,448]{2,1,0:T(8,128)} %get-tuple-element.29.o_ref, bf16[2,128,448]{2,1,0:T(8,128)(2,1)} %bitcast.125, bf16[32,2,272,128]{3,2,1,0:T(8,128)(2,1)} %bitcast.138), custom_call_target="tpu_custom_call" | custom-call | flops 49999998976 | bytes 10000000 | tf_op jit(solution)/shard_map/pallas_call | solution.py:671
  250.3 45.1 %shard_map.191 = bf16[2,256,1152]{2,1,0:T(8,128)(2,1)} custom-call(bf16[2,4,4,2,256,128]{5,4,3,2,1,0:T(8,128)(2,1)} %bitcast.108, f32[2,128,448]{2,1,0:T(8,128)} %get-tuple-element.34.dq_ref, f32[2,256,128]{2,1,0:T(8,128)} %pad_maximum_fusion.1.turn), custom_call_target="tpu_custom_call" | custom-call | tf_op jit(solution)/shard_map/pallas_call | solution.py:93
  295.5 2.0 slice.114
  297.5 1.6 convert_reduce_fusion
  299.1 1.3 convert_add_fusion.2
  300.4 0.8 fusion.37
  301.2 2.5 collective-permute-start.2
  303.8 1.6 multiply_reduce_fusion.4
  305.4 0.8 constant_dynamic-slice_fusion.1
  306.2 0.6 fusion.5
  306.8 0.8 convolution_convert_fusion.3
  307.6 0.6 reshape.405
  308.2 1.0 constant_dynamic-slice_fusion
  309.3 2.4 fusion.21
  311.8 1.4 fusion.4
  313.2 0.8 constant_dynamic-update-slice_fusion
  314.1 0.8 fusion.31
  314.8 110.7 %shard_map.192 = bf16[4,4,272,896]{3,2,1,0:T(8,128)(2,1)} custom-call(bf16[4,4,272,896]{3,2,1,0:T(8,128)(2,1)} %bitcast.101), custom_call_target="tpu_custom_call" | custom-call | tf_op jit(solution)/shard_map/pallas_call | solution.py:93
  425.6 9.7 %bitcast_convert_fusion = f32[4352,896]{1,0:T(8,128)} fusion(bf16[4,4,272,896]{3,2,1,0:T(8,128)(2,1)} %shard_map.192), kind=kLoop, calls=%fused_computation | loop fusion | flops 3899392 | bytes 23396352 | tf_op jit(solution)/shard_map/convert_element_type | solution.py:941
  435.3 9.9 %fusion.60 = (f32[1216,896]{1,0:T(8,128)}, f32[896,1216]{0,1:T(8,128)}, f32[896,1216]{0,1:T(8,128)}) fusion(f32[4352,896]{1,0:T(8,128)} %bitcast_convert_fusion), kind=kLoop, calls=%fused_computation.143 | loop fusion | bytes 26148864 | tf_op jit(solution)/shard_map/slice | solution.py:952
  445.2 1.0 fusion.24
  446.2 1.4 slice_reduce_fusion.2
  447.6 2.1 slice.142
  449.6 1.2 reshape.407
  450.8 1.3 fusion.61
  452.2 1.9 fusion.28
  (113 shorter events, 3.4 us)
Async XLA Ops:
  7.2 144.3 %copy-start = (bf16[1216,896]{1,0:T(8,128)(2,1)S(1)}, bf16[1216,896]{1,0:T(8,128)(2,1)}, u32[]{:S(2)}) copy-start(bf16[1216,896]{1,0:T(8,128)(2,1)} %param.20) | copy-start | bytes 6537220
  7.2 134.3 %all-gather.2.cloned.1.call-start = ((), (), s32[]{:S(2)}) async-start(), calls=%async_computation | async-start | bytes 2007040 | tf_op jit(solution)/shard_map/all_gather | solution.py:848
  71.2 65.6 %collective-permute-start = (bf16[2,256,896]{2,1,0:T(8,128)(2,1)}, bf16[2,256,896]{2,1,0:T(8,128)(2,1)}, u32[]{:S(2)}, u32[]{:S(2)}) collective-permute-start(bf16[2,256,896]{2,1,0:T(8,128)(2,1)} %bitcast.104), channel_id=1, source_target_pairs={{0,66},{1,67},{2,64},{3,65},{4,70},{5,71},{6,68},{7,69},{8,74},{9,... | collective-permute-start | bytes 2752520 | tf_op jit(solution)/shard_map/ppermute | solution.py:832
  73.4 43.4 %copy-start.33 = (bf16[224]{0:T(256)(128)(2,1)S(1)}, bf16[224]{0:T(256)(128)(2,1)}, u32[]{:S(2)}) copy-start(bf16[224]{0:T(256)(128)(2,1)} %param.13) | copy-start | bytes 1348
  116.8 17.1 %copy-start.8 = (bf16[128,896]{1,0:T(8,128)(2,1)S(1)}, bf16[128,896]{1,0:T(8,128)(2,1)}, u32[]{:S(2)}) copy-start(bf16[128,896]{1,0:T(8,128)(2,1)} %param.11) | copy-start | bytes 688132
  117.3 19.5 %copy-start.7 = (bf16[2,2,2,64,896]{4,3,2,1,0:T(8,128)(2,1)S(1)}, bf16[2,2,2,64,896]{4,3,2,1,0:T(8,128)(2,1)}, u32[]{:S(2)}) copy-start(bf16[2,2,2,64,896]{4,3,2,1,0:T(8,128)(2,1)} %get-tuple-element.23) | copy-start | bytes 2752516
  141.5 2.2 copy-start.4
  141.5 2.2 copy-start.12
  145.7 46.6 %copy-start.2 = (f32[512,896]{1,0:T(8,128)}, f32[512,896]{1,0:T(8,128)S(1)}, u32[]{:S(2)}) copy-start(f32[512,896]{1,0:T(8,128)S(1)} %get-tuple-element.61) | copy-start | bytes 5505028
  145.7 2.3 copy-start.34
  145.7 36.7 %copy-start.27 = (f32[512]{0:T(512)}, f32[512]{0:T(512)S(1)}, u32[]{:S(2)}) copy-start(f32[512]{0:T(512)S(1)} %add_rsqrt_fusion) | copy-start | bytes 6148
  148.0 7.7 %copy-start.19 = (bf16[512,896]{1,0:T(8,128)(2,1)}, bf16[512,896]{1,0:T(8,128)(2,1)S(1)}, u32[]{:S(2)}) copy-start(bf16[512,896]{1,0:T(8,128)(2,1)S(1)} %multiply_convert_fusion.3) | copy-start | bytes 2752516
  148.0 1.9 copy-start.11
  149.9 1.5 copy-start.23
  154.1 4.4 copy-start.35
  154.1 7.3 %copy-start.37 = (bf16[512,1216]{0,1:T(8,128)(2,1)}, bf16[512,1216]{0,1:T(8,128)(2,1)S(1)}, u32[]{:S(2)}) copy-start(bf16[512,1216]{0,1:T(8,128)(2,1)S(1)} %get-tuple-element.47) | copy-start | bytes 3735556
  160.1 1.3 copy-start.21
  161.0 138.1 %collective-permute-start.1 = (bf16[2,2,1,64,896]{4,3,1,2,0:T(8,128)(2,1)}, bf16[2,2,1,64,896]{4,3,1,2,0:T(8,128)(2,1)}, u32[]{:S(2)}, u32[]{:S(2)}) collective-permute-start(bf16[2,2,1,64,896]{4,3,1,2,0:T(8,128)(2,1)} %dynamic-slice_bitcast_fusion), channel_id=1, source_target_pairs={{0,1},{1,0},{2,3},{3,2},{4,5},{5,4},{6,7},{7,6},{8,9},{9,8},{10,11... | collective-permute-start | bytes 1376264 | tf_op jit(solution)/shard_map/ppermute | solution.py:884
  161.4 16.9 %copy-start.20 = (bf16[512,896]{1,0:T(8,128)(2,1)S(1)}, bf16[512,896]{1,0:T(8,128)(2,1)}, u32[]{:S(2)}) copy-start(bf16[512,896]{1,0:T(8,128)(2,1)} %copy-done.19) | copy-start | bytes 2752516
  177.4 5.0 %copy-start.24 = (bf16[1,2,256,896]{3,2,0,1:T(8,128)(2,1)S(1)}, bf16[1,2,256,896]{3,2,0,1:T(8,128)(2,1)}, u32[]{:S(2)}) copy-start(bf16[1,2,256,896]{3,2,0,1:T(8,128)(2,1)} %get-tuple-element.52) | copy-start | bytes 2752516
  177.4 5.0 %copy-start.36 = (bf16[512,1216]{0,1:T(8,128)(2,1)S(1)}, bf16[512,1216]{0,1:T(8,128)(2,1)}, u32[]{:S(2)}) copy-start(bf16[512,1216]{0,1:T(8,128)(2,1)} %copy-done.35) | copy-start | bytes 3735556
  177.4 14.5 %collective-permute-start.3 = (bf16[256,896]{1,0:T(8,128)(2,1)}, bf16[256,896]{1,0:T(8,128)(2,1)S(1)}, u32[]{:S(2)}, u32[]{:S(2)}) collective-permute-start(bf16[256,896]{1,0:T(8,128)(2,1)} %bitcast.102), channel_id=1, source_target_pairs={{0,66},{1,67},{2,64},{3,65},{4,70},{5,71},{6,68},{7,69},{8,74},{9,... | collective-permute-start | bytes 1376264 | tf_op jit(solution)/shard_map/ppermute | solution.py:832
  182.4 9.5 %copy-start.6 = (bf16[2,2,64,896]{3,2,1,0:T(8,128)(2,1)S(1)}, bf16[2,2,64,896]{3,2,1,0:T(8,128)(2,1)}, u32[]{:S(2)}) copy-start(bf16[2,2,64,896]{3,2,1,0:T(8,128)(2,1)} %shard_map.189) | copy-start | bytes 1376260
  192.3 3.1 copy-start.9
  195.4 54.9 %copy-start.16 = (bf16[256,896]{1,0:T(8,128)(2,1)}, bf16[256,896]{1,0:T(8,128)(2,1)S(1)}, u32[]{:S(2)}) copy-start(bf16[256,896]{1,0:T(8,128)(2,1)S(1)} %get-tuple-element.40) | copy-start | bytes 1376260
  295.5 3.6 copy-start.22
  295.5 8.3 %copy-start.28 = (f32[512]{0:T(512)S(1)}, f32[512]{0:T(512)}, u32[]{:S(2)}) copy-start(f32[512]{0:T(512)} %copy-done.27) | copy-start | bytes 6148
  297.5 7.9 %copy-start.15 = (f32[256,896]{1,0:T(8,128)S(1)}, f32[256,896]{1,0:T(8,128)}, u32[]{:S(2)}) copy-start(f32[256,896]{1,0:T(8,128)} %get-tuple-element.41) | copy-start | bytes 2752516
  299.1 7.1 %copy-start.3 = (bf16[2,256,1152]{2,1,0:T(8,128)(2,1)S(1)}, bf16[2,256,1152]{2,1,0:T(8,128)(2,1)}, u32[]{:S(2)}) copy-start(bf16[2,256,1152]{2,1,0:T(8,128)(2,1)} %shard_map.191) | copy-start | bytes 3538948
  299.1 7.1 %copy-start.5 = (f32[1,2,256,896]{3,2,0,1:T(8,128)S(1)}, f32[1,2,256,896]{3,2,0,1:T(8,128)}, u32[]{:S(2)}) copy-start(f32[1,2,256,896]{3,2,0,1:T(8,128)} %get-tuple-element.53) | copy-start | bytes 5505028
  299.1 7.1 %copy-start.25 = (bf16[224,1152]{1,0:T(8,128)(2,1)S(1)}, bf16[224,1152]{1,0:T(8,128)(2,1)}, u32[]{:S(2)}) copy-start(bf16[224,1152]{1,0:T(8,128)(2,1)} %w_ref.1) | copy-start | bytes 1548292
  299.1 7.1 %copy-start.30 = (f32[1,2,2,128]{3,1,2,0:T(2,128)S(1)}, f32[1,2,2,128]{3,1,2,0:T(2,128)}, u32[]{:S(2)}) copy-start(f32[1,2,2,128]{3,1,2,0:T(2,128)} %copy.34) | copy-start | bytes 6148
  300.4 6.4 %copy-start.10 = (f32[2,2,1,64,896]{4,3,1,2,0:T(8,128)}, f32[2,2,1,64,896]{4,3,1,2,0:T(8,128)S(1)}, u32[]{:S(2)}) copy-start(f32[2,2,1,64,896]{4,3,1,2,0:T(8,128)S(1)} %convert_add_fusion.2) | copy-start | bytes 2752516
  301.2 5.5 %copy-start.32 = (f32[224]{0:T(256)S(1)}, f32[224]{0:T(256)}, u32[]{:S(2)}) copy-start(f32[224]{0:T(256)} %convert_element_type.205) | copy-start | bytes 2692
  301.2 151.0 %collective-permute-start.2 = (bf16[2,1,64,896]{3,2,1,0:T(8,128)(2,1)}, bf16[2,1,64,896]{3,2,1,0:T(8,128)(2,1)S(1)}, u32[]{:S(2)}, u32[]{:S(2)}) collective-permute-start(bf16[2,1,64,896]{3,2,1,0:T(8,128)(2,1)} %fusion.37), channel_id=1, source_target_pairs={{0,66},{1,67},{2,64},{3,65},{4,70},{5,71},{6,68},{7,69},{8,74},{9,... | collective-permute-start | bytes 688136 | tf_op jit(solution)/shard_map/ppermute | solution.py:832
  306.8 2.5 copy-start.29
  306.8 2.5 copy-start.31
  307.6 4.2 copy-start.13
  307.6 4.2 copy-start.14
  307.6 4.2 copy-start.17
  308.2 3.6 copy-start.26
  435.3 9.9 %copy-start.18 = (f32[2,1,64,896]{3,2,1,0:T(8,128)S(1)}, f32[2,1,64,896]{3,2,1,0:T(8,128)}, u32[]{:S(2)}) copy-start(f32[2,1,64,896]{3,2,1,0:T(8,128)} %constant_dynamic-slice_fusion.1) | copy-start | bytes 1376260
  446.2 3.5 slice-start
  449.6 4.4 copy-start.1
Sparse Core Ops, SparseCore 0:
  71.3 21.0 all-gather.1

commit v3 on v2

--- a/solution.py
+++ b/solution.py
@@ -76,10 +76,14 @@
             device_id_type=MESH,
         )
 
+    def ready(self, src, dst, device):
+        copy = self.copy(src, dst, device)
+        self.started.append(copy)
+        return copy
+
     def start(self, src, dst, device):
-        copy = self.copy(src, dst, device)
+        copy = self.ready(src, dst, device)
         copy.start()
-        self.started.append(copy)
         return copy
 
     def finish(self):
@@ -276,26 +280,16 @@
 
     parts = [(0, 48, 48), (96, 48, 48), (192, 48, 32)]
     for stage in range(3):
-        firsts = []
+        jobs = []
         for (row, n0, n1), order in zip(parts, orders):
             axis, free = order[stage], order[:stage]
-            at = along(place, axis)
-            block = chips(all_ref, place, free, axis, at, pl.ds(row, n0 + n1))
-            firsts.append(
-                [sems.start(block, block, moved(place, axis, by)) for by in (1, -1)]
-            )
-        seconds = []
-        for (row, n0, n1), order, (to_right, to_left) in zip(parts, orders, firsts):
-            axis, free = order[stage], order[:stage]
-            at = along(place, axis)
-            to_right.wait_recv()
-            left = chips(all_ref, place, free, axis, (at + 3) % 4, pl.ds(row, n0))
-            seconds.append(sems.start(left, left, moved(place, axis, 1)))
-            to_left.wait_recv()
-            right = chips(all_ref, place, free, axis, (at + 1) % 4, pl.ds(row + n0, n1))
-            seconds.append(sems.start(right, right, moved(place, axis, -1)))
-        for copy in seconds:
-            copy.wait_recv()
+
+            def view(at, half, row=row, n0=n0, n1=n1, axis=axis, free=free):
+                rows = {None: pl.ds(row, n0 + n1), 0: pl.ds(row, n0), 1: pl.ds(row + n0, n1)}
+                return chips(all_ref, place, free, axis, at, rows[half])
+
+            jobs.append((axis, view))
+        phases(ring_spread(place, sems, jobs))
     sems.finish()
 
 
@@ -336,37 +330,84 @@
 
 
 def ring_sum(place, sems, jobs):
-    state = []
+    plans = []
     for axis, view, land, shape in jobs:
         at = along(place, axis)
+        after, far, before = (at + 1) % 4, (at + 2) % 4, (at + 3) % 4
         right, left = moved(place, axis, 1), moved(place, axis, -1)
-        far = (at + 2) % 4
-        state.append(
+        early = [
+            sems.ready(view(far, 1), land[0], right),
+            sems.ready(view(far, 0), land[1], left),
+            sems.ready(view(after, 0), land[2], right),
+            sems.ready(view(before, 1), land[3], left),
+        ]
+        sums = [view(after, 1), view(before, 0)]
+        late = [sems.ready(sums[0], land[4], right), sems.ready(sums[1], land[5], left)]
+        plans.append((early, sums, late, [view(at, 0), view(at, 1)], land, shape))
+
+    def first():
+        for early, *_ in plans:
+            for copy in early[:2]:
+                copy.start()
+        for early, *_ in plans:
+            for copy in early[2:]:
+                copy.start()
+
+    def middle():
+        for early, sums, late, own, land, shape in plans:
+            for i in range(2):
+                early[i].wait_recv()
+                added(sums[i], [land[i]], shape)
+                late[i].start()
+
+    def last():
+        for early, sums, late, own, land, shape in plans:
+            early[2].wait_recv()
+            late[1].wait_recv()
+            added(own[0], [land[2], land[5]], shape)
+            early[3].wait_recv()
+            late[0].wait_recv()
+            added(own[1], [land[3], land[4]], shape)
+
+    return first, middle, last
+
+
+def ring_spread(place, sems, jobs):
+    plans = []
+    for axis, view in jobs:
+        at = along(place, axis)
+        after, before = (at + 1) % 4, (at + 3) % 4
+        right, left = moved(place, axis, 1), moved(place, axis, -1)
+        here, from_left, from_right = view(at, None), view(before, 0), view(after, 1)
+        plans.append(
             (
-                sems.start(view(far, 1), land[0], right),
-                sems.start(view(far, 0), land[1], left),
-                sems.start(view((at + 1) % 4, 0), land[2], right),
-                sems.start(view((at + 3) % 4, 1), land[3], left),
+                [sems.ready(here, here, right), sems.ready(here, here, left)],
+                [sems.ready(from_left, from_left, right), sems.ready(from_right, from_right, left)],
             )
         )
-    lasts = []
-    for (axis, view, land, shape), (far_right, far_left, _, _) in zip(jobs, state):
-        at = along(place, axis)
-        right, left = moved(place, axis, 1), moved(place, axis, -1)
-        far_right.wait_recv()
-        added(view((at + 1) % 4, 1), [land[0]], shape)
-        one = sems.start(view((at + 1) % 4, 1), land[4], right)
-        far_left.wait_recv()
-        added(view((at + 3) % 4, 0), [land[1]], shape)
-        lasts.append((one, sems.start(view((at + 3) % 4, 0), land[5], left)))
-    for (axis, view, land, shape), (_, _, near_r, near_l), (one, two) in zip(jobs, state, lasts):
-        at = along(place, axis)
-        near_r.wait_recv()
-        two.wait_recv()
-        added(view(at, 0), [land[2], land[5]], shape)
-        near_l.wait_recv()
-        one.wait_recv()
-        added(view(at, 1), [land[3], land[4]], shape)
+
+    def first():
+        for one, two in plans:
+            for copy in one:
+                copy.start()
+
+    def middle():
+        for one, two in plans:
+            for i in range(2):
+                one[i].wait_recv()
+                two[i].start()
+
+    def last():
+        for one, two in plans:
+            for copy in two:
+                copy.wait_recv()
+
+    return first, middle, last
+
+
+def phases(made):
+    for phase in made:
+        phase()
 
 
 sum_parts = [(0, 48, 48), (96, 48, 48), (192, 32, 32)]
@@ -407,7 +448,7 @@
 
             jobs.append((axis, view, lands[at_land : at_land + 6], kv_shape(free)))
             at_land += 6
-        ring_sum(place, sems, jobs)
+        phases(ring_sum(place, sems, jobs))
     grads = work[x % 2, z, y, x // 2].astype(f32)
     cosine, sine = turn[0], turn[1]
     keys = grads * cosine - swapped(grads) * sine
@@ -472,98 +513,138 @@
     )
 
 
-weight_parts = [(0, 80, 64, "zy"), (144, 64, 64, "yz")]
-
-
-def weight_view(ref, place, first, at, rows, second=None):
+big_rows, small_rows = 240, 48
+big_parts = [
+    ("zy", (0, 128, 0, D), (0, 64, 0, D), (64, 64, 0, D)),
+    ("yz", (128, 112, 0, D), (128, 64, 0, D), (192, 48, 0, D)),
+]
+small_parts = [
+    ("zy", (0, 48, 0, 512), (0, 48, 0, 256), (0, 48, 256, 256)),
+    ("yz", (0, 48, 512, 384), (0, 48, 512, 256), (0, 48, 768, 128)),
+]
+
+
+def block_at(ref, lead, block):
+    row, rows, column, columns = block
+    return ref.at[(*lead, pl.ds(row, rows), pl.ds(column, columns))]
+
+
+def weight_view(ref, place, order, stage, halves):
     _, y, z, _ = place
     every = slice(None)
-    if second is None:
-        return ref.at[at, every, rows] if first == "z" else ref.at[every, at, rows]
-    return ref.at[z, at, rows] if first == "z" else ref.at[at, y, rows]
-
-
-def weight_kernel(part_ref, out_ref, work, local_sem, *more):
+
+    def view(at, half):
+        if stage == 0:
+            lead = (at, every) if order[0] == "z" else (every, at)
+        else:
+            lead = (z, at) if order[0] == "z" else (at, y)
+        return block_at(ref, lead, halves[0 if half is None else half + 1])
+
+    return view
+
+
+def sum_lands(parts, stage):
+    lead = (4,) if stage == 0 else ()
+    return [
+        pltpu.VMEM((*lead, halves[h + 1][1], halves[h + 1][3]), bf16)
+        for _, *halves in parts
+        for h in (1, 0, 0, 1, 1, 0)
+    ]
+
+
+def weight_ring_sum(place, sems, parts, work, stage, lands):
+    return ring_sum(
+        place,
+        sems,
+        [
+            (
+                order[stage],
+                weight_view(work, place, order, stage, halves),
+                lands[6 * i : 6 * i + 6],
+                (4,) if stage == 0 else (),
+            )
+            for i, (order, *halves) in enumerate(parts)
+        ],
+    )
+
+
+def weight_ring_spread(place, sems, parts, out, stage):
+    return ring_spread(
+        place,
+        sems,
+        [
+            (order[stage], weight_view(out, place, order, stage, halves))
+            for order, *halves in parts
+        ],
+    )
+
+
+def mate_of(place):
+    x, y, z, core = place
+    return dev(x + 1 - 2 * (x % 2), y, z, core)
+
+
+def final_kernel(big_ref, small_ref, big_out, small_out, work, swap, local_sem, *more):
     lands, (send, recv) = more[:-2], more[-2:]
     place = my_place()
     x, y, z, core = place
-    mate = dev(x + 1 - 2 * (x % 2), y, z, core)
-    load = pltpu.make_async_copy(part_ref, work, local_sem.at[0])
-    load.start()
-    greet([moved(place, a, b) for a in "yz" for b in (1, -1)] + [mate])
-    load.wait()
+    loads = [
+        pltpu.make_async_copy(small_ref, work, local_sem.at[0]),
+        pltpu.make_async_copy(big_ref, big_out.at[z, y], local_sem.at[1]),
+    ]
+    for copy in loads:
+        copy.start()
+    greet([moved(place, a, b) for a in "yz" for b in (1, -1)] + [mate_of(place)])
+    for copy in loads:
+        copy.wait()
     sems = Sems(send, recv)
-    at_land = 0
-    for stage in range(2):
-        jobs = []
-        for row, n0, n1, order in weight_parts:
-
-            def view(at, half, row=row, n0=n0, n1=n1, order=order, stage=stage):
-                rows = pl.ds(row, n0) if half == 0 else pl.ds(row + n0, n1)
-                second = order[1] if stage == 1 else None
-                return weight_view(work, place, order[0], at, rows, second)
-
-            jobs.append(
-                (order[stage], view, lands[at_land : at_land + 6], (4,) if stage == 0 else ())
-            )
-            at_land += 6
-        ring_sum(place, sems, jobs)
-    swaps = []
-    for row, n0, n1, order in weight_parts:
-        mine = work.at[z, y, pl.ds(row, n0 + n1)]
-        swaps.append(sems.start(mine, lands[at_land], mate))
-        at_land += 1
-    for i, ((row, n0, n1, order), copy) in enumerate(zip(weight_parts, swaps)):
-        copy.wait_recv()
-        rows = pl.ds(row, n0 + n1)
-        land = lands[at_land - len(weight_parts) + i]
-        out_ref[z, y, rows] = (
-            work[z, y, rows].astype(f32) + land[...].astype(f32)
-        ).astype(bf16)
-    for stage in (1, 0):
-        firsts = []
-        for row, n0, n1, order in weight_parts:
-            axis = order[stage]
-            rows = pl.ds(row, n0 + n1)
-            second = order[1] if stage == 1 else None
-            here = weight_view(out_ref, place, order[0], along(place, axis), rows, second)
-            firsts.append([sems.start(here, here, moved(place, axis, by)) for by in (1, -1)])
-        seconds = []
-        for (row, n0, n1, order), (to_right, to_left) in zip(weight_parts, firsts):
-            axis = order[stage]
-            at = along(place, axis)
-            second = order[1] if stage == 1 else None
-            to_right.wait_recv()
-            left = weight_view(out_ref, place, order[0], (at + 3) % 4, pl.ds(row, n0), second)
-            seconds.append(sems.start(left, left, moved(place, axis, 1)))
-            to_left.wait_recv()
-            right = weight_view(
-                out_ref, place, order[0], (at + 1) % 4, pl.ds(row + n0, n1), second
-            )
-            seconds.append(sems.start(right, right, moved(place, axis, -1)))
-        for copy in seconds:
-            copy.wait_recv()
+    sum0 = weight_ring_sum(place, sems, small_parts, work, 0, lands[:12])
+    sum1 = weight_ring_sum(place, sems, small_parts, work, 1, lands[12:])
+    pair = sems.ready(work.at[z, y], swap, mate_of(place))
+    big1 = weight_ring_spread(place, sems, big_parts, big_out, 1)
+    big0 = weight_ring_spread(place, sems, big_parts, big_out, 0)
+    out1 = weight_ring_spread(place, sems, small_parts, small_out, 1)
+    out0 = weight_ring_spread(place, sems, small_parts, small_out, 0)
+    sum0[0]()
+    big1[0]()
+    sum0[1]()
+    big1[1]()
+    sum0[2]()
+    sum1[0]()
+    big1[2]()
+    big0[0]()
+    sum1[1]()
+    sum1[2]()
+    pair.start()
+    pair.wait_recv()
+    small_out[z, y] = (work[z, y].astype(f32) + swap[...].astype(f32)).astype(bf16)
+    out1[0]()
+    out1[1]()
+    out1[2]()
+    out0[0]()
+    big0[1]()
+    out0[1]()
+    out0[2]()
+    big0[2]()
     sems.finish()
 
 
-def weight_sum(part, cid):
-    lands = []
-    for stage in range(2):
-        for row, n0, n1, order in weight_parts:
-            lead = (4,) if stage == 0 else ()
-            for n in (n1, n0, n0, n1, n1, n0):
-                lands.append(pltpu.VMEM((*lead, n, D), bf16))
-    for row, n0, n1, order in weight_parts:
-        lands.append(pltpu.VMEM((n0 + n1, D), bf16))
-    big = (4, 4, 272, D)
+def final(big, small, cid):
+    shapes = [(4, 4, n, D) for n in (big_rows, small_rows)]
     return call(
-        weight_kernel,
-        jax.ShapeDtypeStruct(big, bf16),
-        [pltpu.VMEM(big, bf16), pltpu.SemaphoreType.DMA((1,)), *lands],
-        len(weight_parts) * (6 * 2 + 1 + 4 * 2),
+        final_kernel,
+        tuple(jax.ShapeDtypeStruct(s, bf16) for s in shapes),
+        [
+            pltpu.VMEM(shapes[1], bf16),
+            pltpu.VMEM((small_rows, D), bf16),
+            pltpu.SemaphoreType.DMA((2,)),
+            *sum_lands(small_parts, 0),
+            *sum_lands(small_parts, 1),
+        ],
+        24 + 1 + 32,
         cid,
-        (part.reshape(big),),
-        [pl.BlockSpec(memory_space=pl.ANY)],
+        (big, small.reshape(shapes[1])),
+        [pl.BlockSpec(memory_space=pltpu.VMEM), pl.BlockSpec(memory_space=pl.ANY)],
     )
 
 
@@ -583,11 +664,16 @@
 
 
 def keys_of(kv_ref, c, half):
-    rows = pl.ds(pl.multiple_of(half * 128, 128), 128)
-    tile = kv_ref[c, :, rows, :].reshape(256, 128)
+    start = half * 128 if isinstance(half, int) else pl.multiple_of(half * 128, 128)
+    tile = kv_ref[c, :, pl.ds(start, 128), :].reshape(256, 128)
     lane = lanes((256, 128))
     ones = jnp.ones((256, 128), bf16)
     return jnp.where(lane < HD, tile, ones), jnp.where(lane < HD, ones, tile)
+
+
+def both_keys(kv_ref, c0, c1):
+    pairs = zip(keys_of(kv_ref, c0, 0), keys_of(kv_ref, c1, 0))
+    return [jnp.concatenate(pair, 0) for pair in pairs]
 
 
 def hidden_keys(xhi):
@@ -598,7 +684,6 @@
 
 def forward_kernel(scal, q_ref, kv_ref, o_ref, qe_ref, peak, acc):
     me, xhi = scal[32], scal[33]
-    lane = lanes((128, 128))
     for h in range(2):
         for g in range(G):
             piece = q_ref[h, :, g * HD : (g + 1) * HD].astype(f32) * (1.0 / math.sqrt(HD))
@@ -607,60 +692,45 @@
     peak[...] = jnp.full((2, ROWS, 128), -1e30, f32)
     acc[...] = jnp.zeros((2, ROWS, 128), f32)
 
-    def scores(half, kk):
-        return lax.dot_general(qe_ref[half], kk, NT, preferred_element_type=f32)
-
-    def top(half, s):
-        peak[half] = jnp.maximum(peak[half], jnp.maximum(s[:, :128], s[:, 128:]))
-
-    def fold(half, s, vv):
-        p = jnp.exp(s).astype(bf16)
-        acc[half] += jnp.dot(p, vv, preferred_element_type=f32)
-
-    def others(work):
-        def one(i, carry):
-            c = (me + i) % 32
-            kk, vv = keys_of(kv_ref, c, 0)
-            work(1, kk, vv, None)
-            sel = scal[c]
-            kk, vv = keys_of(kv_ref, c, sel)
-            work(sel, kk, vv, None)
-            return carry
-
-        lax.fori_loop(1, 32, one, 0)
-        early_k, early_v = keys_of(kv_ref, me, 0)
-        late_k, late_v = keys_of(kv_ref, me, 1)
-        work(1, early_k, early_v, None)
-        work(0, early_k, early_v, hidden_keys(xhi))
-        work(1, late_k, late_v, hidden_keys(xhi))
-
-    def first(half, kk, vv, hide):
-        s = scores(half, kk)
-        top(half, s if hide is None else jnp.where(hide, -1e30, s))
-
-    def second(half, kk, vv, hide):
-        s = scores(half, kk)
-        fold(half, s if hide is None else jnp.where(hide, -1e30, s), vv)
-
-    others(first)
-    wide_lane = lanes((ROWS, 128))
-
-    def with_column(half, column):
-        one, two, three = split3(-column)
-        held = qe_ref[half].astype(f32)
-        held = jnp.where(wide_lane == HD, one, held)
-        held = jnp.where(wide_lane == HD + 1, two, held)
-        held = jnp.where(wide_lane == HD + 2, three, held)
-        qe_ref[half] = held.astype(bf16)
-
-    for h in range(2):
-        highest = jnp.max(peak[h], 1, keepdims=True)
-        peak[h] = jnp.broadcast_to(highest, (ROWS, 128))
-        with_column(h, highest)
-    others(second)
+    def fold(half, kk, vv, hide=None):
+        s = lax.dot_general(qe_ref[half], kk, NT, preferred_element_type=f32)
+        if hide is not None:
+            s = jnp.where(hide, -1e30, s)
+        tiles = [s[:, e : e + 128] for e in range(0, s.shape[1], 128)]
+        old = peak[half]
+        top = jnp.maximum(
+            old, jnp.max(functools.reduce(jnp.maximum, tiles), 1, keepdims=True)
+        )
+        peak[half] = top
+        p = jnp.concatenate([jnp.exp(t - top) for t in tiles], 1).astype(bf16)
+        acc[half] = acc[half] * jnp.exp(old - top) + jnp.dot(p, vv, preferred_element_type=f32)
+
+    def early_pair(c0, c1):
+        fold(1, *both_keys(kv_ref, c0, c1))
+
+    def other(c):
+        sel = scal[c]
+        fold(sel, *keys_of(kv_ref, c, sel))
+
+    def one(i, carry):
+        c0, c1 = (me + 2 * i + 1) % 32, (me + 2 * i + 2) % 32
+        early_pair(c0, c1)
+        other(c0)
+        other(c1)
+        return carry
+
+    lax.fori_loop(0, 15, one, 0)
+    early_pair((me + 31) % 32, me)
+    other((me + 31) % 32)
+    fold(0, *keys_of(kv_ref, me, 0), hidden_keys(xhi))
+    fold(1, *keys_of(kv_ref, me, 1), hidden_keys(xhi))
+    lane = lanes((ROWS, 128))
     for h in range(2):
         total = acc[h][:, :1]
-        with_column(h, peak[h][:, :1] + jnp.log(total))
+        held = qe_ref[h].astype(f32)
+        for i, part in enumerate(split3(-(peak[h][:, :1] + jnp.log(total)))):
+            held = jnp.where(lane == HD + i, part, held)
+        qe_ref[h] = held.astype(bf16)
         out = acc[h] / total
         for g in range(G):
             o_ref[h, :, g * HD : (g + 1) * HD] = out[g * 128 : (g + 1) * 128, HD:]
@@ -694,86 +764,131 @@
     )
 
 
-def backward_kernel(scal, qe_ref, o_ref, g_ref, kv_ref, dq_ref, dkv_ref, ge, qt, gt, dq, step):
-    me, xhi = scal[32], scal[33]
+def backward_kernel(
+    scal, qe_ref, o_ref, g_ref, kv_ref, part_ref,
+    dq_ref, dkv_ref, sum_ref,
+    ge, qt, gt, dq, work, swap, local_sem, *more,
+):
+    lands, (send, recv) = more[:-2], more[-2:]
+    place = my_place()
+    x, y, z, core = place
+    me, xhi = lax.axis_index("ctx"), x // 2
+    load = pltpu.make_async_copy(part_ref, work, local_sem.at[0])
+    load.start()
+    greet([moved(place, a, b) for a in "yz" for b in (1, -1)] + [mate_of(place)])
+    load.wait()
+    sems = Sems(send, recv)
+    sum0 = weight_ring_sum(place, sems, big_parts, work, 0, lands[:12])
+    sum1 = weight_ring_sum(place, sems, big_parts, work, 1, lands[12:])
+    pair = sems.ready(work.at[z, y], swap, mate_of(place))
+    sum0[0]()
+
     lane = lanes((128, 128))
     for h in range(2):
         for g in range(G):
             cols = slice(g * HD, (g + 1) * HD)
             piece = g_ref[h, :, cols].astype(f32)
             delta = jnp.sum(piece * o_ref[h, :, cols], 1, keepdims=True)
-            one, two, three = split3(-delta)
             held = jnp.concatenate([jnp.zeros((128, HD), f32), piece], 1)
-            held = jnp.where(lane == 0, one, held)
-            held = jnp.where(lane == 1, two, held)
-            held = jnp.where(lane == 2, three, held)
+            for i, value in enumerate(split3(-delta)):
+                held = jnp.where(lane == i, value, held)
             rows = slice(g * 128, (g + 1) * 128)
             ge[h, rows, :] = held.astype(bf16)
             gt[h, :, rows] = held.T.astype(bf16)
             qt[h, :, rows] = qe_ref[h, rows, :].astype(f32).T.astype(bf16)
     dq[...] = jnp.zeros((2, ROWS, 128), f32)
-    under = lax.broadcasted_iota(jnp.int32, (128, 256), 0) < HD
-
-    def tile(half, kk, vv, hide):
-        s = lax.dot_general(qe_ref[half], kk, NT, preferred_element_type=f32)
+
+    def picked(sel, early, late):
+        return jnp.where(jnp.full(early.shape, sel, jnp.int32) > 0, late, early)
+
+    def tile(half, kk, vv, hide=None, late=None):
+        def rows_of(ref):
+            return ref[half] if late is None else picked(half, ref[0], ref[1])
+
+        s = lax.dot_general(rows_of(qe_ref), kk, NT, preferred_element_type=f32)
         if hide is not None:
             s = jnp.where(hide, -1e30, s)
         p = jnp.exp(s)
-        dp = lax.dot_general(ge[half], vv, NT, preferred_element_type=f32)
+        dp = lax.dot_general(rows_of(ge), vv, NT, preferred_element_type=f32)
         ds = (p * dp).astype(bf16)
-        dq[half] += jnp.dot(ds, kk, preferred_element_type=f32)
-        dk = jnp.dot(qt[half], ds, preferred_element_type=f32)
-        dv = jnp.dot(gt[half], p.astype(bf16), preferred_element_type=f32)
-        return jnp.where(under, dk, dv).T
+        step = jnp.dot(ds, kk, preferred_element_type=f32)
+        if late is None:
+            dq[half] += step
+        else:
+            dq[1] += step * late
+            dq[0] += step * (1.0 - late)
+        dk = jnp.dot(rows_of(qt), ds, preferred_element_type=f32)
+        dv = jnp.dot(rows_of(gt), p.astype(bf16), preferred_element_type=f32)
+        return jnp.concatenate([dk[:HD], dv[HD:]], 0).T
 
     def put(c, half, value):
-        rows = pl.ds(pl.multiple_of(half * 128, 128), 128)
-        dkv_ref[c, :, rows, :] = value.astype(bf16).reshape(2, 128, 128)
+        dkv_ref[c, :, half * 128 : (half + 1) * 128, :] = value.astype(bf16).reshape(2, 128, 128)
+
+    def other(c, early):
+        sel = scal[c]
+        late = sel.astype(f32)
+        pairs = zip(keys_of(kv_ref, c, 0), keys_of(kv_ref, c, 1))
+        step = tile(sel, *[picked(sel, *pair) for pair in pairs], late=late)
+        put(c, 0, early + step * (1.0 - late))
+        put(c, 1, step * late)
+
+    beside = {3: [sum0[1]], 10: [sum0[2], sum1[0]], 12: [sum1[1]], 14: [sum1[2], pair.start]}
 
     def one(i, carry):
-        c = (me + i) % 32
-        kk, vv = keys_of(kv_ref, c, 0)
-        step[0] = tile(1, kk, vv, None)
-        step[1] = jnp.zeros((256, 128), f32)
-        sel = scal[c]
-        kk, vv = keys_of(kv_ref, c, sel)
-        step[sel] += tile(sel, kk, vv, None)
-        put(c, 0, step[0])
-        put(c, 1, step[1])
+        for at, steps in beside.items():
+
+            @pl.when(i == at)
+            def _(steps=steps):
+                for step in steps:
+                    step()
+
+        c0, c1 = (me + 2 * i + 1) % 32, (me + 2 * i + 2) % 32
+        early = tile(1, *both_keys(kv_ref, c0, c1))
+        other(c0, early[:256])
+        other(c1, early[256:])
         return carry
 
-    lax.fori_loop(1, 32, one, 0)
-    early_k, early_v = keys_of(kv_ref, me, 0)
-    late_k, late_v = keys_of(kv_ref, me, 1)
-    put(
-        me,
-        0,
-        tile(1, early_k, early_v, None) + tile(0, early_k, early_v, hidden_keys(xhi)),
-    )
-    put(me, 1, tile(1, late_k, late_v, hidden_keys(xhi)))
+    lax.fori_loop(0, 15, one, 0)
+    final_c = (me + 31) % 32
+    early = tile(1, *both_keys(kv_ref, final_c, me))
+    other(final_c, early[:256])
+    put(me, 0, early[256:] + tile(0, *keys_of(kv_ref, me, 0), hidden_keys(xhi)))
+    put(me, 1, tile(1, *keys_of(kv_ref, me, 1), hidden_keys(xhi)))
     for h in range(2):
         for g in range(G):
             dq_ref[h, :, g * HD : (g + 1) * HD] = dq[h, g * 128 : (g + 1) * 128, :HD] * (
                 1.0 / math.sqrt(HD)
             )
-
-
-def attention_backward(scal, qe, o, grad, kv):
-    return local_call(
+    pair.wait_recv()
+    sum_ref[...] = (work[z, y].astype(f32) + swap[...].astype(f32)).astype(bf16)
+    sems.finish()
+
+
+def attention_backward(scal, qe, o, grad, kv, part, cid):
+    big = (4, 4, big_rows, D)
+    vmem = pl.BlockSpec(memory_space=pltpu.VMEM)
+    return call(
         backward_kernel,
         (
             jax.ShapeDtypeStruct((2, 128, QC), f32),
             jax.ShapeDtypeStruct((32, 2, CHIP, 128), bf16),
+            jax.ShapeDtypeStruct((big_rows, D), bf16),
         ),
         [
             pltpu.VMEM((2, ROWS, 128), bf16),
             pltpu.VMEM((2, 128, ROWS), bf16),
             pltpu.VMEM((2, 128, ROWS), bf16),
             pltpu.VMEM((2, ROWS, 128), f32),
-            pltpu.VMEM((2, 256, 128), f32),
+            pltpu.VMEM(big, bf16),
+            pltpu.VMEM((big_rows, D), bf16),
+            pltpu.SemaphoreType.DMA((1,)),
+            *sum_lands(big_parts, 0),
+            *sum_lands(big_parts, 1),
         ],
-        (scal, qe, o, grad, kv),
-        50_000_000_000,
+        25,
+        cid,
+        (scal, qe, o, grad, kv, part.reshape(big)),
+        [pl.BlockSpec(memory_space=pltpu.SMEM), *[vmem] * 4, pl.BlockSpec(memory_space=pl.ANY)],
     )
 
 
@@ -884,8 +999,6 @@
     mlp_got = lax.ppermute(cut(mlp_part, 1 - core, 1, 2), ("ctx", "wsh"), twin)
     mlp_sum = cut(mlp_part, core, 1, 2).astype(f32) + mlp_got.astype(f32)
     mlp_far = crossed(mlp_sum[1].astype(bf16))
-    mlp_own = (mlp_sum[0] + mlp_far.astype(f32)).reshape(TOK, D)
-    output = (own_rows(stream[:CHIP]) + mlp_own).astype(bf16)
     gate_wgrad = jnp.einsum("tf,td->fd", gate_grad, normed_two, preferred_element_type=f32)
     up_wgrad = jnp.einsum("tf,td->fd", up_grad, normed_two, preferred_element_type=f32)
     down_wgrad = jnp.einsum("tf,td->fd", hidden, cot, preferred_element_type=f32)
@@ -901,10 +1014,21 @@
     att_grad = jnp.einsum(
         "td,id->ti", branch_grad, cut(out_full, core * QC, QC, 0), preferred_element_type=f32
     ).astype(bf16)
-    dq, dkv_part = attention_backward(
-        scal, qe, attended_f, att_grad.reshape(2, 128, QC), kv_all
-    )
+    large = jnp.concatenate(
+        [
+            *[w.astype(bf16) for w in (gate_wgrad, up_wgrad, down_wgrad)],
+            jnp.zeros((16 * big_rows - 3 * FS, D), bf16),
+        ],
+        0,
+    )
+    dq, dkv_part, large_own = attention_backward(
+        scal, qe, attended_f, att_grad.reshape(2, 128, QC), kv_all, large, 5
+    )
+    norm_other, mlp_far, dq = lax.optimization_barrier((norm_other, mlp_far, dq))
     pg = closing(dkv_part.reshape(2, 4, 4, 2, CHIP, 128), dq, turn, 4).reshape(2 * CHIP, QKV)
+
+    mlp_own = (mlp_sum[0] + mlp_far.astype(f32)).reshape(TOK, D)
+    output = (own_rows(stream[:CHIP]) + mlp_own).astype(bf16)
 
     bias_grad = cut(jnp.sum(pg.astype(f32), 0), wsh * 288, 288, 0)
     inv_one = rms_inverse(resid_both)
@@ -930,26 +1054,27 @@
     vectors = jnp.stack(
         [jnp.pad(v, (0, D - v.shape[0])) for v in (bias_grad, gain_one_grad, gain_two_grad)]
     )
-    part = jnp.concatenate(
+    small = jnp.concatenate(
         [
-            *[w.astype(bf16) for w in (gate_wgrad, up_wgrad, down_wgrad, out_wgrad)],
+            out_wgrad.astype(bf16),
             qkv_wgrad.astype(bf16).reshape(288, D),
-            jnp.pad(vectors, ((0, 189), (0, 0))).astype(bf16),
+            jnp.pad(vectors, ((0, 16 * small_rows - 515), (0, 0))).astype(bf16),
         ],
         0,
     )
-    total = weight_sum(part, 6).reshape(16 * 272, D).astype(f32)
+    large, small = final(large_own, small, 6)
+    large, small = large.reshape(16 * big_rows, D), small.reshape(16 * small_rows, D)
     return (
         output,
         token_grad,
-        total[4161, :224],
-        total[3872:4160].reshape(224, QKV),
-        total[4160, :288],
-        total[3648:3872],
-        total[4162, :224],
-        total[:1216].T,
-        total[1216:2432].T,
-        total[2432:3648],
+        small[513, :224].astype(f32),
+        small[224:512].reshape(224, QKV).astype(f32),
+        small[512, :288].astype(f32),
+        small[:224].astype(f32),
+        small[514, :224].astype(f32),
+        large[:FS].astype(f32).T,
+        large[FS : 2 * FS].astype(f32).T,
+        large[2 * FS : 3 * FS].astype(f32),
     )
 
 

time: 470 us -> 412 us (0.88)
  the two profiles are of different devices: /device:TPU:0 before, /device:TPU:2 now
where the time goes in v3:
time: 412 us; the launch traced here: 405 us
  Pallas kernels  288 us (70%)
  other arithmetic  46.7 us (11%)
  matrix products  27.7 us (7%)
  local copies, waits for them, and re-layouts  19.4 us (5%)
  between operations  17.9 us (4%)
  starting transfers between devices  4.89 us (1%)
    pallas_call x6, Pallas kernels, call(): pl.pallas_call(kernel, out_shape=out_shape, in_specs=specs if specs is no...  260 us
    pallas_call x1, Pallas kernels, local_call(): pl.pallas_call(kernel, out_shape=out_shape, in_specs=[pl.BlockSpec(memory...  28.7 us
    dot_general x5, matrix products, dot(): return jnp.dot(a, b, preferred_element_type=f32)  8.68 us
  transfers between devices with their start and end apart: 5, of which 0 were waited for; matrix products, arithmetic and copies ran while one was open for 8% of the time, Pallas kernels for 29%

profile of v3, /device:TPU:2, one launch (start us, length us, event | category | flops | bytes accessed | tf_op | source)
XLA Modules:
  0.0 405.0 jit_solution(9493501672823102503)
XLA Ops:
  10.0 0.7 tile.31
  10.8 0.7 tile.14
  11.5 0.7 tile.12
  13.0 0.7 pad_maximum_fusion.2.turn
  13.7 0.6 fusion.38.small
  14.3 0.6 broadcast_in_dim.36.mark
  14.9 54.0 %shard_map.186 = (bf16[2,2,2,64,896]{4,3,2,1,0:T(8,128)(2,1)}, bf16[4,224,1152]{2,1,0:T(8,128)(2,1)}, bf16[4,16,1152]{2,1,0:T(8,128)(2,1)}, bf16[2,128,448]{2,1,0:T(8,128)(2,1)}, bf16[2,4,4,2,272,128]{5,4,3,2,1,0:T(8,128)(2,1)}) custom-call(bf16[2,64,896]{2,1,0:T(8,128)(2,1)} %bitcast.116, bf16[2,64,896]{2,1,0:T(8,128)(2,1)} %bitcast.137, ...), custom_call_target="tpu_custom_call" | custom-call | tf_op jit(solution)/shard_map/pallas_call | solution.py:97
  68.9 2.1 collective-permute-start
  71.0 1.5 fusion.39
  72.5 0.7 pad_add_fusion.scal
  73.1 28.7 %shard_map.187 = (f32[2,128,448]{2,1,0:T(8,128)}, bf16[2,896,128]{2,1,0:T(8,128)(2,1)}) custom-call(s32[34]{0:T(128)} %pad_add_fusion.scal, bf16[2,128,448]{2,1,0:T(8,128)(2,1)} %get-tuple-element.33.q_ref, bf16[32,2,272,128]{3,2,1,0:T(8,128)(2,1)} %bitcast.113), custom_call_target="tpu_custom_call" | custom-call | flops 20000000000 | bytes 10000000 | tf_op jit(solution)/shard_map/pallas_call | solution.py:741
  102.4 1.8 convert_element_type.202
  104.2 10.1 %shard_map.188 = bf16[2,2,256,448]{3,2,1,0:T(8,128)(2,1)} custom-call(bf16[256,448]{1,0:T(8,128)(2,1)} %bitcast.126), custom_call_target="tpu_custom_call" | custom-call | tf_op jit(solution)/shard_map/pallas_call | solution.py:97
  114.3 0.7 pad.50.clone
  115.0 0.8 convert_reduce_fusion.1
  115.8 0.6 slice_reduce_fusion
  116.6 0.6 add_rsqrt_fusion.1
  117.2 2.2 fusion.56
  119.7 0.6 copy.34
  120.3 1.7 pad_maximum_fusion.1
  122.0 2.2 fusion.12
  124.2 2.0 multiply_reduce_fusion.1
  127.0 1.4 copy-done.43
  128.4 1.5 fusion.59
  130.1 1.5 fusion.58
  131.6 2.6 multiply_convert_fusion
  134.2 1.6 convolution_convert_fusion.4
  135.7 2.8 convolution_convert_fusion
  138.6 1.5 fusion.60
  140.1 2.8 convolution_convert_fusion.2
  142.9 0.8 dynamic-slice_bitcast_fusion
  144.3 2.8 convolution_convert_fusion.1
  147.1 2.5 add_convert_fusion
  149.6 12.4 %shard_map.189 = bf16[2,2,64,896]{3,2,1,0:T(8,128)(2,1)} custom-call(bf16[2,2,2,64,896]{4,3,2,1,0:T(8,128)(2,1)} %bitcast.128), custom_call_target="tpu_custom_call" | custom-call | tf_op jit(solution)/shard_map/pallas_call | solution.py:97
  162.0 1.3 multiply_reduce_fusion.3
  163.3 2.0 collective-permute-start.2
  165.3 6.9 %maximum_maximum_fusion = bf16[3840,896]{1,0:T(8,128)(2,1)} fusion(bf16[1216,896]{1,0:T(8,128)(2,1)} %convolution_convert_fusion, bf16[1216,896]{1,0:T(8,128)(2,1)} %convolution_convert_fusion.1, bf16[1216,896]{1,0:T(8,128)(2,1)} %convolution_convert_fusion.2, bf16[3840]{0:T(1024)(128)(2,1)S(1)} %copy-done.34), kind=kLoop, calls=%fused_computation | loop fusion | flops 27525120 | bytes 13426176 | tf_op jit(solution)/shard_map/concatenate | solution.py:1017
  172.3 2.4 fusion.55
  174.8 1.3 convert_add_fusion.2
  176.1 0.9 copy-done.12
  177.0 0.7 fusion.32
  178.4 0.8 copy.28
  179.3 65.7 %shard_map.190 = (f32[2,128,448]{2,1,0:T(8,128)}, bf16[32,2,256,128]{3,2,1,0:T(8,128)(2,1)}, bf16[240,896]{1,0:T(8,128)(2,1)}) custom-call(s32[34]{0:T(128)} %pad_add_fusion.scal, bf16[2,896,128]{2,1,0:T(8,128)(2,1)} %get-tuple-element.38.qe_ref, f32[2,128,448]{2,1,0:T(8,128)} %get-tuple-element.35.o_ref, bf16[2,128,448]{2,1,0:T(8,128)(2,1)} %bitcast.127, ...), custom_call_target="tpu_custom_call" | custom-call | tf_op jit(solution)/shard_map/pallas_call | solution.py:97
  245.0 0.8 constant_dynamic-slice_fusion.1
  245.8 45.2 %shard_map.191 = bf16[2,256,1152]{2,1,0:T(8,128)(2,1)} custom-call(bf16[2,4,4,2,256,128]{5,4,3,2,1,0:T(8,128)(2,1)} %bitcast.115, f32[2,128,448]{2,1,0:T(8,128)} %get-tuple-element.42.dq_ref, f32[2,256,128]{2,1,0:T(8,128)} %pad_maximum_fusion.2.turn), custom_call_target="tpu_custom_call" | custom-call | tf_op jit(solution)/shard_map/pallas_call | solution.py:97
  291.0 1.6 convert_reduce_fusion
  292.6 1.9 slice.114
  294.6 1.3 multiply_reduce_fusion.4
  296.5 1.6 convolution_convert_fusion.3
  298.0 2.4 reshape.418
  300.4 1.3 multiply_reduce_fusion.2
  301.9 2.4 fusion.10
  304.3 0.6 convolution_convert_fusion.5
  305.3 1.2 pad_maximum_fusion
  306.5 72.4 %shard_map.192 = (bf16[4,4,240,896]{3,2,1,0:T(8,128)(2,1)}, bf16[4,4,48,896]{3,2,1,0:T(8,128)(2,1)}) custom-call(bf16[240,896]{1,0:T(8,128)(2,1)} %get-tuple-element.44.big_ref, bf16[4,4,48,896]{3,2,1,0:T(8,128)(2,1)} %bitcast.111), custom_call_target="tpu_custom_call" | custom-call | tf_op jit(solution)/shard_map/pallas_call | solution.py:97
  379.0 1.4 fusion.46
  380.4 1.3 slice_convert_fusion.6
  381.7 1.9 slice_convert_fusion.3
  383.7 1.1 slice_convert_fusion.1
  384.9 0.8 fusion.17
  385.7 1.2 reshape.427
  386.9 8.2 %slice_convert_fusion = (f32[1216,896]{1,0:T(8,128)}, f32[896,1216]{0,1:T(8,128)}, f32[896,1216]{0,1:T(8,128)}) fusion(bf16[3840,896]{1,0:T(8,128)(2,1)} %bitcast.104), kind=kLoop, calls=%fused_computation.13 | loop fusion | flops 3268608 | bytes 19611648 | tf_op jit(solution)/shard_map/convert_element_type | solution.py:1077
  395.1 1.7 fusion.26
  396.8 1.0 fusion.20
  (128 shorter events, 5.3 us)
Async XLA Ops:
  7.2 124.4 %copy-start = (bf16[1216,896]{1,0:T(8,128)(2,1)S(1)}, bf16[1216,896]{1,0:T(8,128)(2,1)}, u32[]{:S(2)}) copy-start(bf16[1216,896]{1,0:T(8,128)(2,1)} %param.20) | copy-start | bytes 6537220
  7.2 114.8 %all-gather.2.cloned.1.call-start = ((), (), s32[]{:S(2)}) async-start(), calls=%async_computation | async-start | bytes 2007040 | tf_op jit(solution)/shard_map/all_gather | solution.py:963
  68.9 50.5 %collective-permute-start = (bf16[2,256,896]{2,1,0:T(8,128)(2,1)}, bf16[2,256,896]{2,1,0:T(8,128)(2,1)S(1)}, u32[]{:S(2)}, u32[]{:S(2)}) collective-permute-start(bf16[2,256,896]{2,1,0:T(8,128)(2,1)} %bitcast.107), channel_id=1, source_target_pairs={{0,66},{1,67},{2,64},{3,65},{4,70},{5,71},{6,68},{7,69},{8,74},{9,... | collective-permute-start | bytes 2752520 | tf_op jit(solution)/shard_map/ppermute | solution.py:947
  73.1 28.7 %copy-start.42 = (bf16[224]{0:T(256)(128)(2,1)S(1)}, bf16[224]{0:T(256)(128)(2,1)}, u32[]{:S(2)}) copy-start(bf16[224]{0:T(256)(128)(2,1)} %param.13) | copy-start | bytes 1348
  101.9 14.6 %copy-start.9 = (bf16[128,896]{1,0:T(8,128)(2,1)S(1)}, bf16[128,896]{1,0:T(8,128)(2,1)}, u32[]{:S(2)}) copy-start(bf16[128,896]{1,0:T(8,128)(2,1)} %param.11) | copy-start | bytes 688132
  114.3 5.1 %copy-start.8 = (bf16[2,2,2,64,896]{4,3,2,1,0:T(8,128)(2,1)S(1)}, bf16[2,2,2,64,896]{4,3,2,1,0:T(8,128)(2,1)}, u32[]{:S(2)}) copy-start(bf16[2,2,2,64,896]{4,3,2,1,0:T(8,128)(2,1)} %get-tuple-element.29) | copy-start | bytes 2752516
  116.4 45.6 %copy-start.30 = (f32[896]{0:T(1024)}, f32[896]{0:T(1024)S(1)}, u32[]{:S(2)}) copy-start(f32[896]{0:T(1024)S(1)} %get-tuple-element.49) | copy-start | bytes 10756
  122.0 2.2 copy-start.5
  122.0 2.2 copy-start.15
  126.2 35.9 %copy-start.2 = (f32[512,896]{1,0:T(8,128)}, f32[512,896]{1,0:T(8,128)S(1)}, u32[]{:S(2)}) copy-start(f32[512,896]{1,0:T(8,128)S(1)} %get-tuple-element.71) | copy-start | bytes 5505028
  126.2 2.3 copy-start.43
  126.2 3.8 copy-start.32
  126.8 35.3 %copy-start.37 = (f32[256]{0:T(256)}, f32[256]{0:T(256)S(1)}, u32[]{:S(2)}) copy-start(f32[256]{0:T(256)S(1)} %get-tuple-element.67) | copy-start | bytes 3076
  128.4 1.6 copy-start.14
  130.1 1.5 copy-start.28
  135.7 7.2 %copy-start.26 = (bf16[512,896]{1,0:T(8,128)(2,1)}, bf16[512,896]{1,0:T(8,128)(2,1)S(1)}, u32[]{:S(2)}) copy-start(bf16[512,896]{1,0:T(8,128)(2,1)S(1)} %convolution_convert_fusion.4) | copy-start | bytes 2752516
  143.7 31.0 %collective-permute-start.1 = (bf16[2,2,1,64,896]{4,3,1,2,0:T(8,128)(2,1)}, bf16[2,2,1,64,896]{4,3,1,2,0:T(8,128)(2,1)}, u32[]{:S(2)}, u32[]{:S(2)}) collective-permute-start(bf16[2,2,1,64,896]{4,3,1,2,0:T(8,128)(2,1)} %dynamic-slice_bitcast_fusion), channel_id=1, source_target_pairs={{0,1},{1,0},{2,3},{3,2},{4,5},{5,4},{6,7},{7,6},{8,9},{9,8},{10,11... | collective-permute-start | bytes 1376264 | tf_op jit(solution)/shard_map/ppermute | solution.py:999
  149.6 15.7 %copy-start.34 = (bf16[3840]{0:T(1024)(128)(2,1)S(1)}, bf16[3840]{0:T(1024)(128)(2,1)}, u32[]{:S(2)}) copy-start(bf16[3840]{0:T(1024)(128)(2,1)} %pad.50.clone) | copy-start | bytes 23044
  163.3 9.0 %copy-start.3 = (f32[512,896]{1,0:T(8,128)S(1)}, f32[512,896]{1,0:T(8,128)}, u32[]{:S(2)}) copy-start(f32[512,896]{1,0:T(8,128)} %copy-done.2) | copy-start | bytes 5505028
  163.3 9.0 %copy-start.7 = (bf16[2,2,64,896]{3,2,1,0:T(8,128)(2,1)S(1)}, bf16[2,2,64,896]{3,2,1,0:T(8,128)(2,1)}, u32[]{:S(2)}) copy-start(bf16[2,2,64,896]{3,2,1,0:T(8,128)(2,1)} %shard_map.189) | copy-start | bytes 1376260
  163.3 9.0 %copy-start.31 = (f32[896]{0:T(1024)S(1)}, f32[896]{0:T(1024)}, u32[]{:S(2)}) copy-start(f32[896]{0:T(1024)} %copy-done.30) | copy-start | bytes 10756
  163.3 9.0 %copy-start.38 = (f32[256]{0:T(256)S(1)}, f32[256]{0:T(256)}, u32[]{:S(2)}) copy-start(f32[256]{0:T(256)} %copy-done.37) | copy-start | bytes 3076
  163.3 82.4 %collective-permute-start.2 = (bf16[256,896]{1,0:T(8,128)(2,1)}, bf16[256,896]{1,0:T(8,128)(2,1)}, u32[]{:S(2)}, u32[]{:S(2)}) collective-permute-start(bf16[256,896]{1,0:T(8,128)(2,1)} %bitcast.102), channel_id=1, source_target_pairs={{0,66},{1,67},{2,64},{3,65},{4,70},{5,71},{6,68},{7,69},{8,74},{9,... | collective-permute-start | bytes 1376264 | tf_op jit(solution)/shard_map/ppermute | solution.py:947
  172.3 2.5 copy-start.27
  172.3 5.7 %copy-start.11 = (bf16[896,896]{1,0:T(8,128)(2,1)S(1)}, bf16[896,896]{1,0:T(8,128)(2,1)}, u32[]{:S(2)}) copy-start(bf16[896,896]{1,0:T(8,128)(2,1)} %all-gather.2.cloned.1.call-done) | copy-start | bytes 4816900
  174.8 3.2 copy-start.23
  176.1 0.9 copy-start.12
  177.7 68.1 %collective-permute-start.3 = (bf16[2,1,64,896]{3,2,1,0:T(8,128)(2,1)}, bf16[2,1,64,896]{3,2,1,0:T(8,128)(2,1)}, u32[]{:S(2)}, u32[]{:S(2)}) collective-permute-start(bf16[2,1,64,896]{3,2,1,0:T(8,128)(2,1)} %fusion.32), channel_id=1, source_target_pairs={{0,66},{1,67},{2,64},{3,65},{4,70},{5,71},{6,68},{7,69},{8,74},{9,... | collective-permute-start | bytes 688136 | tf_op jit(solution)/shard_map/ppermute | solution.py:947
  179.3 65.7 %copy-start.18 = (f32[256,896]{1,0:T(8,128)S(1)}, f32[256,896]{1,0:T(8,128)}, u32[]{:S(2)}) copy-start(f32[256,896]{1,0:T(8,128)} %get-tuple-element.51) | copy-start | bytes 2752516
  245.8 48.8 %copy-start.33 = (f32[512]{0:T(512)S(1)}, f32[512]{0:T(512)}, u32[]{:S(2)}) copy-start(f32[512]{0:T(512)} %copy-done.32) | copy-start | bytes 6148
  291.0 4.9 %copy-start.4 = (bf16[2,256,1152]{2,1,0:T(8,128)(2,1)S(1)}, bf16[2,256,1152]{2,1,0:T(8,128)(2,1)}, u32[]{:S(2)}) copy-start(bf16[2,256,1152]{2,1,0:T(8,128)(2,1)} %shard_map.191) | copy-start | bytes 3538948
  291.0 4.9 %copy-start.6 = (f32[1,2,256,896]{3,2,0,1:T(8,128)S(1)}, f32[1,2,256,896]{3,2,0,1:T(8,128)}, u32[]{:S(2)}) copy-start(f32[1,2,256,896]{3,2,0,1:T(8,128)} %get-tuple-element.61) | copy-start | bytes 5505028
  291.0 4.9 %copy-start.29 = (bf16[224,1152]{1,0:T(8,128)(2,1)S(1)}, bf16[224,1152]{1,0:T(8,128)(2,1)}, u32[]{:S(2)}) copy-start(bf16[224,1152]{1,0:T(8,128)(2,1)} %w_ref.1) | copy-start | bytes 1548292
  291.0 4.9 %copy-start.39 = (f32[1,2,2,128]{3,1,2,0:T(2,128)S(1)}, f32[1,2,2,128]{3,1,2,0:T(2,128)}, u32[]{:S(2)}) copy-start(f32[1,2,2,128]{3,1,2,0:T(2,128)} %copy.34) | copy-start | bytes 6148
  294.6 1.9 copy-start.41
  296.5 4.0 copy-start.36
  301.9 2.4 copy-start.16
  301.9 2.4 copy-start.17
  301.9 2.4 copy-start.24
  304.3 1.0 copy-start.21
  306.5 78.2 %copy-start.25 = (bf16[1,256,1152]{2,1,0:T(8,128)(2,1)S(1)}, bf16[1,256,1152]{2,1,0:T(8,128)(2,1)}, u32[]{:S(2)}) copy-start(bf16[1,256,1152]{2,1,0:T(8,128)(2,1)} %slice.114) | copy-start | bytes 1769476
  378.9 5.9 %copy-start.10 = (bf16[128,896]{1,0:T(8,128)(2,1)S(1)}, bf16[128,896]{1,0:T(8,128)(2,1)}, u32[]{:S(2)}) copy-start(bf16[128,896]{1,0:T(8,128)(2,1)} %param.11) | copy-start | bytes 688132
  378.9 5.9 %copy-start.19 = (bf16[4,224,1152]{2,1,0:T(8,128)(2,1)S(1)}, bf16[4,224,1152]{2,1,0:T(8,128)(2,1)}, u32[]{:S(2)}) copy-start(bf16[4,224,1152]{2,1,0:T(8,128)(2,1)} %get-tuple-element.43) | copy-start | bytes 6193156
  378.9 5.9 %copy-start.35 = (f32[896]{0:T(1024)S(1)}, f32[896]{0:T(1024)}, u32[]{:S(2)}) copy-start(f32[896]{0:T(1024)} %get-tuple-element.48) | copy-start | bytes 10756
  379.0 5.9 %copy-start.40 = (f32[128]{0:T(128)S(1)}, f32[128]{0:T(128)}, u32[]{:S(2)}) copy-start(f32[128]{0:T(128)} %add_rsqrt_fusion.1) | copy-start | bytes 1540
  386.9 8.2 %copy-start.13 = (f32[2,2,1,64,896]{4,3,1,2,0:T(8,128)S(1)}, f32[2,2,1,64,896]{4,3,1,2,0:T(8,128)}, u32[]{:S(2)}) copy-start(f32[2,2,1,64,896]{4,3,1,2,0:T(8,128)} %copy-done.12) | copy-start | bytes 2752516
  386.9 8.2 %copy-start.20 = (f32[256,896]{1,0:T(8,128)S(1)}, f32[256,896]{1,0:T(8,128)}, u32[]{:S(2)}) copy-start(f32[256,896]{1,0:T(8,128)} %get-tuple-element.59) | copy-start | bytes 2752516
  386.9 9.9 %copy-start.22 = (f32[2,1,64,896]{3,2,1,0:T(8,128)S(1)}, f32[2,1,64,896]{3,2,1,0:T(8,128)}, u32[]{:S(2)}) copy-start(f32[2,1,64,896]{3,2,1,0:T(8,128)} %constant_dynamic-slice_fusion.1) | copy-start | bytes 1376260
  386.9 10.9 %copy-start.1 = (bf16[1216,896]{1,0:T(8,128)(2,1)S(1)}, bf16[1216,896]{1,0:T(8,128)(2,1)}, u32[]{:S(2)}) copy-start(bf16[1216,896]{1,0:T(8,128)(2,1)} %param.20) | copy-start | bytes 6537220
Sparse Core Ops, SparseCore 0:
  69.0 22.4 all-gather.1

commit v4 on v3

--- a/solution.py
+++ b/solution.py
@@ -50,6 +50,10 @@
 
 def along(place, axis):
     return place["xyz".index(axis)]
+
+
+def others(place, axes):
+    return [moved(place, a, k) for a in axes for k in (1, 2, 3)]
 
 
 def greet(devices):
@@ -212,7 +216,7 @@
     x, y, z, core = place
     sibling, cross = pair_of(place)
     mate = dev(x + 1 - 2 * (x % 2), y, z, core)
-    greet([sibling] + [moved(place, a, b) for a in "xyz" for b in (1, -1)])
+    greet([sibling] + others(place, "xyz"))
     sems = Sems(send, recv)
     mine = (x // 2) * 2 + core
     theirs = (1 - x // 2) * 2 + core
@@ -289,7 +293,7 @@
                 return chips(all_ref, place, free, axis, at, rows[half])
 
             jobs.append((axis, view))
-        phases(ring_spread(place, sems, jobs))
+        phases((ring_spread if stage == 2 else direct_spread)(place, sems, jobs))
     sems.finish()
 
 
@@ -405,6 +409,67 @@
     return first, middle, last
 
 
+def direct_sum(place, sems, jobs):
+    plans = []
+    for axis, view, land, shape in jobs:
+        at = along(place, axis)
+        copies = [
+            sems.ready(view((at + k) % 4, None), land[k - 1], moved(place, axis, k))
+            for k in (1, 3, 2)
+        ]
+        plans.append((copies, view(at, None), land, shape))
+
+    def first():
+        for copies, *_ in plans:
+            for copy in copies:
+                copy.start()
+
+    def last():
+        for copies, own, land, shape in plans:
+            for copy in copies:
+                copy.wait_recv()
+            added(own, land, shape)
+
+    return first, last
+
+
+def direct_spread(place, sems, jobs):
+    plans = []
+    for axis, view in jobs:
+        here = view(along(place, axis), None)
+        plans.append([sems.ready(here, here, moved(place, axis, k)) for k in (1, 3, 2)])
+
+    def first():
+        for copies in plans:
+            for copy in copies:
+                copy.start()
+
+    def last():
+        for copies in plans:
+            for copy in copies:
+                copy.wait_recv()
+
+    return first, last
+
+
+def whole_sum(place, sems, axis, source, land, result):
+    copies = [
+        sems.ready(source, land[k - 1], moved(place, axis, k)) for k in (1, 3, 2)
+    ]
+
+    def first():
+        for copy in copies:
+            copy.start()
+
+    def last():
+        for copy in copies:
+            copy.wait_recv()
+        total = sum([t[...].astype(f32) for t in land], source[...].astype(f32))
+        result[...] = total.astype(bf16)
+
+    return first, last
+
+
 def phases(made):
     for phase in made:
         phase()
@@ -431,7 +496,7 @@
     place = my_place()
     x, y, z, core = place
     sibling, cross = pair_of(place)
-    greet([sibling] + [moved(place, a, b) for a in "xyz" for b in (1, -1)])
+    greet([sibling] + others(place, "xyz"))
     keep = pltpu.make_async_copy(part_ref, work, local_sem.at[0])
     keep.start()
     keep.wait()
@@ -443,12 +508,13 @@
             axis, free = order[stage], order[stage + 1 :]
 
             def view(at, half, row=row, n0=n0, n1=n1, axis=axis, free=free):
-                rows = pl.ds(row, n0) if half == 0 else pl.ds(row + n0, n1)
-                return chips(work, place, free, axis, at, rows)
-
-            jobs.append((axis, view, lands[at_land : at_land + 6], kv_shape(free)))
-            at_land += 6
-        phases(ring_sum(place, sems, jobs))
+                rows = {None: pl.ds(row, n0 + n1), 0: pl.ds(row, n0), 1: pl.ds(row + n0, n1)}
+                return chips(work, place, free, axis, at, rows[half])
+
+            n_lands = 6 if stage == 0 else 3
+            jobs.append((axis, view, lands[at_land : at_land + n_lands], kv_shape(free)))
+            at_land += n_lands
+        phases((ring_sum if stage == 0 else direct_sum)(place, sems, jobs))
     grads = work[x % 2, z, y, x // 2].astype(f32)
     cosine, sine = turn[0], turn[1]
     keys = grads * cosine - swapped(grads) * sine
@@ -494,7 +560,7 @@
     for stage in range(3):
         for (row, n0, n1), order in zip(sum_parts, orders):
             lead = kv_shape(order[stage + 1 :])
-            for n in (n1, n0, n0, n1, n1, n0):
+            for n in (n1, n0, n0, n1, n1, n0) if stage == 0 else [n0 + n1] * 3:
                 lands.append(pltpu.VMEM((*lead, n, 128), bf16))
     shape = (2, 4, 4, 2, CHIP, 128)
     return call(
@@ -513,15 +579,12 @@
     )
 
 
-big_rows, small_rows = 240, 48
+big_rows, small_rows = 240, 32
 big_parts = [
     ("zy", (0, 128, 0, D), (0, 64, 0, D), (64, 64, 0, D)),
     ("yz", (128, 112, 0, D), (128, 64, 0, D), (192, 48, 0, D)),
 ]
-small_parts = [
-    ("zy", (0, 48, 0, 512), (0, 48, 0, 256), (0, 48, 256, 256)),
-    ("yz", (0, 48, 512, 384), (0, 48, 512, 256), (0, 48, 768, 128)),
-]
+small_parts = [("zy", (0, 32, 0, 512)), ("yz", (0, 32, 512, 384))]
 
 
 def block_at(ref, lead, block):
@@ -529,13 +592,12 @@
     return ref.at[(*lead, pl.ds(row, rows), pl.ds(column, columns))]
 
 
-def weight_view(ref, place, order, stage, halves):
+def weight_view(ref, place, order, stage, halves, only=slice(None)):
     _, y, z, _ = place
-    every = slice(None)
 
     def view(at, half):
         if stage == 0:
-            lead = (at, every) if order[0] == "z" else (every, at)
+            lead = (at, only) if order[0] == "z" else (only, at)
         else:
             lead = (z, at) if order[0] == "z" else (at, y)
         return block_at(ref, lead, halves[0 if half is None else half + 1])
@@ -552,15 +614,16 @@
     ]
 
 
-def weight_ring_sum(place, sems, parts, work, stage, lands):
-    return ring_sum(
+def weight_sum(kind, place, sems, parts, work, stage, lands):
+    n = len(lands) // len(parts)
+    return kind(
         place,
         sems,
         [
             (
                 order[stage],
                 weight_view(work, place, order, stage, halves),
-                lands[6 * i : 6 * i + 6],
+                lands[n * i : n * i + n],
                 (4,) if stage == 0 else (),
             )
             for i, (order, *halves) in enumerate(parts)
@@ -568,12 +631,12 @@
     )
 
 
-def weight_ring_spread(place, sems, parts, out, stage):
-    return ring_spread(
+def weight_spread(kind, place, sems, parts, out, stage, only=slice(None)):
+    return kind(
         place,
         sems,
         [
-            (order[stage], weight_view(out, place, order, stage, halves))
+            (order[stage], weight_view(out, place, order, stage, halves, only))
             for order, *halves in parts
         ],
     )
@@ -584,67 +647,93 @@
     return dev(x + 1 - 2 * (x % 2), y, z, core)
 
 
-def final_kernel(big_ref, small_ref, big_out, small_out, work, swap, local_sem, *more):
+def final_kernel(
+    big_ref, small_ref, vec_ref, big_out, small_out, vec_out,
+    work, swap, vec_sums, vec_lands, local_sem, *more,
+):
     lands, (send, recv) = more[:-2], more[-2:]
     place = my_place()
     x, y, z, core = place
+    mate = mate_of(place)
     loads = [
         pltpu.make_async_copy(small_ref, work, local_sem.at[0]),
         pltpu.make_async_copy(big_ref, big_out.at[z, y], local_sem.at[1]),
     ]
     for copy in loads:
         copy.start()
-    greet([moved(place, a, b) for a in "yz" for b in (1, -1)] + [mate_of(place)])
+    greet([*others(place, "yz"), mate])
     for copy in loads:
         copy.wait()
     sems = Sems(send, recv)
-    sum0 = weight_ring_sum(place, sems, small_parts, work, 0, lands[:12])
-    sum1 = weight_ring_sum(place, sems, small_parts, work, 1, lands[12:])
-    pair = sems.ready(work.at[z, y], swap, mate_of(place))
-    big1 = weight_ring_spread(place, sems, big_parts, big_out, 1)
-    big0 = weight_ring_spread(place, sems, big_parts, big_out, 0)
-    out1 = weight_ring_spread(place, sems, small_parts, small_out, 1)
-    out0 = weight_ring_spread(place, sems, small_parts, small_out, 0)
+    sum0 = weight_sum(direct_sum, place, sems, small_parts, work, 0, lands[:6])
+    sum1 = weight_sum(direct_sum, place, sems, small_parts, work, 1, lands[6:])
+    vec_land = [vec_lands.at[i] for i in range(7)]
+    vec0 = whole_sum(place, sems, "z", vec_ref, vec_land[:3], vec_sums.at[0])
+    vec1 = whole_sum(place, sems, "y", vec_sums.at[0], vec_land[3:6], vec_sums.at[1])
+    vec_pair = sems.ready(vec_sums.at[1], vec_land[6], mate)
+    pair = sems.ready(work.at[z, y], swap, mate)
+    big1 = weight_spread(direct_spread, place, sems, big_parts, big_out, 1)
+    big0 = [
+        weight_spread(ring_spread, place, sems, big_parts, big_out, 0, only) for only in range(4)
+    ]
+    out1 = weight_spread(direct_spread, place, sems, small_parts, small_out, 1)
+    out0 = weight_spread(direct_spread, place, sems, small_parts, small_out, 0)
     sum0[0]()
+    vec0[0]()
     big1[0]()
     sum0[1]()
+    vec0[1]()
+    sum1[0]()
+    vec1[0]()
     big1[1]()
-    sum0[2]()
-    sum1[0]()
-    big1[2]()
-    big0[0]()
+    big0[0][0]()
+    big0[1][0]()
     sum1[1]()
-    sum1[2]()
+    vec1[1]()
     pair.start()
+    vec_pair.start()
+    big0[0][1]()
+    big0[2][0]()
     pair.wait_recv()
     small_out[z, y] = (work[z, y].astype(f32) + swap[...].astype(f32)).astype(bf16)
     out1[0]()
+    vec_pair.wait_recv()
+    vec_out[...] = vec_sums[1].astype(f32) + vec_land[6][...].astype(f32)
+    big0[1][1]()
+    big0[3][0]()
     out1[1]()
-    out1[2]()
     out0[0]()
-    big0[1]()
+    big0[2][1]()
+    big0[3][1]()
     out0[1]()
-    out0[2]()
-    big0[2]()
+    for one in big0:
+        one[2]()
     sems.finish()
 
 
-def final(big, small, cid):
+def final(big, small, vectors, cid):
     shapes = [(4, 4, n, D) for n in (big_rows, small_rows)]
+    vmem = pl.BlockSpec(memory_space=pltpu.VMEM)
     return call(
         final_kernel,
-        tuple(jax.ShapeDtypeStruct(s, bf16) for s in shapes),
+        (*[jax.ShapeDtypeStruct(s, bf16) for s in shapes], jax.ShapeDtypeStruct((16, D), f32)),
         [
             pltpu.VMEM(shapes[1], bf16),
             pltpu.VMEM((small_rows, D), bf16),
+            pltpu.VMEM((2, 16, D), bf16),
+            pltpu.VMEM((7, 16, D), bf16),
             pltpu.SemaphoreType.DMA((2,)),
-            *sum_lands(small_parts, 0),
-            *sum_lands(small_parts, 1),
+            *[
+                pltpu.VMEM((*lead, block[1], block[3]), bf16)
+                for lead in ((4,), ())
+                for _, block in small_parts
+                for _ in range(3)
+            ],
         ],
-        24 + 1 + 32,
+        12 + 8 + 6 + 32 + 12,
         cid,
-        (big, small.reshape(shapes[1])),
-        [pl.BlockSpec(memory_space=pltpu.VMEM), pl.BlockSpec(memory_space=pl.ANY)],
+        (big, small.reshape(shapes[1]), vectors),
+        [vmem, pl.BlockSpec(memory_space=pl.ANY), vmem],
     )
 
 
@@ -765,7 +854,7 @@
 
 
 def backward_kernel(
-    scal, qe_ref, o_ref, g_ref, kv_ref, part_ref,
+    scal, qe_ref, o_ref, g_ref, kv_ref, gate_ref, up_ref, down_ref,
     dq_ref, dkv_ref, sum_ref,
     ge, qt, gt, dq, work, swap, local_sem, *more,
 ):
@@ -773,13 +862,27 @@
     place = my_place()
     x, y, z, core = place
     me, xhi = lax.axis_index("ctx"), x // 2
-    load = pltpu.make_async_copy(part_ref, work, local_sem.at[0])
-    load.start()
+    loads = []
+    for i, ref in enumerate((gate_ref, up_ref, down_ref)):
+        row = 0
+        while row < FS:
+            chunk, at = divmod(i * FS + row, big_rows)
+            n = min(FS - row, big_rows - at)
+            into = work.at[chunk // 4, chunk % 4, pl.ds(at, n)]
+            loads.append(
+                pltpu.make_async_copy(ref.at[pl.ds(row, n)], into, local_sem.at[len(loads)])
+            )
+            row += n
+    for copy in loads:
+        copy.start()
+    unused = 3 * FS - 15 * big_rows
+    work[3, 3, unused:] = jnp.zeros((big_rows - unused, D), bf16)
     greet([moved(place, a, b) for a in "yz" for b in (1, -1)] + [mate_of(place)])
-    load.wait()
+    for copy in loads:
+        copy.wait()
     sems = Sems(send, recv)
-    sum0 = weight_ring_sum(place, sems, big_parts, work, 0, lands[:12])
-    sum1 = weight_ring_sum(place, sems, big_parts, work, 1, lands[12:])
+    sum0 = weight_sum(ring_sum, place, sems, big_parts, work, 0, lands[:12])
+    sum1 = weight_sum(ring_sum, place, sems, big_parts, work, 1, lands[12:])
     pair = sems.ready(work.at[z, y], swap, mate_of(place))
     sum0[0]()
 
@@ -864,7 +967,7 @@
     sems.finish()
 
 
-def attention_backward(scal, qe, o, grad, kv, part, cid):
+def attention_backward(scal, qe, o, grad, kv, weight_grads, cid):
     big = (4, 4, big_rows, D)
     vmem = pl.BlockSpec(memory_space=pltpu.VMEM)
     return call(
@@ -881,14 +984,18 @@
             pltpu.VMEM((2, ROWS, 128), f32),
             pltpu.VMEM(big, bf16),
             pltpu.VMEM((big_rows, D), bf16),
-            pltpu.SemaphoreType.DMA((1,)),
+            pltpu.SemaphoreType.DMA((20,)),
             *sum_lands(big_parts, 0),
             *sum_lands(big_parts, 1),
         ],
         25,
         cid,
-        (scal, qe, o, grad, kv, part.reshape(big)),
-        [pl.BlockSpec(memory_space=pltpu.SMEM), *[vmem] * 4, pl.BlockSpec(memory_space=pl.ANY)],
+        (scal, qe, o, grad, kv, *weight_grads),
+        [
+            pl.BlockSpec(memory_space=pltpu.SMEM),
+            *[vmem] * 4,
+            *[pl.BlockSpec(memory_space=pl.ANY)] * 3,
+        ],
     )
 
 
@@ -1014,13 +1121,7 @@
     att_grad = jnp.einsum(
         "td,id->ti", branch_grad, cut(out_full, core * QC, QC, 0), preferred_element_type=f32
     ).astype(bf16)
-    large = jnp.concatenate(
-        [
-            *[w.astype(bf16) for w in (gate_wgrad, up_wgrad, down_wgrad)],
-            jnp.zeros((16 * big_rows - 3 * FS, D), bf16),
-        ],
-        0,
-    )
+    large = [w.astype(bf16) for w in (gate_wgrad, up_wgrad, down_wgrad)]
     dq, dkv_part, large_own = attention_backward(
         scal, qe, attended_f, att_grad.reshape(2, 128, QC), kv_all, large, 5
     )
@@ -1055,23 +1156,19 @@
         [jnp.pad(v, (0, D - v.shape[0])) for v in (bias_grad, gain_one_grad, gain_two_grad)]
     )
     small = jnp.concatenate(
-        [
-            out_wgrad.astype(bf16),
-            qkv_wgrad.astype(bf16).reshape(288, D),
-            jnp.pad(vectors, ((0, 16 * small_rows - 515), (0, 0))).astype(bf16),
-        ],
-        0,
-    )
-    large, small = final(large_own, small, 6)
+        [out_wgrad.astype(bf16), qkv_wgrad.astype(bf16).reshape(288, D)], 0
+    )
+    vectors = jnp.pad(vectors, ((0, 13), (0, 0))).astype(bf16)
+    large, small, vectors = final(large_own, small, vectors, 6)
     large, small = large.reshape(16 * big_rows, D), small.reshape(16 * small_rows, D)
     return (
         output,
         token_grad,
-        small[513, :224].astype(f32),
-        small[224:512].reshape(224, QKV).astype(f32),
-        small[512, :288].astype(f32),
+        vectors[1, :224],
+        small[224:].reshape(224, QKV).astype(f32),
+        vectors[0, :288],
         small[:224].astype(f32),
-        small[514, :224].astype(f32),
+        vectors[2, :224],
         large[:FS].astype(f32).T,
         large[FS : 2 * FS].astype(f32).T,
         large[2 * FS : 3 * FS].astype(f32),

time: 412 us -> 393 us (0.954)
  the two profiles are of different devices: /device:TPU:2 before, /device:TPU:0 now
where the time goes in v4:
time: 393 us; the launch traced here: 386 us
  Pallas kernels  274 us (70%)
  other arithmetic  35.1 us (9%)
  matrix products  28.4 us (7%)
  local copies, waits for them, and re-layouts  23.7 us (6%)
  between operations  17.8 us (5%)
  starting transfers between devices  6.24 us (2%)
    pallas_call x6, Pallas kernels, call(): pl.pallas_call(kernel, out_shape=out_shape, in_specs=specs if specs is no...  245 us
    pallas_call x1, Pallas kernels, local_call(): pl.pallas_call(kernel, out_shape=out_shape, in_specs=[pl.BlockSpec(memory...  28.7 us
    dot_general x5, matrix products, dot(): return jnp.dot(a, b, preferred_element_type=f32)  8.69 us
    convert_element_type x1, other arithmetic, body(): large[2 * FS:3 * FS].astype(f32)  8.17 us
  transfers between devices with their start and end apart: 5, of which 0 were waited for; matrix products, arithmetic and copies ran while one was open for 8% of the time, Pallas kernels for 29%

profile of v4, /device:TPU:0, one launch (start us, length us, event | category | flops | bytes accessed | tf_op | source)
XLA Modules:
  0.0 385.6 jit_solution(10461421502331852915)
XLA Ops:
  10.0 0.7 tile.31
  10.8 0.7 tile.14
  11.5 0.7 tile.12
  13.0 0.7 pad_maximum_fusion.2.turn
  13.7 0.6 fusion.36.small
  14.3 0.6 broadcast_in_dim.33.mark
  14.9 54.0 %shard_map.186 = (bf16[2,2,2,64,896]{4,3,2,1,0:T(8,128)(2,1)}, bf16[4,224,1152]{2,1,0:T(8,128)(2,1)}, bf16[4,16,1152]{2,1,0:T(8,128)(2,1)}, bf16[2,128,448]{2,1,0:T(8,128)(2,1)}, bf16[2,4,4,2,272,128]{5,4,3,2,1,0:T(8,128)(2,1)}) custom-call(bf16[2,64,896]{2,1,0:T(8,128)(2,1)} %bitcast.114, bf16[2,64,896]{2,1,0:T(8,128)(2,1)} %bitcast.133, ...), custom_call_target="tpu_custom_call" | custom-call | tf_op jit(solution)/shard_map/pallas_call | solution.py:101
  69.0 2.2 collective-permute-start
  71.2 1.5 fusion.39
  73.3 28.7 %shard_map.187 = (f32[2,128,448]{2,1,0:T(8,128)}, bf16[2,896,128]{2,1,0:T(8,128)(2,1)}) custom-call(s32[34]{0:T(128)} %pad_add_fusion.scal, bf16[2,128,448]{2,1,0:T(8,128)(2,1)} %get-tuple-element.34.q_ref, bf16[32,2,272,128]{3,2,1,0:T(8,128)(2,1)} %bitcast.110), custom_call_target="tpu_custom_call" | custom-call | flops 20000000000 | bytes 10000000 | tf_op jit(solution)/shard_map/pallas_call | solution.py:830
  102.6 1.8 convert_element_type.184
  104.4 11.1 %shard_map.188 = bf16[2,2,256,448]{3,2,1,0:T(8,128)(2,1)} custom-call(bf16[256,448]{1,0:T(8,128)(2,1)} %bitcast.124), custom_call_target="tpu_custom_call" | custom-call | tf_op jit(solution)/shard_map/pallas_call | solution.py:101
  115.5 0.9 convert_reduce_fusion.1
  116.5 0.6 slice_reduce_fusion
  117.2 0.6 add_rsqrt_fusion.1
  117.8 2.3 fusion.55
  120.3 0.6 copy.34
  120.9 1.7 pad_maximum_fusion
  122.7 2.1 fusion.9
  124.8 2.0 multiply_reduce_fusion.1
  127.7 1.5 copy-done.48
  129.1 1.5 fusion.59
  131.1 1.5 fusion.58
  132.6 2.6 multiply_convert_fusion
  135.2 1.6 convolution_convert_fusion.4
  136.8 2.8 convolution_convert_fusion.down_ref
  139.6 0.8 dynamic-slice_bitcast_fusion
  140.9 1.6 fusion.60
  142.5 2.8 convolution_convert_fusion.1.up_ref
  145.3 2.5 add_convert_fusion
  147.8 13.5 %shard_map.189 = bf16[2,2,64,896]{3,2,1,0:T(8,128)(2,1)} custom-call(bf16[2,2,2,64,896]{4,3,2,1,0:T(8,128)(2,1)} %bitcast.128), custom_call_target="tpu_custom_call" | custom-call | tf_op jit(solution)/shard_map/pallas_call | solution.py:101
  161.4 1.3 multiply_reduce_fusion.3
  162.7 2.4 fusion.54
  165.2 2.2 collective-permute-start.2
  167.3 2.8 convolution_convert_fusion.2.gate_ref
  170.1 1.2 convert_add_fusion.2
  171.4 0.9 copy-done.15
  172.3 0.7 fusion.27
  173.0 1.4 collective-permute-start.3
  174.4 1.1 convolution_convert_fusion.6
  175.5 1.8 copy.28
  177.3 59.9 %shard_map.190 = (f32[2,128,448]{2,1,0:T(8,128)}, bf16[32,2,256,128]{3,2,1,0:T(8,128)(2,1)}, bf16[240,896]{1,0:T(8,128)(2,1)}) custom-call(s32[34]{0:T(128)} %pad_add_fusion.scal, bf16[2,896,128]{2,1,0:T(8,128)(2,1)} %get-tuple-element.39.qe_ref, f32[2,128,448]{2,1,0:T(8,128)} %get-tuple-element.36.o_ref, bf16[2,128,448]{2,1,0:T(8,128)(2,1)} %bitcast.125, ...), custom_call_target="tpu_custom_call" | custom-call | tf_op jit(solution)/shard_map/pallas_call | solution.py:101
  237.2 0.8 constant_dynamic-slice_fusion.1
  238.0 0.8 copy-done.10
  238.8 42.4 %shard_map.191 = bf16[2,256,1152]{2,1,0:T(8,128)(2,1)} custom-call(bf16[2,4,4,2,256,128]{5,4,3,2,1,0:T(8,128)(2,1)} %bitcast.112, f32[2,128,448]{2,1,0:T(8,128)} %get-tuple-element.43.dq_ref, f32[2,256,128]{2,1,0:T(8,128)} %pad_maximum_fusion.2.turn), custom_call_target="tpu_custom_call" | custom-call | tf_op jit(solution)/shard_map/pallas_call | solution.py:101
  281.3 1.6 convert_reduce_fusion
  282.9 1.9 slice.114
  284.9 1.3 multiply_reduce_fusion.4
  286.8 1.6 convolution_convert_fusion.3
  288.3 2.4 reshape.408
  291.2 1.2 fusion.7
  292.8 0.6 convolution_convert_fusion.5
  293.5 1.0 pad_maximum_fusion.1
  294.5 0.6 fusion.38.vec_ref
  295.1 64.4 %shard_map.192 = (bf16[4,4,240,896]{3,2,1,0:T(8,128)(2,1)}, bf16[4,4,32,896]{3,2,1,0:T(8,128)(2,1)}, f32[16,896]{1,0:T(8,128)}) custom-call(bf16[240,896]{1,0:T(8,128)(2,1)} %get-tuple-element.45.big_ref, bf16[4,4,32,896]{3,2,1,0:T(8,128)(2,1)} %bitcast.113, bf16[16,896]{1,0:T(8,128)(2,1)} %fusion.38.vec_ref), custom_call_target="tpu_custom_call" | custom-call | tf_op jit(solution)/shard_map/pallas_call | solution.py:101
  359.6 1.5 slice_reduce_fusion.2
  361.1 1.3 fusion.56
  362.4 1.9 slice_convert_fusion.3
  364.4 1.1 slice_convert_fusion.1
  365.6 0.8 fusion.14
  366.4 1.2 reshape.416
  367.6 8.2 %slice_convert_fusion = (f32[1216,896]{1,0:T(8,128)}, f32[896,1216]{0,1:T(8,128)}, f32[896,1216]{0,1:T(8,128)}) fusion(bf16[3840,896]{1,0:T(8,128)(2,1)} %bitcast.102), kind=kLoop, calls=%fused_computation.12 | loop fusion | flops 3268608 | bytes 19611648 | tf_op jit(solution)/shard_map/convert_element_type | solution.py:1174
  375.8 1.7 fusion.21
  377.5 1.0 fusion.17
  (135 shorter events, 5.8 us)
Async XLA Ops:
  7.2 125.4 %copy-start = (bf16[1216,896]{1,0:T(8,128)(2,1)S(1)}, bf16[1216,896]{1,0:T(8,128)(2,1)}, u32[]{:S(2)}) copy-start(bf16[1216,896]{1,0:T(8,128)(2,1)} %param.20) | copy-start | bytes 6537220
  7.2 115.5 %all-gather.2.cloned.1.call-start = ((), (), s32[]{:S(2)}) async-start(), calls=%async_computation | async-start | bytes 2007040 | tf_op jit(solution)/shard_map/all_gather | solution.py:1070
  69.0 51.1 %collective-permute-start = (bf16[2,256,896]{2,1,0:T(8,128)(2,1)}, bf16[2,256,896]{2,1,0:T(8,128)(2,1)S(1)}, u32[]{:S(2)}, u32[]{:S(2)}) collective-permute-start(bf16[2,256,896]{2,1,0:T(8,128)(2,1)} %bitcast.105), channel_id=1, source_target_pairs={{0,66},{1,67},{2,64},{3,65},{4,70},{5,71},{6,68},{7,69},{8,74},{9,... | collective-permute-start | bytes 2752520 | tf_op jit(solution)/shard_map/ppermute | solution.py:1054
  73.3 28.8 %copy-start.47 = (bf16[224]{0:T(256)(128)(2,1)S(1)}, bf16[224]{0:T(256)(128)(2,1)}, u32[]{:S(2)}) copy-start(bf16[224]{0:T(256)(128)(2,1)} %param.13) | copy-start | bytes 1348
  102.0 15.0 %copy-start.12 = (bf16[128,896]{1,0:T(8,128)(2,1)S(1)}, bf16[128,896]{1,0:T(8,128)(2,1)}, u32[]{:S(2)}) copy-start(bf16[128,896]{1,0:T(8,128)(2,1)} %param.11) | copy-start | bytes 688132
  115.5 4.5 %copy-start.8 = (bf16[2,2,2,64,896]{4,3,2,1,0:T(8,128)(2,1)S(1)}, bf16[2,2,2,64,896]{4,3,2,1,0:T(8,128)(2,1)}, u32[]{:S(2)}) copy-start(bf16[2,2,2,64,896]{4,3,2,1,0:T(8,128)(2,1)} %get-tuple-element.30) | copy-start | bytes 2752516
  117.1 44.3 %copy-start.37 = (f32[896]{0:T(1024)}, f32[896]{0:T(1024)S(1)}, u32[]{:S(2)}) copy-start(f32[896]{0:T(1024)S(1)} %get-tuple-element.51) | copy-start | bytes 10756
  122.7 2.2 copy-start.5
  122.7 2.2 copy-start.18
  126.8 35.9 %copy-start.2 = (f32[512,896]{1,0:T(8,128)}, f32[512,896]{1,0:T(8,128)S(1)}, u32[]{:S(2)}) copy-start(f32[512,896]{1,0:T(8,128)S(1)} %get-tuple-element.73) | copy-start | bytes 5505028
  126.8 2.3 copy-start.48
  126.9 3.8 copy-start.39
  127.4 33.9 %copy-start.43 = (f32[256]{0:T(256)}, f32[256]{0:T(256)S(1)}, u32[]{:S(2)}) copy-start(f32[256]{0:T(256)S(1)} %get-tuple-element.69) | copy-start | bytes 3076
  129.1 13.4 %copy-start.31 = (bf16[512,896]{1,0:T(8,128)(2,1)}, bf16[512,896]{1,0:T(8,128)(2,1)S(1)}, u32[]{:S(2)}) copy-start(bf16[512,896]{1,0:T(8,128)(2,1)S(1)} %multiply_convert_fusion.3) | copy-start | bytes 2752516
  129.1 1.9 copy-start.17
  131.1 1.5 copy-start.35
  135.2 5.7 %copy-start.29 = (bf16[512,1216]{0,1:T(8,128)(2,1)}, bf16[512,1216]{0,1:T(8,128)(2,1)S(1)}, u32[]{:S(2)}) copy-start(bf16[512,1216]{0,1:T(8,128)(2,1)S(1)} %get-tuple-element.58) | copy-start | bytes 3735556
  136.8 2.8 copy-start.33
  140.4 29.7 %collective-permute-start.1 = (bf16[2,2,1,64,896]{4,3,1,2,0:T(8,128)(2,1)}, bf16[2,2,1,64,896]{4,3,1,2,0:T(8,128)(2,1)}, u32[]{:S(2)}, u32[]{:S(2)}) collective-permute-start(bf16[2,2,1,64,896]{4,3,1,2,0:T(8,128)(2,1)} %dynamic-slice_bitcast_fusion), channel_id=1, source_target_pairs={{0,1},{1,0},{2,3},{3,2},{4,5},{5,4},{6,7},{7,6},{8,9},{9,8},{10,11... | collective-permute-start | bytes 1376264 | tf_op jit(solution)/shard_map/ppermute | solution.py:1106
  147.8 14.9 %copy-start.9 = (bf16[2,2,2,64,896]{4,3,2,1,0:T(8,128)(2,1)S(1)}, bf16[2,2,2,64,896]{4,3,2,1,0:T(8,128)(2,1)}, u32[]{:S(2)}) copy-start(bf16[2,2,2,64,896]{4,3,2,1,0:T(8,128)(2,1)} %get-tuple-element.30) | copy-start | bytes 2752516
  162.7 2.5 copy-start.7
  162.7 4.7 %copy-start.30 = (bf16[512,1216]{0,1:T(8,128)(2,1)S(1)}, bf16[512,1216]{0,1:T(8,128)(2,1)}, u32[]{:S(2)}) copy-start(bf16[512,1216]{0,1:T(8,128)(2,1)} %copy-done.29) | copy-start | bytes 3735556
  162.7 4.6 %copy-start.32 = (bf16[512,896]{1,0:T(8,128)(2,1)S(1)}, bf16[512,896]{1,0:T(8,128)(2,1)}, u32[]{:S(2)}) copy-start(bf16[512,896]{1,0:T(8,128)(2,1)} %copy-done.31) | copy-start | bytes 2752516
  165.2 9.2 %copy-start.26 = (bf16[256,896]{1,0:T(8,128)(2,1)}, bf16[256,896]{1,0:T(8,128)(2,1)S(1)}, u32[]{:S(2)}) copy-start(bf16[256,896]{1,0:T(8,128)(2,1)S(1)} %get-tuple-element.52) | copy-start | bytes 1376260
  165.2 5.0 %copy-start.34 = (bf16[512,896]{1,0:T(8,128)(2,1)S(1)}, bf16[512,896]{1,0:T(8,128)(2,1)}, u32[]{:S(2)}) copy-start(bf16[512,896]{1,0:T(8,128)(2,1)} %copy-done.33) | copy-start | bytes 2752516
  165.2 72.9 %collective-permute-start.2 = (bf16[256,896]{1,0:T(8,128)(2,1)S(1)}, bf16[256,896]{1,0:T(8,128)(2,1)S(1)}, u32[]{:S(2)}, u32[]{:S(2)}) collective-permute-start(bf16[256,896]{1,0:T(8,128)(2,1)S(1)} %bitcast.100), channel_id=1, source_target_pairs={{0,66},{1,67},{2,64},{3,65},{4,70},{5,71},{6,68},{7,69},{8,74},{9,... | collective-permute-start | bytes 1376264 | tf_op jit(solution)/shard_map/ppermute | solution.py:1054
  170.1 4.3 %copy-start.14 = (bf16[896,896]{1,0:T(8,128)(2,1)S(1)}, bf16[896,896]{1,0:T(8,128)(2,1)}, u32[]{:S(2)}) copy-start(bf16[896,896]{1,0:T(8,128)(2,1)} %all-gather.2.cloned.1.call-done) | copy-start | bytes 4816900
  171.4 0.9 copy-start.15
  173.0 65.0 %collective-permute-start.3 = (bf16[2,1,64,896]{3,2,1,0:T(8,128)(2,1)}, bf16[2,1,64,896]{3,2,1,0:T(8,128)(2,1)}, u32[]{:S(2)}, u32[]{:S(2)}) collective-permute-start(bf16[2,1,64,896]{3,2,1,0:T(8,128)(2,1)} %fusion.27), channel_id=1, source_target_pairs={{0,66},{1,67},{2,64},{3,65},{4,70},{5,71},{6,68},{7,69},{8,74},{9,... | collective-permute-start | bytes 688136 | tf_op jit(solution)/shard_map/ppermute | solution.py:1054
  177.3 59.9 %copy-start.21 = (f32[256,896]{1,0:T(8,128)S(1)}, f32[256,896]{1,0:T(8,128)}, u32[]{:S(2)}) copy-start(f32[256,896]{1,0:T(8,128)} %get-tuple-element.53) | copy-start | bytes 2752516
  238.0 0.8 copy-start.10
  238.8 46.0 %copy-start.40 = (f32[512]{0:T(512)S(1)}, f32[512]{0:T(512)}, u32[]{:S(2)}) copy-start(f32[512]{0:T(512)} %copy-done.39) | copy-start | bytes 6148
  238.8 47.4 %copy-start.6 = (f32[1,2,256,896]{3,2,0,1:T(8,128)S(1)}, f32[1,2,256,896]{3,2,0,1:T(8,128)}, u32[]{:S(2)}) copy-start(f32[1,2,256,896]{3,2,0,1:T(8,128)} %get-tuple-element.63) | copy-start | bytes 5505028
  281.3 3.6 copy-start.3
  281.3 4.9 %copy-start.4 = (bf16[2,256,1152]{2,1,0:T(8,128)(2,1)S(1)}, bf16[2,256,1152]{2,1,0:T(8,128)(2,1)}, u32[]{:S(2)}) copy-start(bf16[2,256,1152]{2,1,0:T(8,128)(2,1)} %shard_map.191) | copy-start | bytes 3538948
  281.3 4.9 %copy-start.36 = (bf16[224,1152]{1,0:T(8,128)(2,1)S(1)}, bf16[224,1152]{1,0:T(8,128)(2,1)}, u32[]{:S(2)}) copy-start(bf16[224,1152]{1,0:T(8,128)(2,1)} %w_ref.1) | copy-start | bytes 1548292
  281.3 4.9 %copy-start.44 = (f32[1,2,2,128]{3,1,2,0:T(2,128)S(1)}, f32[1,2,2,128]{3,1,2,0:T(2,128)}, u32[]{:S(2)}) copy-start(f32[1,2,2,128]{3,1,2,0:T(2,128)} %copy.34) | copy-start | bytes 6148
  284.9 1.9 copy-start.46
  286.7 4.0 %copy-start.11 = (bf16[256,896]{1,0:T(8,128)(2,1)S(1)}, bf16[256,896]{1,0:T(8,128)(2,1)}, u32[]{:S(2)}) copy-start(bf16[256,896]{1,0:T(8,128)(2,1)} %copy-done.10) | copy-start | bytes 1376260
  286.8 4.0 %copy-start.38 = (f32[896]{0:T(1024)S(1)}, f32[896]{0:T(1024)}, u32[]{:S(2)}) copy-start(f32[896]{0:T(1024)} %copy-done.37) | copy-start | bytes 10756
  286.8 4.0 %copy-start.42 = (f32[256]{0:T(256)S(1)}, f32[256]{0:T(256)}, u32[]{:S(2)}) copy-start(f32[256]{0:T(256)} %get-tuple-element.68) | copy-start | bytes 3076
  291.2 1.3 copy-start.19
  291.2 1.3 copy-start.20
  291.2 1.6 copy-start.27
  292.4 1.1 copy-start.22
  295.1 70.3 %copy-start.28 = (bf16[1,256,1152]{2,1,0:T(8,128)(2,1)S(1)}, bf16[1,256,1152]{2,1,0:T(8,128)(2,1)}, u32[]{:S(2)}) copy-start(bf16[1,256,1152]{2,1,0:T(8,128)(2,1)} %slice.114) | copy-start | bytes 1769476
  359.6 5.9 %copy-start.13 = (bf16[128,896]{1,0:T(8,128)(2,1)S(1)}, bf16[128,896]{1,0:T(8,128)(2,1)}, u32[]{:S(2)}) copy-start(bf16[128,896]{1,0:T(8,128)(2,1)} %param.11) | copy-start | bytes 688132
  359.6 5.9 %copy-start.23 = (bf16[4,224,1152]{2,1,0:T(8,128)(2,1)S(1)}, bf16[4,224,1152]{2,1,0:T(8,128)(2,1)}, u32[]{:S(2)}) copy-start(bf16[4,224,1152]{2,1,0:T(8,128)(2,1)} %get-tuple-element.44) | copy-start | bytes 6193156
  359.6 5.9 %copy-start.41 = (f32[896]{0:T(1024)S(1)}, f32[896]{0:T(1024)}, u32[]{:S(2)}) copy-start(f32[896]{0:T(1024)} %get-tuple-element.50) | copy-start | bytes 10756
  359.6 5.9 %copy-start.45 = (f32[128]{0:T(128)S(1)}, f32[128]{0:T(128)}, u32[]{:S(2)}) copy-start(f32[128]{0:T(128)} %add_rsqrt_fusion.1) | copy-start | bytes 1540
  367.6 8.2 %copy-start.16 = (f32[2,2,1,64,896]{4,3,1,2,0:T(8,128)S(1)}, f32[2,2,1,64,896]{4,3,1,2,0:T(8,128)}, u32[]{:S(2)}) copy-start(f32[2,2,1,64,896]{4,3,1,2,0:T(8,128)} %copy-done.15) | copy-start | bytes 2752516
  367.6 8.2 %copy-start.24 = (f32[256,896]{1,0:T(8,128)S(1)}, f32[256,896]{1,0:T(8,128)}, u32[]{:S(2)}) copy-start(f32[256,896]{1,0:T(8,128)} %get-tuple-element.61) | copy-start | bytes 2752516
  367.6 9.9 %copy-start.25 = (f32[2,1,64,896]{3,2,1,0:T(8,128)S(1)}, f32[2,1,64,896]{3,2,1,0:T(8,128)}, u32[]{:S(2)}) copy-start(f32[2,1,64,896]{3,2,1,0:T(8,128)} %constant_dynamic-slice_fusion.1) | copy-start | bytes 1376260
  367.6 10.9 %copy-start.1 = (bf16[1216,896]{1,0:T(8,128)(2,1)S(1)}, bf16[1216,896]{1,0:T(8,128)(2,1)}, u32[]{:S(2)}) copy-start(bf16[1216,896]{1,0:T(8,128)(2,1)} %param.20) | copy-start | bytes 6537220
Sparse Core Ops, SparseCore 0:
  69.1 21.7 all-gather.1
